TPU v7x, 32 devices: a whole 2x2x4 slice. The times are simulated.
32 devices in a mesh: sec: 2 (over x), dev: 8 (over z, y), rep: 2 (over core).
Axes of the slice: x: 2, y: 2, z: 4, core: 2. Of those that a mesh axis runs over, the one named last changes fastest.
Arguments:
- resid: bfloat16 [2048, 4096], P(('rep', 'dev')), parts along dimension 0, may hold values from -27 to 27
- queries: bfloat16 [2048, 4096], P(('rep', 'dev'), 'sec'), parts along dimension 0, may hold values from -30 to 30
- keys: bfloat16 [2048, 1024], P(('rep', 'dev'), 'sec'), parts along dimension 0, may hold values from -6 to 6
- values: bfloat16 [2048, 1024], P(('rep', 'dev'), 'sec'), parts along dimension 0, may hold values from -6 to 6
- norm_gain: float32 [4096], replicated, may hold values from 0.1 to 1.9
- expert_ids: int32 [2048, 2], P(('rep', 'dev')), parts along dimension 0, may hold values from 0 to 3, all different within a row; in each aligned block of 128 rows (0 to 127, 128 to 255, ...) at most 80 rows name the same one
- gate_weights: float32 [2048, 2], P(('rep', 'dev')), parts along dimension 0, may hold values from 0.2 to 1
- w_gate: bfloat16 [8, 4096, 768], P('dev', None, 'sec'), may hold values from -0.09375 to 0.09375
- w_up: bfloat16 [8, 4096, 768], P('dev', None, 'sec'), may hold values from -0.09375 to 0.09375
- w_down: bfloat16 [8, 768, 4096], P('dev', 'sec'), may hold values from -0.15625 to 0.15625
Outputs:
- out: bfloat16 [2048, 4096], P(('rep', 'dev'), 'sec'), parts along dimension 0
There are 2 independent parts, one for each index of `rep`. A program takes and returns all parts, laid end to end along the dimension named above; an argument that names none is the same for every part. Nothing has to cross between parts.
Inputs may be any that keep to these rules, and one draw needn't show every extreme that they name: `expert_ids`: each token names 2 different experts; among the tokens of one index of dev no expert is named more than 80 times.
All inputs are finite; a program needn't handle non-finite values.
Results may differ from a plain program's by a relative error of at most 0.008.
Values may be sent and summed in bfloat16 or wider, within the bound.
No kernel may reach another device: no remote copies, remote signals or barrier semaphores. Data moves between devices by JAX's collectives and lax.ppermute only.
A program may use at most 128 MiB of HBM per device.

v0:
```python
import math

import jax
import jax.numpy as jnp
from jax import lax
from jax.sharding import PartitionSpec as P

HD = 128


def absorb(state, block_keys, block_values, grouped, score_scale):
    run_max, run_total, run_mixed = state
    scores = (
        jnp.einsum("tgrd,ngd->grtn", grouped, block_keys, preferred_element_type=jnp.float32)
        * score_scale
    )
    new_max = jnp.maximum(run_max, jnp.max(scores, axis=-1))
    factor = jnp.exp(run_max - new_max)
    raised = jnp.exp(scores - new_max[..., None])
    run_total = run_total * factor + jnp.sum(raised, axis=-1)
    added = jnp.einsum(
        "grtn,ngd->grtd",
        raised.astype(jnp.bfloat16),
        block_values,
        preferred_element_type=jnp.float32,
    )
    run_mixed = run_mixed * factor[..., None] + added
    return (new_max, run_total, run_mixed)


def body(resid, queries, keys, values, norm_gain, expert_ids, gate_weights, w_gate, w_up, w_down):
    row_count = resid.shape[0]
    model_width = resid.shape[1]
    heads_here = queries.shape[1] // HD
    kv_here = keys.shape[1] // HD
    group_size = heads_here // kv_here
    score_scale = 1.0 / math.sqrt(HD)
    grouped = queries.reshape(row_count, kv_here, group_size, HD)
    initial = (
        jnp.full((kv_here, group_size, row_count), -1e30, jnp.float32),
        jnp.zeros((kv_here, group_size, row_count), jnp.float32),
        jnp.zeros((kv_here, group_size, row_count, HD), jnp.float32),
    )
    state = initial
    piece_keys = lax.all_gather(keys, "dev", axis=0, tiled=True)
    piece_values = lax.all_gather(values, "dev", axis=0, tiled=True)
    piece_rows = piece_keys.shape[0]
    block_keys = 1024
    keys_blocks = piece_keys.reshape(piece_rows // block_keys, block_keys, kv_here, HD)
    values_blocks = piece_values.reshape(piece_rows // block_keys, block_keys, kv_here, HD)

    def advance(inner, pair):
        return (absorb(inner, pair[0], pair[1], grouped, score_scale), None)

    state, _ = lax.scan(advance, state, (keys_blocks, values_blocks))
    run_max, run_total, run_mixed = state
    attended = (
        (run_mixed / run_total[..., None])
        .transpose(2, 0, 1, 3)
        .reshape(row_count, heads_here * HD)
        .astype(jnp.bfloat16)
    )
    joined = lax.all_gather(attended, "sec", axis=1, tiled=True)
    stream = resid.astype(jnp.float32) + joined.astype(jnp.float32)
    normed = (
        stream * lax.rsqrt(jnp.mean(stream * stream, axis=-1, keepdims=True) + 1e-06) * norm_gain
    ).astype(jnp.bfloat16)
    expert_count = lax.axis_size("dev") // 2
    topk_count = expert_ids.shape[1]
    capacity = max(2, (row_count * topk_count * 5 + 4 * expert_count - 1) // (4 * expert_count))
    onehot_ids = (
        expert_ids[:, :, None] == jnp.arange(expert_count, dtype=jnp.int32)[None, None, :]
    ).astype(jnp.int32)
    onehot_ids = onehot_ids.reshape(row_count * topk_count, expert_count)
    earlier = jnp.cumsum(onehot_ids, axis=0) - onehot_ids
    slot_index = jnp.sum(earlier * onehot_ids, axis=1)
    target = expert_ids.reshape(-1) * capacity + slot_index
    placed = (
        target[:, None] == jnp.arange(expert_count * capacity, dtype=jnp.int32)[None, :]
    ).astype(jnp.float32)
    placed = placed.reshape(row_count, topk_count, expert_count * capacity)
    pick_table = jnp.sum(placed, axis=1).astype(jnp.bfloat16)
    buffer_rows = jnp.einsum(
        "ts,td->sd", pick_table, normed, preferred_element_type=jnp.float32
    ).astype(jnp.bfloat16)
    buffer_rows = buffer_rows.reshape(expert_count, capacity, model_width)
    outgoing = jnp.repeat(buffer_rows, 2, axis=0)
    arrived = lax.all_to_all(outgoing, "dev", split_axis=0, concat_axis=0, tiled=True)
    flat_rows = arrived.reshape(-1, model_width)
    gate_out = jnp.dot(flat_rows, w_gate[0], preferred_element_type=jnp.float32)
    up_out = jnp.dot(flat_rows, w_up[0], preferred_element_type=jnp.float32)
    activation = (jax.nn.silu(gate_out) * up_out).astype(jnp.bfloat16)
    partial_out = jnp.dot(activation, w_down[0], preferred_element_type=jnp.float32).astype(
        jnp.bfloat16
    )
    returned = lax.all_to_all(
        partial_out.reshape(arrived.shape), "dev", split_axis=0, concat_axis=0, tiled=True
    )
    returned_rows = returned.reshape(expert_count, 2, capacity, model_width)
    slot_grid = slot_index.reshape(row_count, topk_count)
    taken = returned_rows[expert_ids, :, slot_grid].astype(jnp.float32)
    pair_sum = jnp.sum(taken, axis=2)
    moe_local = jnp.sum(pair_sum * gate_weights[:, :, None], axis=1)
    moe_half = lax.psum_scatter(
        moe_local.astype(jnp.bfloat16), "sec", scatter_dimension=1, tiled=True
    ).astype(jnp.float32)
    half_cols = model_width // 2
    own_stream = lax.dynamic_slice_in_dim(stream, lax.axis_index("sec") * half_cols, half_cols, 1)
    return (own_stream + moe_half).astype(jnp.bfloat16)


def solution(mesh):
    in_specs = (
        P(("rep", "dev"), None),
        P(("rep", "dev"), "sec"),
        P(("rep", "dev"), "sec"),
        P(("rep", "dev"), "sec"),
        P(),
        P(("rep", "dev"), None),
        P(("rep", "dev"), None),
        P("dev", None, "sec"),
        P("dev", None, "sec"),
        P("dev", "sec", None),
    )
    out_specs = P(("rep", "dev"), "sec")
    return jax.shard_map(body, mesh=mesh, in_specs=in_specs, out_specs=out_specs, check_vma=False)
```

profile of v0, /device:TPU:0, one launch (start us, length us, event | category | flops | bytes accessed | tf_op | source)
XLA Modules:
  0.0 472.7 jit_solution(8479521354418965428)
XLA Ops:
  6.5 1.8 copy.96
  8.3 0.0 all-gather.4.cloned.1.call-update
  8.4 0.0 all-gather.6.cloned.1.call-start
  8.4 0.7 all-gather.6.cloned.1.call-update
  9.1 0.0 all-gather.8.cloned.1.call-start
  9.2 2.2 reshape.114
  11.4 40.3 %all-gather.4.cloned.1.call-done = bf16[1024,512]{0,1:T(8,128)(2,1)} async-done(((bf16[128,512]{0,1:T(8,128)(2,1)}), bf16[1024,512]{0,1:T(8,128)(2,1)}) %all-gather.4.cloned.1.call-update) | async-done | bytes 1048592 | tf_op jit(solution)/shard_map/all_gather | solution.py:45
  51.7 2.7 bitcast_reduce_fusion
  54.4 1.4 fusion.1
  55.8 1.8 copy-done.2
  57.6 35.3 %all-gather.6.cloned.1.call-done = bf16[1024,512]{1,0:T(8,128)(2,1)} async-done(((bf16[128,512]{1,0:T(8,128)(2,1)}), bf16[1024,512]{1,0:T(8,128)(2,1)}) %all-gather.6.cloned.1.call-update) | async-done | bytes 1048592 | tf_op jit(solution)/shard_map/all_gather | solution.py:46
  92.9 2.3 copy.99
  95.1 6.1 %divide_convert_fusion = bf16[128,4,4,128]{0,3,2,1:T(8,128)(2,1)} fusion(bf16[1024,4,128,1]{0,2,3,1:T(8,128)(2,1)} %bitcast.95, f32[4,1024,128,4]{2,1,3,0:T(8,128)} %copy-done.2, f32[4,4,128]{2,1,0:T(4,128)S(1)} %get-tuple-element.20, f32[128,4,4]{0,2,1:T(4,128)S(1)} %bitcast_add_fusion, f32[128,4,4]{0,2,1:T(4,128)S(1)} %get-tuple-element.19), kind=kOutput, calls=%fused_computation.28 | convolution fusion | flops 543948800 | bytes 9986048 | tf_op jit(solution)/shard_map/while/body/eval_jaxpr/grtn,ngd->grtd/dot_general | solution.py:21
  101.2 2.1 copy.101
  103.4 0.1 copy.102
  103.5 0.1 eq.44
  103.6 0.1 eq.40
  103.8 1.2 reduce-window.6
  105.0 0.1 slice.10
  105.1 0.1 copy.104
  105.2 0.1 copy.105
  105.3 0.1 add_bitcast_fusion
  105.4 0.1 reduce_sum.62
  105.6 0.1 copy.106
  105.6 0.1 convert_reduce_fusion.1
  105.7 17.9 %all-gather.8.cloned.1.call-done = bf16[128,4096]{1,0:T(8,128)(2,1)} async-done(((bf16[128,2048]{1,0:T(8,128)(2,1)}), bf16[128,4096]{1,0:T(8,128)(2,1)}) %all-gather.8.cloned.1.call-update) | async-done | bytes 1048592 | tf_op jit(solution)/shard_map/all_gather | solution.py:63
  123.6 3.3 convert_add_fusion
  126.9 0.9 convolution_convert_fusion.1
  127.9 0.6 broadcast_in_dim.14
  128.5 121.2 %all_to_all.10 = bf16[8,80,4096]{2,1,0:T(8,128)(2,1)S(1)} all-to-all(bf16[8,80,4096]{2,1,0:T(8,128)(2,1)S(1)} %bitcast.89), channel_id=1, replica_groups=mesh['sec'=2,'dev'=8,'rep'=2] {'dev'}, dimensions={0} | all-to-all | bytes 10485760 | tf_op jit(solution)/shard_map/all_to_all | solution.py:88
  249.8 2.3 copy-done.3
  252.1 3.9 fusion.10
  256.0 11.5 %convolution_convert_fusion = bf16[640,4096]{1,0:T(8,128)(2,1)} fusion(bf16[1,384,4096]{2,1,0:T(8,128)(2,1)S(1)} %copy-done, bf16[640,4096]{1,0:T(8,128)(2,1)} %bitcast.93, bf16[1,4096,384]{2,1,0:T(8,128)(2,1)} %param.18, f32[640,384]{1,0:T(8,128)} %fusion.10), kind=kOutput, calls=%fused_computation.7 | convolution fusion | flops 4030627840 | bytes 17760256 | tf_op jit(solution)/shard_map/dot_general | solution.py:93
  267.5 4.8 %all-to-all-start.1 = ((bf16[8,80,4096]{2,1,0:T(8,128)(2,1)}), bf16[8,80,4096]{2,1,0:T(8,128)(2,1)}, u32[]{:S(2)}, u32[]{:S(2)}) async-start(bf16[8,80,4096]{2,1,0:T(8,128)(2,1)} %bitcast.91), calls=%async_computation.1 | async-start | bytes 10485760 | tf_op jit(solution)/shard_map/all_to_all | solution.py:96
  272.3 0.3 reduce-scatter.2.cloned.1.call-start
  272.6 0.1 reshape.121
  272.8 0.1 copy.107
  272.8 0.1 copy.110
  273.0 0.1 reshape.122
  273.1 0.1 copy.112
  273.2 113.9 %all-to-all-done.1 = bf16[8,80,4096]{2,1,0:T(8,128)(2,1)} async-done(((bf16[8,80,4096]{2,1,0:T(8,128)(2,1)}), bf16[8,80,4096]{2,1,0:T(8,128)(2,1)}, u32[]{:S(2)}, u32[]{:S(2)}) %all-to-all-start.1) | async-done | bytes 5242912 | tf_op jit(solution)/shard_map/all_to_all | solution.py:96
  387.1 10.3 %copy.111 = bf16[4,2,80,4096]{3,1,2,0:T(2,128)(2,1)} copy(bf16[4,2,80,4096]{3,2,1,0:T(8,128)(2,1)} %bitcast.19) | data formatting | bytes 10485760 | tf_op jit(solution)/shard_map/reshape | solution.py:99
  397.4 17.9 %gather_fusion = bf16[256,2,4096]{2,1,0:T(2,128)(2,1)} fusion(bf16[4,2,80,4096]{3,1,2,0:T(2,128)(2,1)} %copy.111, s32[256]{0:T(256)S(1)} %reshape.122), kind=kCustom, calls=%fused_computation | custom fusion | bytes 8390656 | tf_op jit(solution)/shard_map/gather | solution.py:101
  415.3 14.2 %convert_reduce_fusion = f32[256,4096]{1,0:T(8,128)} fusion(bf16[256,2,4096]{2,1,0:T(2,128)(2,1)} %gather_fusion), kind=kLoop, calls=%fused_computation.4 | loop fusion | flops 3145728 | bytes 8388608 | tf_op jit(solution)/shard_map/reduce_sum | solution.py:102
  429.5 6.0 %reshape.132 = f32[128,2,4096]{2,1,0:T(2,128)} reshape(f32[256,4096]{1,0:T(8,128)} %convert_reduce_fusion) | data formatting | bytes 8388608 | tf_op jit(solution)/shard_map/reduce_sum | solution.py:102
  435.5 9.7 %multiply_reduce_fusion = bf16[128,4096]{1,0:T(8,128)(2,1)} fusion(f32[128,2,4096]{2,1,0:T(2,128)} %reshape.132, f32[128,2]{1,0:T(8,128)S(1)} %copy.112), kind=kLoop, calls=%fused_computation.10 | loop fusion | flops 1572864 | bytes 5243904 | tf_op jit(solution)/shard_map/reduce_sum | solution.py:103
  445.3 18.6 %reduce-scatter.2.cloned.1.call-done = bf16[128,2048]{1,0:T(8,128)(2,1)} async-done(((bf16[128,4096]{1,0:T(8,128)(2,1)}), bf16[128,2048]{1,0:T(8,128)(2,1)}) %reduce-scatter.2.cloned.1.call-update) | async-done | bytes 524304 | tf_op jit(solution)/shard_map/reduce_scatter | solution.py:104
  463.8 2.3 add_convert_fusion
  (30 shorter events, 0.2 us)
Async XLA Ops:
  6.5 249.5 %copy-start = (bf16[1,384,4096]{2,1,0:T(8,128)(2,1)S(1)}, bf16[1,384,4096]{2,1,0:T(8,128)(2,1)}, u32[]{:S(2)}) copy-start(bf16[1,384,4096]{2,1,0:T(8,128)(2,1)} %param.19) | copy-start | bytes 9437188
  6.5 45.1 %all-gather.4.cloned.1.call-start = ((), (), s32[]{:S(2)}) async-start(), calls=%async_computation.3 | async-start | bytes 1179648 | tf_op jit(solution)/shard_map/all_gather | solution.py:45
  8.4 84.5 %all-gather.6.cloned.1.call-start = ((), (), s32[]{:S(2)}) async-start(), calls=%async_computation.4 | async-start | bytes 1179648 | tf_op jit(solution)/shard_map/all_gather | solution.py:46
  9.1 114.4 %all-gather.8.cloned.1.call-start = ((), (), s32[]{:S(2)}) async-start(), calls=%async_computation.5 | async-start | bytes 1572864 | tf_op jit(solution)/shard_map/all_gather | solution.py:63
  54.4 3.2 copy-start.2
  95.1 8.2 %copy-start.7 = (s32[128,2]{0,1:T(2,128)S(1)}, s32[128,2]{0,1:T(2,128)}, u32[]{:S(2)}) copy-start(s32[128,2]{0,1:T(2,128)} %param.15) | copy-start | bytes 3076
  101.2 25.7 %copy-start.6 = (f32[4096]{0:T(1024)S(1)}, f32[4096]{0:T(1024)}, u32[]{:S(2)}) copy-start(f32[4096]{0:T(1024)} %param.14) | copy-start | bytes 49156
  123.6 3.4 copy-start.4
  123.6 3.4 copy-start.5
  128.5 123.6 %copy-start.9 = (bf16[1,4096,384]{2,1,0:T(8,128)(2,1)S(1)}, bf16[1,4096,384]{2,1,0:T(8,128)(2,1)}, u32[]{:S(2)}) copy-start(bf16[1,4096,384]{2,1,0:T(8,128)(2,1)} %param.17) | copy-start | bytes 9437188
  249.8 2.3 copy-start.3
  267.5 5.6 %copy-start.8 = (f32[128,2]{0,1:T(2,128)S(1)}, f32[128,2]{0,1:T(2,128)}, u32[]{:S(2)}) copy-start(f32[128,2]{0,1:T(2,128)} %param.16) | copy-start | bytes 3076
  267.5 119.6 %all-to-all-start.1 = ((bf16[8,80,4096]{2,1,0:T(8,128)(2,1)}), bf16[8,80,4096]{2,1,0:T(8,128)(2,1)}, u32[]{:S(2)}, u32[]{:S(2)}) async-start(bf16[8,80,4096]{2,1,0:T(8,128)(2,1)} %bitcast.91), calls=%async_computation.1 | async-start | bytes 10485760 | tf_op jit(solution)/shard_map/all_to_all | solution.py:96
  272.3 191.5 %reduce-scatter.2.cloned.1.call-start = ((), (), s32[]{:S(2)}) async-start(), calls=%async_computation.6 | async-start | bytes 1572864 | tf_op jit(solution)/shard_map/reduce_scatter | solution.py:104
  429.5 36.6 %copy-start.1 = (bf16[1,384,4096]{2,1,0:T(8,128)(2,1)S(1)}, bf16[1,384,4096]{2,1,0:T(8,128)(2,1)}, u32[]{:S(2)}) copy-start(bf16[1,384,4096]{2,1,0:T(8,128)(2,1)} %param.19) | copy-start | bytes 9437188
Sparse Core Ops, SparseCore 0:
  9.4 42.2 all-gather.3
  53.8 39.0 all-gather.5
  103.5 20.0 all-gather.7
  445.4 18.4 reduce-scatter.1
where the time goes:
time: 473 us
  waiting for transfers between devices  227 us (48%)
  blocking collectives  121 us (26%)
  local copies, waits for them, and re-layouts  48.7 us (10%)
  other arithmetic  32.5 us (7%)
  matrix products  25.2 us (5%)
  between operations  13.3 us (3%)
  starting transfers between devices  5.14 us (1%)
    all_to_all x1, blocking collectives, body(): lax.all_to_all(outgoing, 'dev', split_axis=0, concat_axis=0, tiled=True)  121 us
    all_to_all x1, waiting for transfers between devices, body(): lax.all_to_all(partial_out.reshape(arrived.shape), 'dev', split_axis=0, c...  114 us
    all_gather x1, waiting for transfers between devices, body(): piece_keys = lax.all_gather(keys, 'dev', axis=0, tiled=True)  40.3 us
    all_gather x1, waiting for transfers between devices, body(): piece_values = lax.all_gather(values, 'dev', axis=0, tiled=True)  35.3 us
    reduce_scatter x1, waiting for transfers between devices, body(): lax.psum_scatter(moe_local.astype(jnp.bfloat16), 'sec', scatter_dimension...  18.6 us
    gather x1, local copies, waits for them, and re-layouts, body(): taken = returned_rows[expert_ids, :, slot_grid].astype(jnp.float32)  17.9 us
    all_gather x1, waiting for transfers between devices, body(): joined = lax.all_gather(attended, 'sec', axis=1, tiled=True)  17.9 us
    reduce_sum x1, other arithmetic, body(): pair_sum = jnp.sum(taken, axis=2)  14.2 us
  transfers between devices with their start and end apart: 5, of which 5 were waited for; matrix products, arithmetic and copies ran while one was open for 2% of the time, Pallas kernels for 0%

commit v1 on v0

v1 whole, which is shorter than its diff:
```python
import functools
import math

import jax
import jax.numpy as jnp
from jax import lax
from jax.experimental import pallas as pl
from jax.experimental.pallas import tpu as pltpu
from jax.sharding import PartitionSpec as P

HD = 128
F32 = jnp.float32
BF16 = jnp.bfloat16
VMEM = pl.BlockSpec(memory_space=pltpu.VMEM)


def params(megabytes):
    return pltpu.CompilerParams(vmem_limit_bytes=megabytes * 1024 * 1024)


def cost(flops, moved):
    return pl.CostEstimate(flops=int(flops), bytes_accessed=int(moved), transcendentals=0)


def attend_kernel(blocks, kv_here, group_size, q_ref, resid_ref, *refs):
    kv_refs, (stream_ref, square_ref) = refs[:-2], refs[-2:]
    rows = q_ref.shape[0]
    factor = math.log2(math.e) / math.sqrt(HD)
    squares = jnp.zeros((rows, 1), F32)
    for g in range(kv_here):
        heads = [q_ref[:, (g * group_size + r) * HD : (g * group_size + r + 1) * HD] for r in range(group_size)]
        query = jnp.concatenate(heads, axis=0)
        run_max = None
        for block in blocks:
            keys = jnp.concatenate([kv_refs[i][:, g * HD : (g + 1) * HD] for i in block], axis=0)
            values = jnp.concatenate(
                [kv_refs[i][:, (kv_here + g) * HD : (kv_here + g + 1) * HD] for i in block], axis=0
            )
            scores = lax.dot_general(query, keys, (((1,), (1,)), ((), ())), preferred_element_type=F32)
            top = jnp.max(scores, axis=1, keepdims=True)
            new_max = top if run_max is None else jnp.maximum(run_max, top)
            raised = jnp.exp2((scores - new_max) * factor)
            total = jnp.sum(raised, axis=1, keepdims=True)
            mixed = jnp.dot(raised.astype(BF16), values, preferred_element_type=F32)
            if run_max is None:
                run_total, run_mixed = total, mixed
            else:
                old = jnp.exp2((run_max - new_max) * factor)
                run_total, run_mixed = run_total * old + total, run_mixed * old + mixed
            run_max = new_max
        attended = (run_mixed / run_total).astype(BF16).astype(F32)
        for r in range(group_size):
            low = (g * group_size + r) * HD
            stream = resid_ref[:, low : low + HD].astype(F32) + attended[r * rows : (r + 1) * rows]
            stream_ref[:, low : low + HD] = stream
            squares = squares + jnp.sum(stream * stream, axis=1, keepdims=True)
    square_ref[...] = jnp.broadcast_to(squares, square_ref.shape)


def attend_long(queries, resid_half, pieces):
    rows, kv_here = queries.shape[0], pieces[0].shape[1] // (2 * HD)
    grouped = queries.reshape(rows, kv_here, -1, HD)
    scale = 1.0 / math.sqrt(HD)
    state = None
    for i in range(0, len(pieces), 8):
        block = jnp.concatenate(pieces[i : i + 8], axis=0).reshape(-1, 2, kv_here, HD)
        scores = jnp.einsum("tgrd,ngd->grtn", grouped, block[:, 0], preferred_element_type=F32) * scale
        top = jnp.max(scores, axis=-1, keepdims=True)
        new_max = top if state is None else jnp.maximum(state[0], top)
        raised = jnp.exp(scores - new_max)
        total = jnp.sum(raised, axis=-1, keepdims=True)
        mixed = jnp.einsum("grtn,ngd->grtd", raised.astype(BF16), block[:, 1], preferred_element_type=F32)
        if state is not None:
            old = jnp.exp(state[0] - new_max)
            total, mixed = state[1] * old + total, state[2] * old + mixed
        state = (new_max, total, mixed)
    attended = (state[2] / state[1]).transpose(2, 0, 1, 3).reshape(rows, -1).astype(BF16)
    stream = resid_half.astype(F32) + attended.astype(F32)
    return stream, jnp.broadcast_to(jnp.sum(stream * stream, axis=1, keepdims=True), (rows, HD))


def pick_kernel(width, stream_ref, own_ref, other_ref, gain_ref, pick_ref, *outs):
    squares = own_ref[:, :1] + other_ref[:, :1]
    normed = (stream_ref[...] * lax.rsqrt(squares / width + 1e-06) * gain_ref[...]).astype(BF16)
    for k, out_ref in enumerate(outs):
        out_ref[...] = jnp.dot(pick_ref[k], normed, preferred_element_type=F32).astype(BF16)


def hidden_kernel(sec_ref, *refs):
    pieces, (gate_ref, up_ref, act_ref, gate_sum, up_sum) = refs[:8], refs[8:]
    step = pl.program_id(0)
    for j in range(4):

        @pl.when(step == j)
        def _(j=j):
            rows = jnp.concatenate([pieces[2 * j][...], pieces[2 * j + 1][...]], axis=0)
            gate = jnp.dot(rows, gate_ref[...], preferred_element_type=F32)
            up = jnp.dot(rows, up_ref[...], preferred_element_type=F32)
            if j == 0:
                gate_sum[...] = gate
                up_sum[...] = up
            elif j < 3:
                gate_sum[...] += gate
                up_sum[...] += up
            else:
                gate = gate_sum[...] + gate
                up = up_sum[...] + up
                act_ref[...] = (gate / (1.0 + jnp.exp(-gate)) * up).astype(BF16)


def down_kernel(own_act, other_act, own_w, other_w, keep_ref, send_ref):
    rows = keep_ref.shape[0]
    total = jnp.dot(own_act[...], own_w[...], preferred_element_type=F32)
    total = total + jnp.dot(other_act[...], other_w[...], preferred_element_type=F32)
    keep_ref[...] = total[:rows]
    send_ref[...] = total[rows:].astype(BF16)


def combine_kernel(stream_ref, high_ref, low_ref, *refs):
    returned, out_ref = refs[:-1], refs[-1]
    total = stream_ref[...]
    for k, ref in enumerate(returned):
        rows = ref[...]
        total = total + jnp.dot(high_ref[k], rows, preferred_element_type=F32)
        total = total + jnp.dot(low_ref[k], rows, preferred_element_type=F32)
    out_ref[...] = total.astype(BF16)


def body(resid, queries, keys, values, norm_gain, expert_ids, gate_weights, w_gate, w_up, w_down):
    rows, width = resid.shape
    half = width // 2
    quarter = half // 2
    heads_here = queries.shape[1] // HD
    kv_here = keys.shape[1] // HD
    group_size = heads_here // kv_here
    n_dev = lax.axis_size("dev")
    n_exp = n_dev // 2
    topk = expert_ids.shape[1]
    cap = max(2, (rows * topk * 5 + 4 * n_exp - 1) // (4 * n_exp))
    hidden = w_gate.shape[2]
    sec = lax.axis_index("sec")
    plane = lax.axis_index("dev") // 2

    def over_sec(a):
        return lax.ppermute(a, "sec", [(0, 1), (1, 0)])

    def over_y(a):
        return lax.ppermute(a, "dev", [(i, i ^ 1) for i in range(n_dev)])

    def over_z(a, k):
        return lax.ppermute(a, "dev", [(i, ((i // 2) ^ k) * 2 + i % 2) for i in range(n_dev)])

    own_kv = jnp.concatenate([keys, values], axis=1)
    kv_planes = [own_kv] + [over_z(own_kv, k) for k in range(1, n_exp)]
    pieces = kv_planes + [over_y(a) for a in kv_planes]
    down_own = lax.dynamic_slice_in_dim(w_down[0], sec * half, half, 1)
    down_other = over_sec(lax.dynamic_slice_in_dim(w_down[0], (1 - sec) * half, half, 1))

    experts = jnp.arange(n_exp, dtype=jnp.int32)
    onehot = (expert_ids[:, :, None] == experts[None, None, :]).astype(jnp.int32)
    onehot = onehot.reshape(rows * topk, n_exp)
    earlier = jnp.cumsum(onehot, axis=0) - onehot
    slot = jnp.sum(earlier * onehot, axis=1).reshape(rows, topk)
    target = (expert_ids ^ plane) * cap + slot
    placed = target[:, :, None] == jnp.arange(n_exp * cap, dtype=jnp.int32)[None, None, :]
    pick = jnp.sum(placed.astype(F32), axis=1).astype(BF16).T.reshape(n_exp, cap, rows)
    weight = jnp.sum(jnp.where(placed, gate_weights[:, :, None], 0.0), axis=1)
    weight = weight.reshape(rows, n_exp, cap).transpose(1, 0, 2)
    weight_high = weight.astype(BF16)
    weight_low = (weight - weight_high.astype(F32)).astype(BF16)

    resid_half = lax.dynamic_slice_in_dim(resid, sec * half, half, 1)
    gain_half = lax.dynamic_slice_in_dim(norm_gain, sec * half, half, 0).reshape(1, half)

    n_keys = rows * n_dev
    if n_dev <= 8:
        stream, squares = pl.pallas_call(
            functools.partial(attend_kernel, [list(range(len(pieces)))], kv_here, group_size),
            out_shape=(jax.ShapeDtypeStruct((rows, half), F32), jax.ShapeDtypeStruct((rows, HD), F32)),
            in_specs=[VMEM] * (2 + len(pieces)),
            out_specs=(VMEM, VMEM),
            compiler_params=params(56),
            cost_estimate=cost(4 * rows * half * n_keys, n_keys * kv_here * HD * 4 + rows * half * 8),
            name="attend",
        )(queries, resid_half, *pieces)
    else:
        stream, squares = attend_long(queries, resid_half, pieces)

    other_squares = over_sec(squares)
    sent = pl.pallas_call(
        functools.partial(pick_kernel, width),
        out_shape=[jax.ShapeDtypeStruct((cap, half), BF16)] * n_exp,
        in_specs=[VMEM] * 5,
        out_specs=[VMEM] * n_exp,
        compiler_params=params(32),
        cost_estimate=cost(2 * n_exp * cap * rows * half, rows * half * 4 + n_exp * cap * half * 2),
        name="pick",
    )(stream, squares, other_squares, gain_half, pick)

    def plane_gather(rows_here):
        first, second = rows_here[:, :quarter], rows_here[:, quarter:]
        first_x = over_sec(first)
        second_y = over_y(second)
        count = first.shape[0]
        first_y = over_y(jnp.stack([first, first_x]))
        second_x = over_sec(jnp.stack([second, second_y]))
        return [first, first_y[0], second, second_y, first_x, first_y[1], second_x[0], second_x[1]]

    def experts_of(parts):
        count = parts[0].shape[0]
        whole = [pl.BlockSpec((count, quarter), lambda j, s: (0, 0))] * 8
        weights = pl.BlockSpec((quarter, hidden), lambda j, s: ((j + 2 * s[0]) % 4, 0))
        act = pl.pallas_call(
            hidden_kernel,
            grid_spec=pltpu.PrefetchScalarGridSpec(
                num_scalar_prefetch=1,
                grid=(4,),
                in_specs=whole + [weights, weights],
                out_specs=pl.BlockSpec((2 * count, hidden), lambda j, s: (0, 0)),
                scratch_shapes=[pltpu.VMEM((2 * count, hidden), F32)] * 2,
            ),
            out_shape=jax.ShapeDtypeStruct((2 * count, hidden), BF16),
            compiler_params=params(32),
            cost_estimate=cost(8 * count * width * hidden, 4 * width * hidden),
            name="hidden",
        )(sec.astype(jnp.int32).reshape(1), *parts, w_gate[0], w_up[0])
        other_act = over_sec(act)
        keep, send = pl.pallas_call(
            down_kernel,
            out_shape=(jax.ShapeDtypeStruct((count, half), F32), jax.ShapeDtypeStruct((count, half), BF16)),
            in_specs=[VMEM] * 4,
            out_specs=(VMEM, VMEM),
            compiler_params=params(32),
            cost_estimate=cost(8 * count * half * hidden, 4 * half * hidden),
            name="down",
        )(act, other_act, down_own, down_other)
        return (keep + over_y(send).astype(F32)).astype(BF16)

    arrived = [sent[0]] + [over_z(sent[k], k) for k in range(1, n_exp)]
    n_groups = min(4, n_exp)
    each = n_exp // n_groups
    returned = [None] * n_exp
    for g in range(n_groups):
        members = list(range(g * each, (g + 1) * each))
        block = arrived[members[0]] if each == 1 else jnp.concatenate([arrived[k] for k in members], axis=0)
        result = experts_of(plane_gather(block))
        for n, k in enumerate(members):
            part = result if each == 1 else result[n * cap : (n + 1) * cap]
            returned[k] = part if k == 0 else over_z(part, k)

    return pl.pallas_call(
        combine_kernel,
        out_shape=jax.ShapeDtypeStruct((rows, half), BF16),
        in_specs=[VMEM] * (3 + n_exp),
        out_specs=VMEM,
        compiler_params=params(32),
        cost_estimate=cost(4 * n_exp * cap * rows * half, rows * half * 6 + n_exp * cap * half * 2),
        name="combine",
    )(stream, weight_high, weight_low, *returned)


def solution(mesh):
    in_specs = (
        P(("rep", "dev"), None),
        P(("rep", "dev"), "sec"),
        P(("rep", "dev"), "sec"),
        P(("rep", "dev"), "sec"),
        P(),
        P(("rep", "dev"), None),
        P(("rep", "dev"), None),
        P("dev", None, "sec"),
        P("dev", None, "sec"),
        P("dev", "sec", None),
    )
    out_specs = P(("rep", "dev"), "sec")
    return jax.shard_map(body, mesh=mesh, in_specs=in_specs, out_specs=out_specs, check_vma=False)
```

time: 473 us -> 179 us (0.38)
  waiting for transfers between devices: 227 us -> 77.9 us
  blocking collectives: 121 us -> 0 us
  starting transfers between devices: 5.14 us -> 53.4 us
  local copies, waits for them, and re-layouts: 48.7 us -> 14.5 us
  other arithmetic: 32.5 us -> 5.12 us
  Pallas kernels: 0 us -> 27.3 us
  matrix products: 25.2 us -> 0 us
  between operations: 13.3 us -> 0.45 us
    all_to_all x1 -> x0, blocking collectives: 121 us -> none  [body(): lax.all_to_all(outgoing, 'dev', split_axis=0, concat_axis=0, tiled=True)]
    all_to_all x1 -> x0, waiting for transfers between devices: 114 us -> none  [body(): lax.all_to_all(partial_out.reshape(arrived.shape), 'dev', split_axis=0, c...]
    all_gather x3 -> x0, waiting for transfers between devices: 93.4 us -> none  [the longest x1 40.3 us: body(): piece_keys = lax.all_gather(keys, 'dev', axis=0, tiled=True)]
    ppermute x0 -> x39, waiting for transfers between devices: none -> 77.9 us  [the longest x14 33.7 us: over_sec(): return lax.ppermute(a, 'sec', [(0, 1), (1, 0)])]
    ppermute x0 -> x39, starting transfers between devices: none -> 53.4 us  [the longest x9 18.7 us: over_z(): lax.ppermute(a, 'dev', [(i, (i // 2 ^ k) * 2 + i % 2) for i in range(n_de...]
    pallas_call x0 -> x11, Pallas kernels: none -> 27.3 us  [the longest x4 8.98 us: experts_of(): pl.pallas_call(down_kernel, out_shape=(jax.ShapeDtypeStruct((count, half)...]
    dot_general x5 -> x0, matrix products: 25.2 us -> none  [the longest x1 11.5 us: body(): jnp.dot(activation, w_down[0], preferred_element_type=jnp.float32)]
    reduce_sum x5 -> x2, other arithmetic: 25.4 us -> 0.73 us  [the longest x1 0.71 us: body(): jnp.sum(placed.astype(F32), axis=1).astype(BF16).T.reshape(n_exp, cap, rows)]
  transfers between devices with their start and end apart: 5 -> 39, of which waited for: 5 -> 14; matrix products, arithmetic and copies ran while one was open for 2% -> 7% of each run, Pallas kernels for 0% -> 10%
where the time goes in v1:
time: 179 us
  waiting for transfers between devices  77.9 us (44%)
  starting transfers between devices  53.4 us (30%)
  Pallas kernels  27.3 us (15%)
  local copies, waits for them, and re-layouts  14.5 us (8%)
  other arithmetic  5.12 us (3%)
    ppermute x14, waiting for transfers between devices, over_sec(): return lax.ppermute(a, 'sec', [(0, 1), (1, 0)])  33.7 us
    ppermute x9, waiting for transfers between devices, over_z(): lax.ppermute(a, 'dev', [(i, (i // 2 ^ k) * 2 + i % 2) for i in range(n_de...  33.2 us
    ppermute x9, starting transfers between devices, over_z(): lax.ppermute(a, 'dev', [(i, (i // 2 ^ k) * 2 + i % 2) for i in range(n_de...  18.7 us
    ppermute x16, starting transfers between devices, over_y(): return lax.ppermute(a, 'dev', [(i, i ^ 1) for i in range(n_dev)])  17.8 us
    ppermute x14, starting transfers between devices, over_sec(): return lax.ppermute(a, 'sec', [(0, 1), (1, 0)])  16.9 us
    ppermute x16, waiting for transfers between devices, over_y(): return lax.ppermute(a, 'dev', [(i, i ^ 1) for i in range(n_dev)])  11 us
    pallas_call x4, Pallas kernels, experts_of(): pl.pallas_call(down_kernel, out_shape=(jax.ShapeDtypeStruct((count, half)...  8.98 us
    pallas_call x4, Pallas kernels, experts_of(): pl.pallas_call(hidden_kernel, grid_spec=pltpu.PrefetchScalarGridSpec(num_...  8.78 us
  transfers between devices with their start and end apart: 39, of which 14 were waited for; matrix products, arithmetic and copies ran while one was open for 7% of the time, Pallas kernels for 10%

profile of v1, /device:TPU:0, one launch (start us, length us, event | category | flops | bytes accessed | tf_op | source)
XLA Modules:
  0.0 178.6 jit_solution(4501001713231999581)
XLA Ops:
  1.9 3.1 %collective-permute-start = (bf16[128,1024]{1,0:T(8,128)(2,1)S(1)}, bf16[128,1024]{1,0:T(8,128)(2,1)S(1)}, u32[]{:S(2)}, u32[]{:S(2)}) collective-permute-start(bf16[128,1024]{1,0:T(8,128)(2,1)S(1)} %constant_dynamic-update-slice_fusion.refs_0_), channel_id=1, source_target_pairs={{0,4},{2,6},{4,0},{6,2},{8,12},{10,14},{12,8},{14,10},{1,5},{3,7},... | collective-permute-start | bytes 786440 | tf_op jit(solution)/shard_map/ppermute | solution.py:151
  5.0 2.6 %collective-permute-start.1 = (bf16[128,1024]{1,0:T(8,128)(2,1)S(1)}, bf16[128,1024]{1,0:T(8,128)(2,1)S(1)}, u32[]{:S(2)}, u32[]{:S(2)}) collective-permute-start(bf16[128,1024]{1,0:T(8,128)(2,1)S(1)} %constant_dynamic-update-slice_fusion.refs_0_), channel_id=1, source_target_pairs={{0,8},{2,10},{4,12},{6,14},{8,0},{10,2},{12,4},{14,6},{1,9},{3,11}... | collective-permute-start | bytes 786440 | tf_op jit(solution)/shard_map/ppermute | solution.py:151
  7.6 1.7 collective-permute-start.3
  12.3 3.9 %collective-permute-done.refs_1_ = bf16[128,1024]{1,0:T(8,128)(2,1)S(1)} collective-permute-done((bf16[128,1024]{1,0:T(8,128)(2,1)S(1)}, bf16[128,1024]{1,0:T(8,128)(2,1)S(1)}, u32[]{:S(2)}, u32[]{:S(2)}) %collective-permute-start) | collective-permute-done | bytes 262176 | tf_op jit(solution)/shard_map/ppermute | solution.py:151
  16.2 1.7 collective-permute-start.4
  17.9 8.5 %collective-permute-done.1.refs_2_ = bf16[128,1024]{1,0:T(8,128)(2,1)S(1)} collective-permute-done((bf16[128,1024]{1,0:T(8,128)(2,1)S(1)}, bf16[128,1024]{1,0:T(8,128)(2,1)S(1)}, u32[]{:S(2)}, u32[]{:S(2)}) %collective-permute-start.1) | collective-permute-done | bytes 262176 | tf_op jit(solution)/shard_map/ppermute | solution.py:151
  26.4 1.5 collective-permute-start.5
  30.7 2.1 %collective-permute-done.5.refs_6_ = bf16[128,1024]{1,0:T(8,128)(2,1)S(1)} collective-permute-done((bf16[128,1024]{1,0:T(8,128)(2,1)S(1)}, bf16[128,1024]{1,0:T(8,128)(2,1)S(1)}, u32[]{:S(2)}, u32[]{:S(2)}) %collective-permute-start.5) | collective-permute-done | bytes 262176 | tf_op jit(solution)/shard_map/ppermute | solution.py:148
  32.8 2.8 %collective-permute-done.6.refs_7_ = bf16[128,1024]{1,0:T(8,128)(2,1)S(1)} collective-permute-done((bf16[128,1024]{1,0:T(8,128)(2,1)S(1)}, bf16[128,1024]{1,0:T(8,128)(2,1)S(1)}, u32[]{:S(2)}, u32[]{:S(2)}) %collective-permute-start.6) | collective-permute-done | bytes 262176 | tf_op jit(solution)/shard_map/ppermute | solution.py:148
  36.4 6.2 %attend.1 = (f32[128,2048]{1,0:T(8,128)}, f32[128,128]{1,0:T(8,128)}) custom-call(bf16[128,2048]{1,0:T(8,128)(2,1)} %q_ref.1, bf16[128,2048]{1,0:T(8,128)(2,1)} %constant_dynamic-slice_fusion.resid_ref, bf16[128,1024]{1,0:T(8,128)(2,1)} %copy-done.9, bf16[128,1024]{1,0:T(8,128)(2,1)} %copy-done.11, bf16[128,1024]{1,0:T(8,128)(2,1)} %copy-done.12, ...), custom_call_target="tpu_custom_call" | custom-call | flops 1073741824 | bytes 4194304 | tf_op jit(solution)/shard_map/attend/pallas_call | solution.py:177
  42.5 1.5 collective-permute-start.7
  44.7 2.3 %collective-permute-done.7.other_ref = f32[128,128]{1,0:T(8,128)S(1)} collective-permute-done((f32[128,128]{1,0:T(8,128)}, f32[128,128]{1,0:T(8,128)S(1)}, u32[]{:S(2)}, u32[]{:S(2)}) %collective-permute-start.7) | collective-permute-done | bytes 65568 | tf_op jit(solution)/shard_map/ppermute | solution.py:145
  49.0 1.3 pick.1
  50.4 2.5 %collective-permute-start.31 = (bf16[80,2048]{1,0:T(8,128)(2,1)}, bf16[80,2048]{1,0:T(8,128)(2,1)}, u32[]{:S(2)}, u32[]{:S(2)}) collective-permute-start(bf16[80,2048]{1,0:T(8,128)(2,1)} %get-tuple-element.30), channel_id=1, source_target_pairs={{0,12},{2,14},{4,8},{6,10},{8,4},{10,6},{12,0},{14,2},{1,13},{3,15... | collective-permute-start | bytes 983048 | tf_op jit(solution)/shard_map/ppermute | solution.py:151
  53.7 1.5 collective-permute-start.10
  55.2 1.5 collective-permute-start.8
  56.7 1.6 dynamic-slice_bitcast_fusion
  59.9 1.5 collective-permute-start.23
  62.8 1.6 collective-permute-start.11
  67.0 10.1 %collective-permute-done.23 = bf16[80,2048]{1,0:T(8,128)(2,1)S(1)} collective-permute-done((bf16[80,2048]{1,0:T(8,128)(2,1)}, bf16[80,2048]{1,0:T(8,128)(2,1)S(1)}, u32[]{:S(2)}, u32[]{:S(2)}) %collective-permute-start.23) | collective-permute-done | bytes 327712 | tf_op jit(solution)/shard_map/ppermute | solution.py:151
  77.0 1.5 collective-permute-start.34
  78.6 1.6 collective-permute-start.32
  80.2 21.2 %collective-permute-done.11 = bf16[2,80,1024]{2,1,0:T(8,128)(2,1)S(1)} collective-permute-done((bf16[2,80,1024]{2,1,0:T(8,128)(2,1)S(1)}, bf16[2,80,1024]{2,1,0:T(8,128)(2,1)S(1)}, u32[]{:S(2)}, u32[]{:S(2)}) %collective-permute-start.11) | collective-permute-done | bytes 327712 | tf_op jit(solution)/shard_map/ppermute | solution.py:145
  102.0 1.9 %copy-done.2 = bf16[1,4096,384]{2,1,0:T(8,128)(2,1)S(1)} copy-done((bf16[1,4096,384]{2,1,0:T(8,128)(2,1)S(1)}, bf16[1,4096,384]{2,1,0:T(8,128)(2,1)}, u32[]{:S(2)}) %copy-start.2) | copy-done | bytes 3145752
  103.9 2.1 %hidden.4.own_act = bf16[160,384]{1,0:T(8,128)(2,1)S(1)} custom-call(s32[1]{0:T(128)} %bitcast.4.sec_ref, bf16[80,1024]{1,0:T(8,128)(2,1)S(1)} %get-tuple-element.68.refs_0_, bf16[80,1024]{1,0:T(8,128)(2,1)S(1)} %get-tuple-element.70.refs_1_, bf16[80,1024]{1,0:T(8,128)(2,1)S(1)} %get-tuple-element.67.refs_2_, ...), custom_call_target="tpu_custom_call" | custom-call | flops 1006632960 | bytes 6291456 | tf_op jit(solution)/shard_map/hidden/pallas_call | solution.py:213
  106.1 1.6 collective-permute-start.18
  107.7 2.1 %collective-permute-start.16 = (bf16[80,1024]{1,0:T(8,128)(2,1)S(1)}, bf16[80,1024]{1,0:T(8,128)(2,1)S(1)}, u32[]{:S(2)}, u32[]{:S(2)}) collective-permute-start(bf16[80,1024]{1,0:T(8,128)(2,1)S(1)} %get-tuple-element.60.refs_0_), channel_id=1, source_target_pairs={{0,16},{16,0},{1,17},{17,1},{2,18},{18,2},{3,19},{19,3},{4,20},{20... | collective-permute-start | bytes 491528 | tf_op jit(solution)/shard_map/ppermute | solution.py:145
  109.9 2.1 %collective-permute-start.35 = (bf16[2,80,1024]{2,1,0:T(8,128)(2,1)S(1)}, bf16[2,80,1024]{2,1,0:T(8,128)(2,1)S(1)}, u32[]{:S(2)}, u32[]{:S(2)}) collective-permute-start(bf16[2,80,1024]{2,1,0:T(8,128)(2,1)S(1)} %pad_maximum_fusion.7), channel_id=1, source_target_pairs={{0,16},{16,0},{1,17},{17,1},{2,18},{18,2},{3,19},{19,3},{4,20},{20... | collective-permute-start | bytes 983048 | tf_op jit(solution)/shard_map/ppermute | solution.py:145
  112.1 1.8 collective-permute-start.33
  114.9 2.0 %collective-permute-start.27 = (bf16[2,80,1024]{2,1,0:T(8,128)(2,1)S(1)}, bf16[2,80,1024]{2,1,0:T(8,128)(2,1)S(1)}, u32[]{:S(2)}, u32[]{:S(2)}) collective-permute-start(bf16[2,80,1024]{2,1,0:T(8,128)(2,1)S(1)} %pad_maximum_fusion.5), channel_id=1, source_target_pairs={{0,16},{16,0},{1,17},{17,1},{2,18},{18,2},{3,19},{19,3},{4,20},{20... | collective-permute-start | bytes 983048 | tf_op jit(solution)/shard_map/ppermute | solution.py:145
  116.9 7.5 %collective-permute-done.35 = bf16[2,80,1024]{2,1,0:T(8,128)(2,1)S(1)} collective-permute-done((bf16[2,80,1024]{2,1,0:T(8,128)(2,1)S(1)}, bf16[2,80,1024]{2,1,0:T(8,128)(2,1)S(1)}, u32[]{:S(2)}, u32[]{:S(2)}) %collective-permute-start.35) | collective-permute-done | bytes 327712 | tf_op jit(solution)/shard_map/ppermute | solution.py:145
  126.1 2.2 %hidden.7.own_act = bf16[160,384]{1,0:T(8,128)(2,1)S(1)} custom-call(s32[1]{0:T(128)} %bitcast.4.sec_ref, bf16[80,1024]{1,0:T(8,128)(2,1)S(1)} %get-tuple-element.44.refs_0_, bf16[80,1024]{1,0:T(8,128)(2,1)S(1)} %get-tuple-element.46.refs_1_, bf16[80,1024]{1,0:T(8,128)(2,1)S(1)} %get-tuple-element.43.refs_2_, ...), custom_call_target="tpu_custom_call" | custom-call | flops 1006632960 | bytes 6291456 | tf_op jit(solution)/shard_map/hidden/pallas_call | solution.py:213
  128.3 1.8 collective-permute-done.27
  130.1 2.8 %collective-permute-done.25 = bf16[2,80,1024]{2,1,0:T(8,128)(2,1)S(1)} collective-permute-done((bf16[2,80,1024]{2,1,0:T(8,128)(2,1)S(1)}, bf16[2,80,1024]{2,1,0:T(8,128)(2,1)S(1)}, u32[]{:S(2)}, u32[]{:S(2)}) %collective-permute-start.25) | collective-permute-done | bytes 327712 | tf_op jit(solution)/shard_map/ppermute | solution.py:148
  132.9 2.3 %hidden.6.own_act = bf16[160,384]{1,0:T(8,128)(2,1)S(1)} custom-call(s32[1]{0:T(128)} %bitcast.4.sec_ref, bf16[80,1024]{1,0:T(8,128)(2,1)S(1)} %get-tuple-element.52.refs_0_, bf16[80,1024]{1,0:T(8,128)(2,1)S(1)} %get-tuple-element.54.refs_1_, bf16[80,1024]{1,0:T(8,128)(2,1)S(1)} %get-tuple-element.51.refs_2_, ...), custom_call_target="tpu_custom_call" | custom-call | flops 1006632960 | bytes 6291456 | tf_op jit(solution)/shard_map/hidden/pallas_call | solution.py:213
  135.2 2.1 %collective-permute-start.28 = (bf16[160,384]{1,0:T(8,128)(2,1)S(1)}, bf16[160,384]{1,0:T(8,128)(2,1)S(1)}, u32[]{:S(2)}, u32[]{:S(2)}) collective-permute-start(bf16[160,384]{1,0:T(8,128)(2,1)S(1)} %hidden.6.own_act), channel_id=1, source_target_pairs={{0,16},{16,0},{1,17},{17,1},{2,18},{18,2},{3,19},{19,3},{4,20},{20... | collective-permute-start | bytes 368648 | tf_op jit(solution)/shard_map/ppermute | solution.py:145
  137.4 3.3 %collective-permute-done.17 = bf16[2,80,1024]{2,1,0:T(8,128)(2,1)S(1)} collective-permute-done((bf16[2,80,1024]{2,1,0:T(8,128)(2,1)S(1)}, bf16[2,80,1024]{2,1,0:T(8,128)(2,1)S(1)}, u32[]{:S(2)}, u32[]{:S(2)}) %collective-permute-start.17) | collective-permute-done | bytes 327712 | tf_op jit(solution)/shard_map/ppermute | solution.py:148
  140.7 2.2 %hidden.5.own_act = bf16[160,384]{1,0:T(8,128)(2,1)S(1)} custom-call(s32[1]{0:T(128)} %bitcast.4.sec_ref, bf16[80,1024]{1,0:T(8,128)(2,1)S(1)} %get-tuple-element.60.refs_0_, bf16[80,1024]{1,0:T(8,128)(2,1)S(1)} %get-tuple-element.62.refs_1_, bf16[80,1024]{1,0:T(8,128)(2,1)S(1)} %get-tuple-element.59.refs_2_, ...), custom_call_target="tpu_custom_call" | custom-call | flops 1006632960 | bytes 6291456 | tf_op jit(solution)/shard_map/hidden/pallas_call | solution.py:213
  143.6 2.2 %down.7 = (f32[80,2048]{1,0:T(8,128)S(1)}, bf16[80,2048]{1,0:T(8,128)(2,1)S(1)}) custom-call(bf16[160,384]{1,0:T(8,128)(2,1)S(1)} %hidden.7.own_act, bf16[160,384]{1,0:T(8,128)(2,1)S(1)} %collective-permute-done.36.other_act, bf16[384,2048]{1,0:T(8,128)(2,1)S(1)} %get-tuple-element.38.own_w, bf16[384,2048]{1,0:T(8,128)(2,1)} %collective-permute-done.13.other_w), custom_call_target="tpu_custom_call" | custom-call | flops 503316480 | bytes 3145728 | tf_op jit(solution)/shard_map/down/pallas_call | solution.py:228
  146.2 2.2 %down.6 = (f32[80,2048]{1,0:T(8,128)S(1)}, bf16[80,2048]{1,0:T(8,128)(2,1)S(1)}) custom-call(bf16[160,384]{1,0:T(8,128)(2,1)S(1)} %hidden.6.own_act, bf16[160,384]{1,0:T(8,128)(2,1)S(1)} %collective-permute-done.28.other_act, bf16[384,2048]{1,0:T(8,128)(2,1)S(1)} %get-tuple-element.38.own_w, bf16[384,2048]{1,0:T(8,128)(2,1)} %collective-permute-done.13.other_w), custom_call_target="tpu_custom_call" | custom-call | flops 503316480 | bytes 3145728 | tf_op jit(solution)/shard_map/down/pallas_call | solution.py:228
  148.5 1.9 %collective-permute-start.29 = (bf16[80,2048]{1,0:T(8,128)(2,1)S(1)}, bf16[80,2048]{1,0:T(8,128)(2,1)S(1)}, u32[]{:S(2)}, u32[]{:S(2)}) collective-permute-start(bf16[80,2048]{1,0:T(8,128)(2,1)S(1)} %get-tuple-element.29), channel_id=1, source_target_pairs={{0,2},{2,0},{4,6},{6,4},{8,10},{10,8},{12,14},{14,12},{1,3},{3,1},... | collective-permute-start | bytes 983048 | tf_op jit(solution)/shard_map/ppermute | solution.py:148
  150.4 2.2 %down.5 = (f32[80,2048]{1,0:T(8,128)S(1)}, bf16[80,2048]{1,0:T(8,128)(2,1)S(1)}) custom-call(bf16[160,384]{1,0:T(8,128)(2,1)S(1)} %hidden.5.own_act, bf16[160,384]{1,0:T(8,128)(2,1)S(1)} %collective-permute-done.20.other_act, bf16[384,2048]{1,0:T(8,128)(2,1)S(1)} %get-tuple-element.38.own_w, bf16[384,2048]{1,0:T(8,128)(2,1)} %collective-permute-done.13.other_w), custom_call_target="tpu_custom_call" | custom-call | flops 503316480 | bytes 3145728 | tf_op jit(solution)/shard_map/down/pallas_call | solution.py:228
  152.9 2.2 %down.4 = (f32[80,2048]{1,0:T(8,128)S(1)}, bf16[80,2048]{1,0:T(8,128)(2,1)S(1)}) custom-call(bf16[160,384]{1,0:T(8,128)(2,1)S(1)} %hidden.4.own_act, bf16[160,384]{1,0:T(8,128)(2,1)S(1)} %collective-permute-done.12.other_act, bf16[384,2048]{1,0:T(8,128)(2,1)S(1)} %get-tuple-element.38.own_w, bf16[384,2048]{1,0:T(8,128)(2,1)} %collective-permute-done.13.other_w), custom_call_target="tpu_custom_call" | custom-call | flops 503316480 | bytes 3145728 | tf_op jit(solution)/shard_map/down/pallas_call | solution.py:228
  155.2 1.9 %collective-permute-start.14 = (bf16[80,2048]{1,0:T(8,128)(2,1)S(1)}, bf16[80,2048]{1,0:T(8,128)(2,1)S(1)}, u32[]{:S(2)}, u32[]{:S(2)}) collective-permute-start(bf16[80,2048]{1,0:T(8,128)(2,1)S(1)} %get-tuple-element.23), channel_id=1, source_target_pairs={{0,2},{2,0},{4,6},{6,4},{8,10},{10,8},{12,14},{14,12},{1,3},{3,1},... | collective-permute-start | bytes 983048 | tf_op jit(solution)/shard_map/ppermute | solution.py:148
  158.1 6.4 %collective-permute-start.30 = (bf16[80,2048]{1,0:T(8,128)(2,1)S(1)}, bf16[80,2048]{1,0:T(8,128)(2,1)S(1)}, u32[]{:S(2)}, u32[]{:S(2)}) collective-permute-start(bf16[80,2048]{1,0:T(8,128)(2,1)S(1)} %add_convert_fusion.1), channel_id=1, source_target_pairs={{0,8},{2,10},{4,12},{6,14},{8,0},{10,2},{12,4},{14,6},{1,9},{3,11}... | collective-permute-start | bytes 983048 | tf_op jit(solution)/shard_map/ppermute | solution.py:151
  164.5 1.3 collective-permute-start.22
  166.1 10.5 %collective-permute-done.30.refs_2_ = bf16[80,2048]{1,0:T(8,128)(2,1)S(1)} collective-permute-done((bf16[80,2048]{1,0:T(8,128)(2,1)S(1)}, bf16[80,2048]{1,0:T(8,128)(2,1)S(1)}, u32[]{:S(2)}, u32[]{:S(2)}) %collective-permute-start.30) | collective-permute-done | bytes 327712 | tf_op jit(solution)/shard_map/ppermute | solution.py:151
  176.6 2.0 %combine.1 = bf16[128,2048]{1,0:T(8,128)(2,1)} custom-call(f32[128,2048]{1,0:T(8,128)S(1)} %copy-done.4, bf16[4,128,80]{2,1,0:T(8,128)(2,1)S(1)} %get-tuple-element.36.high_ref, bf16[4,128,80]{2,1,0:T(8,128)(2,1)S(1)} %get-tuple-element.35.low_ref, bf16[80,2048]{1,0:T(8,128)(2,1)S(1)} %add_convert_fusion.3.refs_0_, ...), custom_call_target="tpu_custom_call" | custom-call | flops 335544320 | bytes 2883584 | tf_op jit(solution)/shard_map/combine/pallas_call | solution.py:251
  (124 shorter events, 23.9 us)
Async XLA Ops:
  0.0 29.8 %copy-start = (bf16[128,4096]{1,0:T(8,128)(2,1)S(1)}, bf16[128,4096]{1,0:T(8,128)(2,1)}, u32[]{:S(2)}) copy-start(bf16[128,4096]{1,0:T(8,128)(2,1)} %param.10) | copy-start | bytes 3145732
  1.9 33.7 %copy-start.9 = (bf16[128,1024]{1,0:T(8,128)(2,1)}, bf16[128,1024]{1,0:T(8,128)(2,1)S(1)}, u32[]{:S(2)}) copy-start(bf16[128,1024]{1,0:T(8,128)(2,1)S(1)} %constant_dynamic-update-slice_fusion.refs_0_) | copy-start | bytes 786436
  1.9 14.2 %collective-permute-start = (bf16[128,1024]{1,0:T(8,128)(2,1)S(1)}, bf16[128,1024]{1,0:T(8,128)(2,1)S(1)}, u32[]{:S(2)}, u32[]{:S(2)}) collective-permute-start(bf16[128,1024]{1,0:T(8,128)(2,1)S(1)} %constant_dynamic-update-slice_fusion.refs_0_), channel_id=1, source_target_pairs={{0,4},{2,6},{4,0},{6,2},{8,12},{10,14},{12,8},{14,10},{1,5},{3,7},... | collective-permute-start | bytes 786440 | tf_op jit(solution)/shard_map/ppermute | solution.py:151
  5.0 21.4 %collective-permute-start.1 = (bf16[128,1024]{1,0:T(8,128)(2,1)S(1)}, bf16[128,1024]{1,0:T(8,128)(2,1)S(1)}, u32[]{:S(2)}, u32[]{:S(2)}) collective-permute-start(bf16[128,1024]{1,0:T(8,128)(2,1)S(1)} %constant_dynamic-update-slice_fusion.refs_0_), channel_id=1, source_target_pairs={{0,8},{2,10},{4,12},{6,14},{8,0},{10,2},{12,4},{14,6},{1,9},{3,11}... | collective-permute-start | bytes 786440 | tf_op jit(solution)/shard_map/ppermute | solution.py:151
  7.6 20.3 %collective-permute-start.2 = (bf16[128,1024]{1,0:T(8,128)(2,1)S(1)}, bf16[128,1024]{1,0:T(8,128)(2,1)S(1)}, u32[]{:S(2)}, u32[]{:S(2)}) collective-permute-start(bf16[128,1024]{1,0:T(8,128)(2,1)S(1)} %constant_dynamic-update-slice_fusion.refs_0_), channel_id=1, source_target_pairs={{0,12},{2,14},{4,8},{6,10},{8,4},{10,6},{12,0},{14,2},{1,13},{3,15... | collective-permute-start | bytes 786440 | tf_op jit(solution)/shard_map/ppermute | solution.py:151
  7.6 23.0 %collective-permute-start.3 = (bf16[128,1024]{1,0:T(8,128)(2,1)S(1)}, bf16[128,1024]{1,0:T(8,128)(2,1)S(1)}, u32[]{:S(2)}, u32[]{:S(2)}) collective-permute-start(bf16[128,1024]{1,0:T(8,128)(2,1)S(1)} %constant_dynamic-update-slice_fusion.refs_0_), channel_id=1, source_target_pairs={{0,2},{2,0},{4,6},{6,4},{8,10},{10,8},{12,14},{14,12},{1,3},{3,1},... | collective-permute-start | bytes 786440 | tf_op jit(solution)/shard_map/ppermute | solution.py:148
  16.2 19.4 %copy-start.11 = (bf16[128,1024]{1,0:T(8,128)(2,1)}, bf16[128,1024]{1,0:T(8,128)(2,1)S(1)}, u32[]{:S(2)}) copy-start(bf16[128,1024]{1,0:T(8,128)(2,1)S(1)} %collective-permute-done.refs_1_) | copy-start | bytes 786436
  16.2 14.5 %collective-permute-start.4 = (bf16[128,1024]{1,0:T(8,128)(2,1)S(1)}, bf16[128,1024]{1,0:T(8,128)(2,1)S(1)}, u32[]{:S(2)}, u32[]{:S(2)}) collective-permute-start(bf16[128,1024]{1,0:T(8,128)(2,1)S(1)} %collective-permute-done.refs_1_), channel_id=1, source_target_pairs={{0,2},{2,0},{4,6},{6,4},{8,10},{10,8},{12,14},{14,12},{1,3},{3,1},... | collective-permute-start | bytes 786440 | tf_op jit(solution)/shard_map/ppermute | solution.py:148
  26.4 9.2 %copy-start.12 = (bf16[128,1024]{1,0:T(8,128)(2,1)}, bf16[128,1024]{1,0:T(8,128)(2,1)S(1)}, u32[]{:S(2)}) copy-start(bf16[128,1024]{1,0:T(8,128)(2,1)S(1)} %collective-permute-done.1.refs_2_) | copy-start | bytes 786436
  26.4 6.4 %collective-permute-start.5 = (bf16[128,1024]{1,0:T(8,128)(2,1)S(1)}, bf16[128,1024]{1,0:T(8,128)(2,1)S(1)}, u32[]{:S(2)}, u32[]{:S(2)}) collective-permute-start(bf16[128,1024]{1,0:T(8,128)(2,1)S(1)} %collective-permute-done.1.refs_2_), channel_id=1, source_target_pairs={{0,2},{2,0},{4,6},{6,4},{8,10},{10,8},{12,14},{14,12},{1,3},{3,1},... | collective-permute-start | bytes 786440 | tf_op jit(solution)/shard_map/ppermute | solution.py:148
  27.9 7.7 %collective-permute-start.6 = (bf16[128,1024]{1,0:T(8,128)(2,1)S(1)}, bf16[128,1024]{1,0:T(8,128)(2,1)S(1)}, u32[]{:S(2)}, u32[]{:S(2)}) collective-permute-start(bf16[128,1024]{1,0:T(8,128)(2,1)S(1)} %collective-permute-done.2.refs_3_), channel_id=1, source_target_pairs={{0,2},{2,0},{4,6},{6,4},{8,10},{10,8},{12,14},{14,12},{1,3},{3,1},... | collective-permute-start | bytes 786440 | tf_op jit(solution)/shard_map/ppermute | solution.py:148
  30.7 13.3 %copy-start.10 = (f32[128,2]{0,1:T(2,128)S(1)}, f32[128,2]{0,1:T(2,128)}, u32[]{:S(2)}) copy-start(f32[128,2]{0,1:T(2,128)} %param.16) | copy-start | bytes 3076
  36.3 20.3 %copy-start.8 = (bf16[1,384,4096]{2,1,0:T(8,128)(2,1)S(1)}, bf16[1,384,4096]{2,1,0:T(8,128)(2,1)}, u32[]{:S(2)}) copy-start(bf16[1,384,4096]{2,1,0:T(8,128)(2,1)} %param.19) | copy-start | bytes 9437188
  42.5 4.5 %collective-permute-start.7 = (f32[128,128]{1,0:T(8,128)}, f32[128,128]{1,0:T(8,128)S(1)}, u32[]{:S(2)}, u32[]{:S(2)}) collective-permute-start(f32[128,128]{1,0:T(8,128)} %get-tuple-element.20.own_ref), channel_id=1, source_target_pairs={{0,16},{16,0},{1,17},{17,1},{2,18},{18,2},{3,19},{19,3},{4,20},{20... | collective-permute-start | bytes 196616 | tf_op jit(solution)/shard_map/ppermute | solution.py:145
  50.4 7.9 %copy-start.7 = (bf16[80,2048]{1,0:T(8,128)(2,1)}, bf16[80,2048]{1,0:T(8,128)(2,1)S(1)}, u32[]{:S(2)}) copy-start(bf16[80,2048]{1,0:T(8,128)(2,1)S(1)} %get-tuple-element.27) | copy-start | bytes 983044
  50.4 14.9 %collective-permute-start.31 = (bf16[80,2048]{1,0:T(8,128)(2,1)}, bf16[80,2048]{1,0:T(8,128)(2,1)}, u32[]{:S(2)}, u32[]{:S(2)}) collective-permute-start(bf16[80,2048]{1,0:T(8,128)(2,1)} %get-tuple-element.30), channel_id=1, source_target_pairs={{0,12},{2,14},{4,8},{6,10},{8,4},{10,6},{12,0},{14,2},{1,13},{3,15... | collective-permute-start | bytes 983048 | tf_op jit(solution)/shard_map/ppermute | solution.py:151
  53.7 7.7 %collective-permute-start.10 = (bf16[80,1024]{1,0:T(8,128)(2,1)S(1)}, bf16[80,1024]{1,0:T(8,128)(2,1)S(1)}, u32[]{:S(2)}, u32[]{:S(2)}) collective-permute-start(bf16[80,1024]{1,0:T(8,128)(2,1)S(1)} %get-tuple-element.67.refs_2_), channel_id=1, source_target_pairs={{0,2},{2,0},{4,6},{6,4},{8,10},{10,8},{12,14},{14,12},{1,3},{3,1},... | collective-permute-start | bytes 491528 | tf_op jit(solution)/shard_map/ppermute | solution.py:148
  55.2 7.6 %collective-permute-start.8 = (bf16[80,1024]{1,0:T(8,128)(2,1)S(1)}, bf16[80,1024]{1,0:T(8,128)(2,1)S(1)}, u32[]{:S(2)}, u32[]{:S(2)}) collective-permute-start(bf16[80,1024]{1,0:T(8,128)(2,1)S(1)} %get-tuple-element.68.refs_0_), channel_id=1, source_target_pairs={{0,16},{16,0},{1,17},{17,1},{2,18},{18,2},{3,19},{19,3},{4,20},{20... | collective-permute-start | bytes 491528 | tf_op jit(solution)/shard_map/ppermute | solution.py:145
  58.3 85.4 %collective-permute-start.13 = (bf16[384,2048]{1,0:T(8,128)(2,1)}, bf16[384,2048]{1,0:T(8,128)(2,1)}, u32[]{:S(2)}, u32[]{:S(2)}) collective-permute-start(bf16[384,2048]{1,0:T(8,128)(2,1)} %get-tuple-element.37), channel_id=1, source_target_pairs={{0,16},{16,0},{1,17},{17,1},{2,18},{18,2},{3,19},{19,3},{4,20},{20... | collective-permute-start | bytes 4718600 | tf_op jit(solution)/shard_map/ppermute | solution.py:145
  59.9 17.2 %collective-permute-start.23 = (bf16[80,2048]{1,0:T(8,128)(2,1)}, bf16[80,2048]{1,0:T(8,128)(2,1)S(1)}, u32[]{:S(2)}, u32[]{:S(2)}) collective-permute-start(bf16[80,2048]{1,0:T(8,128)(2,1)} %copy-done.7), channel_id=1, source_target_pairs={{0,8},{2,10},{4,12},{6,14},{8,0},{10,2},{12,4},{14,6},{1,9},{3,11}... | collective-permute-start | bytes 983048 | tf_op jit(solution)/shard_map/ppermute | solution.py:151
  61.4 17.2 %collective-permute-start.15 = (bf16[80,2048]{1,0:T(8,128)(2,1)}, bf16[80,2048]{1,0:T(8,128)(2,1)S(1)}, u32[]{:S(2)}, u32[]{:S(2)}) collective-permute-start(bf16[80,2048]{1,0:T(8,128)(2,1)} %copy-done.6), channel_id=1, source_target_pairs={{0,4},{2,6},{4,0},{6,2},{8,12},{10,14},{12,8},{14,10},{1,5},{3,7},... | collective-permute-start | bytes 983048 | tf_op jit(solution)/shard_map/ppermute | solution.py:151
  62.8 38.6 %collective-permute-start.11 = (bf16[2,80,1024]{2,1,0:T(8,128)(2,1)S(1)}, bf16[2,80,1024]{2,1,0:T(8,128)(2,1)S(1)}, u32[]{:S(2)}, u32[]{:S(2)}) collective-permute-start(bf16[2,80,1024]{2,1,0:T(8,128)(2,1)S(1)} %pad_maximum_fusion.1), channel_id=1, source_target_pairs={{0,16},{16,0},{1,17},{17,1},{2,18},{18,2},{3,19},{19,3},{4,20},{20... | collective-permute-start | bytes 983048 | tf_op jit(solution)/shard_map/ppermute | solution.py:145
  65.3 36.6 %collective-permute-start.9 = (bf16[2,80,1024]{2,1,0:T(8,128)(2,1)S(1)}, bf16[2,80,1024]{2,1,0:T(8,128)(2,1)S(1)}, u32[]{:S(2)}, u32[]{:S(2)}) collective-permute-start(bf16[2,80,1024]{2,1,0:T(8,128)(2,1)S(1)} %pad_maximum_fusion), channel_id=1, source_target_pairs={{0,2},{2,0},{4,6},{6,4},{8,10},{10,8},{12,14},{14,12},{1,3},{3,1},... | collective-permute-start | bytes 983048 | tf_op jit(solution)/shard_map/ppermute | solution.py:148
  77.0 25.0 %copy-start.1 = (bf16[1,4096,384]{2,1,0:T(8,128)(2,1)S(1)}, bf16[1,4096,384]{2,1,0:T(8,128)(2,1)}, u32[]{:S(2)}) copy-start(bf16[1,4096,384]{2,1,0:T(8,128)(2,1)} %param.17) | copy-start | bytes 9437188
  77.0 29.0 %collective-permute-start.34 = (bf16[80,1024]{1,0:T(8,128)(2,1)S(1)}, bf16[80,1024]{1,0:T(8,128)(2,1)S(1)}, u32[]{:S(2)}, u32[]{:S(2)}) collective-permute-start(bf16[80,1024]{1,0:T(8,128)(2,1)S(1)} %get-tuple-element.43.refs_2_), channel_id=1, source_target_pairs={{0,2},{2,0},{4,6},{6,4},{8,10},{10,8},{12,14},{14,12},{1,3},{3,1},... | collective-permute-start | bytes 491528 | tf_op jit(solution)/shard_map/ppermute | solution.py:148
  78.6 29.1 %collective-permute-start.32 = (bf16[80,1024]{1,0:T(8,128)(2,1)S(1)}, bf16[80,1024]{1,0:T(8,128)(2,1)S(1)}, u32[]{:S(2)}, u32[]{:S(2)}) collective-permute-start(bf16[80,1024]{1,0:T(8,128)(2,1)S(1)} %get-tuple-element.44.refs_0_), channel_id=1, source_target_pairs={{0,16},{16,0},{1,17},{17,1},{2,18},{18,2},{3,19},{19,3},{4,20},{20... | collective-permute-start | bytes 491528 | tf_op jit(solution)/shard_map/ppermute | solution.py:145
  101.4 8.4 %collective-permute-start.26 = (bf16[80,1024]{1,0:T(8,128)(2,1)S(1)}, bf16[80,1024]{1,0:T(8,128)(2,1)S(1)}, u32[]{:S(2)}, u32[]{:S(2)}) collective-permute-start(bf16[80,1024]{1,0:T(8,128)(2,1)S(1)} %get-tuple-element.51.refs_2_), channel_id=1, source_target_pairs={{0,2},{2,0},{4,6},{6,4},{8,10},{10,8},{12,14},{14,12},{1,3},{3,1},... | collective-permute-start | bytes 491528 | tf_op jit(solution)/shard_map/ppermute | solution.py:148
  101.9 8.0 %collective-permute-start.24 = (bf16[80,1024]{1,0:T(8,128)(2,1)S(1)}, bf16[80,1024]{1,0:T(8,128)(2,1)S(1)}, u32[]{:S(2)}, u32[]{:S(2)}) collective-permute-start(bf16[80,1024]{1,0:T(8,128)(2,1)S(1)} %get-tuple-element.52.refs_0_), channel_id=1, source_target_pairs={{0,16},{16,0},{1,17},{17,1},{2,18},{18,2},{3,19},{19,3},{4,20},{20... | collective-permute-start | bytes 491528 | tf_op jit(solution)/shard_map/ppermute | solution.py:145
  106.1 6.0 %collective-permute-start.18 = (bf16[80,1024]{1,0:T(8,128)(2,1)S(1)}, bf16[80,1024]{1,0:T(8,128)(2,1)S(1)}, u32[]{:S(2)}, u32[]{:S(2)}) collective-permute-start(bf16[80,1024]{1,0:T(8,128)(2,1)S(1)} %get-tuple-element.59.refs_2_), channel_id=1, source_target_pairs={{0,2},{2,0},{4,6},{6,4},{8,10},{10,8},{12,14},{14,12},{1,3},{3,1},... | collective-permute-start | bytes 491528 | tf_op jit(solution)/shard_map/ppermute | solution.py:148
  107.7 7.2 %collective-permute-start.16 = (bf16[80,1024]{1,0:T(8,128)(2,1)S(1)}, bf16[80,1024]{1,0:T(8,128)(2,1)S(1)}, u32[]{:S(2)}, u32[]{:S(2)}) collective-permute-start(bf16[80,1024]{1,0:T(8,128)(2,1)S(1)} %get-tuple-element.60.refs_0_), channel_id=1, source_target_pairs={{0,16},{16,0},{1,17},{17,1},{2,18},{18,2},{3,19},{19,3},{4,20},{20... | collective-permute-start | bytes 491528 | tf_op jit(solution)/shard_map/ppermute | solution.py:145
  109.8 43.1 %collective-permute-start.12 = (bf16[160,384]{1,0:T(8,128)(2,1)S(1)}, bf16[160,384]{1,0:T(8,128)(2,1)S(1)}, u32[]{:S(2)}, u32[]{:S(2)}) collective-permute-start(bf16[160,384]{1,0:T(8,128)(2,1)S(1)} %hidden.4.own_act), channel_id=1, source_target_pairs={{0,16},{16,0},{1,17},{17,1},{2,18},{18,2},{3,19},{19,3},{4,20},{20... | collective-permute-start | bytes 368648 | tf_op jit(solution)/shard_map/ppermute | solution.py:145
  109.9 14.5 %collective-permute-start.35 = (bf16[2,80,1024]{2,1,0:T(8,128)(2,1)S(1)}, bf16[2,80,1024]{2,1,0:T(8,128)(2,1)S(1)}, u32[]{:S(2)}, u32[]{:S(2)}) collective-permute-start(bf16[2,80,1024]{2,1,0:T(8,128)(2,1)S(1)} %pad_maximum_fusion.7), channel_id=1, source_target_pairs={{0,16},{16,0},{1,17},{17,1},{2,18},{18,2},{3,19},{19,3},{4,20},{20... | collective-permute-start | bytes 983048 | tf_op jit(solution)/shard_map/ppermute | solution.py:145
  112.1 12.9 %collective-permute-start.33 = (bf16[2,80,1024]{2,1,0:T(8,128)(2,1)S(1)}, bf16[2,80,1024]{2,1,0:T(8,128)(2,1)S(1)}, u32[]{:S(2)}, u32[]{:S(2)}) collective-permute-start(bf16[2,80,1024]{2,1,0:T(8,128)(2,1)S(1)} %pad_maximum_fusion.6), channel_id=1, source_target_pairs={{0,2},{2,0},{4,6},{6,4},{8,10},{10,8},{12,14},{14,12},{1,3},{3,1},... | collective-permute-start | bytes 983048 | tf_op jit(solution)/shard_map/ppermute | solution.py:148
  114.9 15.1 %collective-permute-start.27 = (bf16[2,80,1024]{2,1,0:T(8,128)(2,1)S(1)}, bf16[2,80,1024]{2,1,0:T(8,128)(2,1)S(1)}, u32[]{:S(2)}, u32[]{:S(2)}) collective-permute-start(bf16[2,80,1024]{2,1,0:T(8,128)(2,1)S(1)} %pad_maximum_fusion.5), channel_id=1, source_target_pairs={{0,16},{16,0},{1,17},{17,1},{2,18},{18,2},{3,19},{19,3},{4,20},{20... | collective-permute-start | bytes 983048 | tf_op jit(solution)/shard_map/ppermute | solution.py:145
  124.4 8.4 %collective-permute-start.25 = (bf16[2,80,1024]{2,1,0:T(8,128)(2,1)S(1)}, bf16[2,80,1024]{2,1,0:T(8,128)(2,1)S(1)}, u32[]{:S(2)}, u32[]{:S(2)}) collective-permute-start(bf16[2,80,1024]{2,1,0:T(8,128)(2,1)S(1)} %pad_maximum_fusion.4), channel_id=1, source_target_pairs={{0,2},{2,0},{4,6},{6,4},{8,10},{10,8},{12,14},{14,12},{1,3},{3,1},... | collective-permute-start | bytes 983048 | tf_op jit(solution)/shard_map/ppermute | solution.py:148
  125.0 10.3 %collective-permute-start.19 = (bf16[2,80,1024]{2,1,0:T(8,128)(2,1)S(1)}, bf16[2,80,1024]{2,1,0:T(8,128)(2,1)S(1)}, u32[]{:S(2)}, u32[]{:S(2)}) collective-permute-start(bf16[2,80,1024]{2,1,0:T(8,128)(2,1)S(1)} %pad_maximum_fusion.3), channel_id=1, source_target_pairs={{0,16},{16,0},{1,17},{17,1},{2,18},{18,2},{3,19},{19,3},{4,20},{20... | collective-permute-start | bytes 983048 | tf_op jit(solution)/shard_map/ppermute | solution.py:145
  130.0 10.6 %collective-permute-start.17 = (bf16[2,80,1024]{2,1,0:T(8,128)(2,1)S(1)}, bf16[2,80,1024]{2,1,0:T(8,128)(2,1)S(1)}, u32[]{:S(2)}, u32[]{:S(2)}) collective-permute-start(bf16[2,80,1024]{2,1,0:T(8,128)(2,1)S(1)} %pad_maximum_fusion.2), channel_id=1, source_target_pairs={{0,2},{2,0},{4,6},{6,4},{8,10},{10,8},{12,14},{14,12},{1,3},{3,1},... | collective-permute-start | bytes 983048 | tf_op jit(solution)/shard_map/ppermute | solution.py:148
  132.9 10.8 %collective-permute-start.36 = (bf16[160,384]{1,0:T(8,128)(2,1)S(1)}, bf16[160,384]{1,0:T(8,128)(2,1)S(1)}, u32[]{:S(2)}, u32[]{:S(2)}) collective-permute-start(bf16[160,384]{1,0:T(8,128)(2,1)S(1)} %hidden.7.own_act), channel_id=1, source_target_pairs={{0,16},{16,0},{1,17},{17,1},{2,18},{18,2},{3,19},{19,3},{4,20},{20... | collective-permute-start | bytes 368648 | tf_op jit(solution)/shard_map/ppermute | solution.py:145
  135.2 11.0 %collective-permute-start.28 = (bf16[160,384]{1,0:T(8,128)(2,1)S(1)}, bf16[160,384]{1,0:T(8,128)(2,1)S(1)}, u32[]{:S(2)}, u32[]{:S(2)}) collective-permute-start(bf16[160,384]{1,0:T(8,128)(2,1)S(1)} %hidden.6.own_act), channel_id=1, source_target_pairs={{0,16},{16,0},{1,17},{17,1},{2,18},{18,2},{3,19},{19,3},{4,20},{20... | collective-permute-start | bytes 368648 | tf_op jit(solution)/shard_map/ppermute | solution.py:145
  142.9 7.5 %collective-permute-start.20 = (bf16[160,384]{1,0:T(8,128)(2,1)S(1)}, bf16[160,384]{1,0:T(8,128)(2,1)S(1)}, u32[]{:S(2)}, u32[]{:S(2)}) collective-permute-start(bf16[160,384]{1,0:T(8,128)(2,1)S(1)} %hidden.5.own_act), channel_id=1, source_target_pairs={{0,16},{16,0},{1,17},{17,1},{2,18},{18,2},{3,19},{19,3},{4,20},{20... | collective-permute-start | bytes 368648 | tf_op jit(solution)/shard_map/ppermute | solution.py:145
  145.9 11.1 %collective-permute-start.37 = (bf16[80,2048]{1,0:T(8,128)(2,1)S(1)}, bf16[80,2048]{1,0:T(8,128)(2,1)S(1)}, u32[]{:S(2)}, u32[]{:S(2)}) collective-permute-start(bf16[80,2048]{1,0:T(8,128)(2,1)S(1)} %get-tuple-element.32), channel_id=1, source_target_pairs={{0,2},{2,0},{4,6},{6,4},{8,10},{10,8},{12,14},{14,12},{1,3},{3,1},... | collective-permute-start | bytes 983048 | tf_op jit(solution)/shard_map/ppermute | solution.py:148
  148.5 9.5 %collective-permute-start.29 = (bf16[80,2048]{1,0:T(8,128)(2,1)S(1)}, bf16[80,2048]{1,0:T(8,128)(2,1)S(1)}, u32[]{:S(2)}, u32[]{:S(2)}) collective-permute-start(bf16[80,2048]{1,0:T(8,128)(2,1)S(1)} %get-tuple-element.29), channel_id=1, source_target_pairs={{0,2},{2,0},{4,6},{6,4},{8,10},{10,8},{12,14},{14,12},{1,3},{3,1},... | collective-permute-start | bytes 983048 | tf_op jit(solution)/shard_map/ppermute | solution.py:148
  152.6 11.8 %collective-permute-start.21 = (bf16[80,2048]{1,0:T(8,128)(2,1)S(1)}, bf16[80,2048]{1,0:T(8,128)(2,1)S(1)}, u32[]{:S(2)}, u32[]{:S(2)}) collective-permute-start(bf16[80,2048]{1,0:T(8,128)(2,1)S(1)} %get-tuple-element.26), channel_id=1, source_target_pairs={{0,2},{2,0},{4,6},{6,4},{8,10},{10,8},{12,14},{14,12},{1,3},{3,1},... | collective-permute-start | bytes 983048 | tf_op jit(solution)/shard_map/ppermute | solution.py:148
  155.2 10.7 %collective-permute-start.14 = (bf16[80,2048]{1,0:T(8,128)(2,1)S(1)}, bf16[80,2048]{1,0:T(8,128)(2,1)S(1)}, u32[]{:S(2)}, u32[]{:S(2)}) collective-permute-start(bf16[80,2048]{1,0:T(8,128)(2,1)S(1)} %get-tuple-element.23), channel_id=1, source_target_pairs={{0,2},{2,0},{4,6},{6,4},{8,10},{10,8},{12,14},{14,12},{1,3},{3,1},... | collective-permute-start | bytes 983048 | tf_op jit(solution)/shard_map/ppermute | solution.py:148
  157.1 9.0 %collective-permute-start.38 = (bf16[80,2048]{1,0:T(8,128)(2,1)S(1)}, bf16[80,2048]{1,0:T(8,128)(2,1)S(1)}, u32[]{:S(2)}, u32[]{:S(2)}) collective-permute-start(bf16[80,2048]{1,0:T(8,128)(2,1)S(1)} %add_convert_fusion), channel_id=1, source_target_pairs={{0,12},{2,14},{4,8},{6,10},{8,4},{10,6},{12,0},{14,2},{1,13},{3,15... | collective-permute-start | bytes 983048 | tf_op jit(solution)/shard_map/ppermute | solution.py:151
  158.1 18.5 %copy-start.4 = (f32[128,2048]{1,0:T(8,128)S(1)}, f32[128,2048]{1,0:T(8,128)}, u32[]{:S(2)}) copy-start(f32[128,2048]{1,0:T(8,128)} %get-tuple-element.19.stream_ref) | copy-start | bytes 3145732
  158.1 18.5 %collective-permute-start.30 = (bf16[80,2048]{1,0:T(8,128)(2,1)S(1)}, bf16[80,2048]{1,0:T(8,128)(2,1)S(1)}, u32[]{:S(2)}, u32[]{:S(2)}) collective-permute-start(bf16[80,2048]{1,0:T(8,128)(2,1)S(1)} %add_convert_fusion.1), channel_id=1, source_target_pairs={{0,8},{2,10},{4,12},{6,14},{8,0},{10,2},{12,4},{14,6},{1,9},{3,11}... | collective-permute-start | bytes 983048 | tf_op jit(solution)/shard_map/ppermute | solution.py:151
  164.5 12.1 %collective-permute-start.22 = (bf16[80,2048]{1,0:T(8,128)(2,1)S(1)}, bf16[80,2048]{1,0:T(8,128)(2,1)S(1)}, u32[]{:S(2)}, u32[]{:S(2)}) collective-permute-start(bf16[80,2048]{1,0:T(8,128)(2,1)S(1)} %add_convert_fusion.2), channel_id=1, source_target_pairs={{0,4},{2,6},{4,0},{6,2},{8,12},{10,14},{12,8},{14,10},{1,5},{3,7},... | collective-permute-start | bytes 983048 | tf_op jit(solution)/shard_map/ppermute | solution.py:151
  (9 other events, 33.0 us)

commit v2 on v1

v2 whole, which is shorter than its diff:
```python
import functools
import math

import jax
import jax.numpy as jnp
from jax import lax
from jax.experimental import pallas as pl
from jax.experimental.pallas import tpu as pltpu
from jax.sharding import PartitionSpec as P

HD = 128
F32 = jnp.float32
BF16 = jnp.bfloat16
VMEM = pl.BlockSpec(memory_space=pltpu.VMEM)
ANY = pl.BlockSpec(memory_space=pl.ANY)


def params():
    return pltpu.CompilerParams(vmem_limit_bytes=20 * 1024 * 1024)


def cost(flops, moved):
    return pl.CostEstimate(flops=int(flops), bytes_accessed=int(moved), transcendentals=0)


def pack_kernel(keys_ref, values_ref, out_ref):
    size = keys_ref.shape[1]
    out_ref[:, :size] = keys_ref[...]
    out_ref[:, size:] = values_ref[...]


def stage_kernel(sec_ref, q_ref, resid_ref, gain_ref, q_out, resid_out, gain_out, inverse_out):
    half = q_out.shape[1]
    q_out[...] = q_ref[...]
    low = pl.multiple_of(sec_ref[0] * half, half)
    resid_out[...] = resid_ref[:, pl.ds(low, half)]
    gain_out[...] = gain_ref[:, pl.ds(low, half)]
    inverse_out[:, :half] = 1.0 / gain_ref[:, pl.ds(low, half)]
    inverse_out[:, half:] = 1.0 / gain_ref[:, pl.ds(pl.multiple_of(half - low, half), half)]


def weights_kernel(sec_ref, gate_ref, up_ref, out_ref, sems):
    half, hidden = gate_ref.shape[0] // 2, gate_ref.shape[1]
    copies = []
    for c in range(2):
        low = pl.multiple_of(lax.rem(sec_ref[0] + c, 2) * half, half)
        for n, ref in enumerate((gate_ref, up_ref)):
            target = out_ref.at[c * half : (c + 1) * half, n * hidden : (n + 1) * hidden]
            copies.append(pltpu.make_async_copy(ref.at[pl.ds(low, half)], target, sems.at[2 * c + n]))
            copies[-1].start()
    for copy in copies:
        copy.wait()


def attend_kernel(n_pieces, q_ref, resid_ref, gain_ref, pick_ref, *refs):
    kv_refs, stream_ref, outs = refs[:n_pieces], refs[n_pieces], refs[n_pieces + 1 :]
    rows = q_ref.shape[0]
    kv_here = kv_refs[0].shape[1] // (2 * HD)
    group_size = q_ref.shape[1] // HD // kv_here
    factor = math.log2(math.e) / math.sqrt(HD)
    for g in range(kv_here):
        heads = [q_ref[:, (g * group_size + r) * HD : (g * group_size + r + 1) * HD] for r in range(group_size)]
        query = jnp.concatenate(heads, axis=0)
        keys = jnp.concatenate([ref[:, g * HD : (g + 1) * HD] for ref in kv_refs], axis=0)
        values = jnp.concatenate([ref[:, (kv_here + g) * HD : (kv_here + g + 1) * HD] for ref in kv_refs], axis=0)
        scores = lax.dot_general(query, keys, (((1,), (1,)), ((), ())), preferred_element_type=F32)
        raised = jnp.exp2((scores - jnp.max(scores, axis=1, keepdims=True)) * factor)
        total = jnp.sum(raised, axis=1, keepdims=True)
        mixed = jnp.dot(raised.astype(BF16), values, preferred_element_type=F32)
        attended = (mixed / total).astype(BF16).astype(F32)
        for r in range(group_size):
            low = (g * group_size + r) * HD
            stream_ref[:, low : low + HD] = resid_ref[:, low : low + HD].astype(F32) + attended[r * rows : (r + 1) * rows]
    scaled = (stream_ref[...] * gain_ref[...]).astype(BF16)
    for k, out_ref in enumerate(outs):
        out_ref[...] = jnp.dot(pick_ref[k], scaled, preferred_element_type=F32).astype(BF16)


def attend_long(queries, resid, gain, pick, pieces):
    rows, kv_here = queries.shape[0], pieces[0].shape[1] // (2 * HD)
    grouped = queries.reshape(rows, kv_here, -1, HD)
    scale = 1.0 / math.sqrt(HD)
    state = None
    for i in range(0, len(pieces), 8):
        block = jnp.concatenate(pieces[i : i + 8], axis=0).reshape(-1, 2, kv_here, HD)
        scores = jnp.einsum("tgrd,ngd->grtn", grouped, block[:, 0], preferred_element_type=F32) * scale
        top = jnp.max(scores, axis=-1, keepdims=True)
        new_max = top if state is None else jnp.maximum(state[0], top)
        raised = jnp.exp(scores - new_max)
        total = jnp.sum(raised, axis=-1, keepdims=True)
        mixed = jnp.einsum("grtn,ngd->grtd", raised.astype(BF16), block[:, 1], preferred_element_type=F32)
        if state is not None:
            old = jnp.exp(state[0] - new_max)
            total, mixed = state[1] * old + total, state[2] * old + mixed
        state = (new_max, total, mixed)
    attended = (state[2] / state[1]).transpose(2, 0, 1, 3).reshape(rows, -1).astype(BF16)
    stream = resid.astype(F32) + attended.astype(F32)
    scaled = (stream * gain).astype(BF16)
    return [stream] + [jnp.dot(p, scaled, preferred_element_type=F32).astype(BF16) for p in pick]


def down_weights_kernel(index_ref, own_ref, near_ref, far_ref, out_ref, sems):
    hidden, quarter = near_ref.shape
    low = pl.multiple_of(index_ref[0] * 2 * quarter, quarter)
    near = pl.multiple_of(index_ref[1] * quarter, quarter)
    other = pl.multiple_of((1 - index_ref[1]) * quarter, quarter)
    copies = [
        pltpu.make_async_copy(own_ref.at[:, pl.ds(low, 2 * quarter)], out_ref.at[:hidden, :], sems.at[0]),
        pltpu.make_async_copy(near_ref, out_ref.at[hidden:, pl.ds(near, quarter)], sems.at[1]),
        pltpu.make_async_copy(far_ref, out_ref.at[hidden:, pl.ds(other, quarter)], sems.at[2]),
    ]
    for copy in copies:
        copy.start()
    for copy in copies:
        copy.wait()


def hidden_kernel(width, own_ref, y_ref, x_ref, both_ref, weights_ref, inverse_ref, act_ref):
    half, hidden = own_ref.shape[1], act_ref.shape[1]
    total = square = 0.0
    for c, refs in enumerate(((own_ref, y_ref), (x_ref, both_ref))):
        rows = jnp.concatenate([ref[...] for ref in refs], axis=0)
        columns = slice(c * half, (c + 1) * half)
        total = total + jnp.dot(rows, weights_ref[columns, :], preferred_element_type=F32)
        stream = rows.astype(F32) * inverse_ref[:, columns]
        square = square + jnp.sum(stream * stream, axis=1, keepdims=True)
    total = total * lax.rsqrt(square / width + 1e-06)
    gate, up = total[:, :hidden], total[:, hidden:]
    act_ref[...] = (gate / (1.0 + jnp.exp(-gate)) * up).astype(BF16)


def down_kernel(own_act, other_act, w_ref, keep_ref, send_ref):
    rows = keep_ref.shape[0]
    act = jnp.concatenate([own_act[...], other_act[...]], axis=1)
    total = jnp.dot(act, w_ref[...], preferred_element_type=F32)
    keep_ref[...] = total[:rows]
    send_ref[...] = total[rows:].astype(BF16)


def combine_kernel(stream_ref, high_ref, low_ref, *refs):
    returned, out_ref = refs[:-1], refs[-1]
    total = stream_ref[...]
    for k, ref in enumerate(returned):
        rows = ref[...]
        total = total + jnp.dot(high_ref[k], rows, preferred_element_type=F32)
        total = total + jnp.dot(low_ref[k], rows, preferred_element_type=F32)
    out_ref[...] = total.astype(BF16)


def near(values):
    return [pltpu.with_memory_space_constraint(v, pltpu.VMEM) for v in values]


def far(values):
    return [pltpu.with_memory_space_constraint(v, pltpu.HBM) for v in values]


def after(value, *others):
    return lax.optimization_barrier((value, *others))[0]


def body(resid, queries, keys, values, norm_gain, expert_ids, gate_weights, w_gate, w_up, w_down):
    rows, width = resid.shape
    half = width // 2
    quarter = half // 2
    n_dev = lax.axis_size("dev")
    n_exp = n_dev // 2
    topk = expert_ids.shape[1]
    cap = max(2, (rows * topk * 5 + 4 * n_exp - 1) // (4 * n_exp))
    hidden = w_gate.shape[2]
    sec = lax.axis_index("sec").astype(jnp.int32)
    rep = lax.axis_index("rep").astype(jnp.int32)
    plane = lax.axis_index("dev").astype(jnp.int32) // 2

    def over_sec(a):
        return lax.ppermute(a, "sec", [(0, 1), (1, 0)])

    def over_rep(a):
        return lax.ppermute(a, "rep", [(0, 1), (1, 0)])

    def over_y(a):
        return lax.ppermute(a, "dev", [(i, i ^ 1) for i in range(n_dev)])

    def over_z(a, k):
        return lax.ppermute(a, "dev", [(i, ((i // 2) ^ k) * 2 + i % 2) for i in range(n_dev)])

    own_kv = pl.pallas_call(
        pack_kernel,
        out_shape=jax.ShapeDtypeStruct((rows, 2 * keys.shape[1]), BF16),
        in_specs=[VMEM] * 2,
        out_specs=VMEM,
        compiler_params=params(),
        cost_estimate=cost(0, 4 * keys.size * 2),
        name="pack",
    )(keys, values)
    planes = [own_kv] + [over_z(own_kv, k) for k in range(1, n_exp)]
    pieces = planes + [over_y(a) for a in planes]

    part = lax.dynamic_slice_in_dim(w_down[0], ((1 - sec) * 2 + rep) * quarter, quarter, 1)
    down_near = over_sec(part)
    down_far = over_rep(after(down_near, pieces[n_exp + 1]))

    experts = jnp.arange(n_exp, dtype=jnp.int32)
    onehot = (expert_ids[:, :, None] == experts[None, None, :]).astype(jnp.int32)
    onehot = onehot.reshape(rows * topk, n_exp)
    earlier = jnp.cumsum(onehot, axis=0) - onehot
    slot = jnp.sum(earlier * onehot, axis=1).reshape(rows, topk)
    target = (expert_ids ^ plane) * cap + slot
    placed = target[:, :, None] == jnp.arange(n_exp * cap, dtype=jnp.int32)[None, None, :]
    pick = jnp.sum(placed.astype(F32), axis=1).astype(BF16).T.reshape(n_exp, cap, rows)
    weight = jnp.sum(jnp.where(placed, gate_weights[:, :, None], 0.0), axis=1)
    weight = weight.reshape(rows, n_exp, cap).transpose(1, 0, 2)
    weight_high = weight.astype(BF16)
    weight_low = (weight - weight_high.astype(F32)).astype(BF16)
    gain = norm_gain.reshape(1, width)
    index = jnp.stack([sec, rep])
    smem = pl.BlockSpec(memory_space=pltpu.SMEM)
    staged = pl.pallas_call(
        stage_kernel,
        out_shape=[
            pltpu.VMEM((rows, half), BF16),
            pltpu.VMEM((rows, half), BF16),
            pltpu.VMEM((1, half), F32),
            pltpu.VMEM((1, width), F32),
        ],
        in_specs=[smem] + [VMEM] * 3,
        out_specs=[VMEM] * 4,
        compiler_params=params(),
        name="stage",
    )(sec.reshape(1), *far([queries, resid, gain]))
    weights = pl.pallas_call(
        weights_kernel,
        out_shape=pltpu.VMEM((width, 2 * hidden), BF16),
        in_specs=[smem] + [ANY] * 2,
        out_specs=VMEM,
        scratch_shapes=[pltpu.SemaphoreType.DMA((4,))],
        compiler_params=params(),
        name="weights",
    )(sec.reshape(1), *far([w_gate[0], w_up[0]]))
    tied = lax.optimization_barrier((pieces[1], pick, weight_high, weight_low, index, weights, down_far, *staged))
    pieces[1], pick, weight_high, weight_low, index, weights, down_far, *staged = tied
    queries, resid, gain, inverse = staged

    if n_dev > 8:
        stream, *sent = attend_long(queries, resid, gain, pick, pieces)
    else:
        n_keys = rows * n_dev
        stream, *sent = pl.pallas_call(
            functools.partial(attend_kernel, len(pieces)),
            in_specs=[VMEM] * (4 + len(pieces)),
            out_specs=[VMEM] * (1 + n_exp),
            out_shape=[pltpu.HBM((rows, half), F32)] + [jax.ShapeDtypeStruct((cap, half), BF16)] * n_exp,
            compiler_params=params(),
            cost_estimate=cost(4 * rows * half * n_keys, n_keys * half * 2),
            name="attend",
        )(queries, resid, gain, pick, *pieces)

    arrived = [sent[0]] + [over_z(sent[k], k) for k in range(1, n_exp)]
    down_weights = pl.pallas_call(
        down_weights_kernel,
        out_shape=pltpu.VMEM((2 * hidden, half), BF16),
        in_specs=[smem] + [ANY] * 3,
        out_specs=VMEM,
        scratch_shapes=[pltpu.SemaphoreType.DMA((3,))],
        compiler_params=params(),
        name="down_weights",
    )(after(index, stream), *far([w_down[0], down_near, down_far]))
    arrived[0], down_weights = lax.optimization_barrier((arrived[0], down_weights))
    each = max(1, n_exp // 4)
    if each > 1:
        arrived = [jnp.concatenate(arrived[i : i + each], axis=0) for i in range(0, n_exp, each)]

    def plane_gather(number, own):
        if number % 2 == 0:
            from_x, from_y = over_sec(own), over_y(own)
            return own, from_y, from_x, over_y(from_x)
        from_y, from_x = over_y(own), over_sec(own)
        return own, from_y, from_x, over_sec(from_y)

    def experts_of(gathered):
        count = gathered[0].shape[0]
        act = pl.pallas_call(
            functools.partial(hidden_kernel, width),
            in_specs=[VMEM] * 6,
            out_specs=VMEM,
            out_shape=jax.ShapeDtypeStruct((2 * count, hidden), BF16),
            compiler_params=params(),
            cost_estimate=cost(8 * count * width * hidden, 4 * width * hidden),
            name="hidden",
        )(*gathered, weights, inverse)
        keep, send = pl.pallas_call(
            down_kernel,
            in_specs=[VMEM] * 3,
            out_specs=[VMEM] * 2,
            out_shape=[jax.ShapeDtypeStruct((count, half), F32), jax.ShapeDtypeStruct((count, half), BF16)],
            compiler_params=params(),
            cost_estimate=cost(8 * count * half * hidden, 4 * half * hidden),
            name="down",
        )(act, over_sec(act), down_weights)
        return (keep + over_y(send).astype(F32)).astype(BF16)

    returned = [None] * n_exp
    gathered = []
    for g, block in enumerate(arrived):
        if g > 0:
            block = after(block, *gathered[-1][1:3])
        gathered.append(plane_gather(g, block))
    for g in range(len(arrived)):
        result = experts_of(gathered[g])
        for n, k in enumerate(range(g * each, (g + 1) * each)):
            back = result if each == 1 else result[n * cap : (n + 1) * cap]
            returned[k] = back if k == 0 else over_z(back, k)

    return pl.pallas_call(
        combine_kernel,
        out_shape=jax.ShapeDtypeStruct((rows, half), BF16),
        in_specs=[VMEM] * (3 + n_exp),
        out_specs=VMEM,
        compiler_params=params(),
        cost_estimate=cost(4 * n_exp * cap * rows * half, rows * half * 6 + n_exp * cap * half * 2),
        name="combine",
    )(stream, weight_high, weight_low, *returned)


def solution(mesh):
    in_specs = (
        P(("rep", "dev"), None),
        P(("rep", "dev"), "sec"),
        P(("rep", "dev"), "sec"),
        P(("rep", "dev"), "sec"),
        P(),
        P(("rep", "dev"), None),
        P(("rep", "dev"), None),
        P("dev", None, "sec"),
        P("dev", None, "sec"),
        P("dev", "sec", None),
    )
    out_specs = P(("rep", "dev"), "sec")
    return jax.shard_map(body, mesh=mesh, in_specs=in_specs, out_specs=out_specs, check_vma=False)
```

time: 179 us -> 153 us (0.85)
  local copies, waits for them, and re-layouts: 14.5 us -> 4.65 us
  Pallas kernels: 27.3 us -> 21.5 us
  waiting for transfers between devices: 77.9 us -> 72.5 us
  starting transfers between devices: 53.4 us -> 49.1 us
  other arithmetic: 5.12 us -> 3.2 us
    ppermute x14 -> x11, waiting for transfers between devices: 33.7 us -> 8.94 us  [over_sec(): return lax.ppermute(a, 'sec', [(0, 1), (1, 0)])]
    ppermute x16 -> x14, waiting for transfers between devices: 11 us -> 31.6 us  [over_y(): return lax.ppermute(a, 'dev', [(i, i ^ 1) for i in range(n_dev)])]
    pallas_call x10 -> x13, Pallas kernels: 25.2 us -> 19.5 us  [the longest x4 5.7 us: experts_of(): pl.pallas_call(functools.partial(hidden_kernel, width), in_specs=[VMEM] *...]
    unnamed x38 -> x9, local copies, waits for them, and re-layouts: 6.5 us -> 2.6 us
    ppermute x9, starting transfers between devices: 18.7 us -> 15.6 us  [over_z(): lax.ppermute(a, 'dev', [(i, (i // 2 ^ k) * 2 + i % 2) for i in range(n_de...]
    another operation x10 -> x3, other arithmetic: 3.35 us -> 1.34 us
    another operation x6 -> x2, local copies, waits for them, and re-layouts: 2.06 us -> 0.1 us  [the longest x4 1.96 us: plane_gather(): second_x = over_sec(jnp.stack([second, second_y]))]
    dynamic_slice x3 -> x1, local copies, waits for them, and re-layouts: 3.14 us -> 1.18 us  [body(): lax.dynamic_slice_in_dim(w_down[0], ((1 - sec) * 2 + rep) * quarter, quar...]
  transfers between devices with their start and end apart: 39 -> 35, of which waited for: 14 -> 21; matrix products, arithmetic and copies ran while one was open for 7% -> 3% of each run, Pallas kernels for 10% -> 8%
where the time goes in v2:
time: 153 us; the launch traced here: 151 us
  waiting for transfers between devices  72.5 us (47%)
  starting transfers between devices  49.1 us (32%)
  Pallas kernels  21.5 us (14%)
  local copies, waits for them, and re-layouts  4.65 us (3%)
  other arithmetic  3.2 us (2%)
    ppermute x9, waiting for transfers between devices, over_z(): lax.ppermute(a, 'dev', [(i, (i // 2 ^ k) * 2 + i % 2) for i in range(n_de...  31.9 us
    ppermute x14, waiting for transfers between devices, over_y(): return lax.ppermute(a, 'dev', [(i, i ^ 1) for i in range(n_dev)])  31.6 us
    ppermute x11, starting transfers between devices, over_sec(): return lax.ppermute(a, 'sec', [(0, 1), (1, 0)])  17.3 us
    ppermute x14, starting transfers between devices, over_y(): return lax.ppermute(a, 'dev', [(i, i ^ 1) for i in range(n_dev)])  16.2 us
    ppermute x9, starting transfers between devices, over_z(): lax.ppermute(a, 'dev', [(i, (i // 2 ^ k) * 2 + i % 2) for i in range(n_de...  15.6 us
    ppermute x11, waiting for transfers between devices, over_sec(): return lax.ppermute(a, 'sec', [(0, 1), (1, 0)])  8.94 us
    pallas_call x4, Pallas kernels, experts_of(): pl.pallas_call(functools.partial(hidden_kernel, width), in_specs=[VMEM] *...  5.7 us
    pallas_call x1, Pallas kernels, body(): pl.pallas_call(functools.partial(attend_kernel, len(pieces)), in_specs=[V...  4.31 us
  transfers between devices with their start and end apart: 35, of which 21 were waited for; matrix products, arithmetic and copies ran while one was open for 3% of the time, Pallas kernels for 8%

profile of v2, /device:TPU:0, one launch (start us, length us, event | category | flops | bytes accessed | tf_op | source)
XLA Modules:
  0.0 151.2 jit_solution(14299572956202389901)
XLA Ops:
  1.2 3.0 %collective-permute-start.1 = (bf16[384,1024]{1,0:T(8,128)(2,1)S(1)}, bf16[384,1024]{1,0:T(8,128)(2,1)S(1)}, u32[]{:S(2)}, u32[]{:S(2)}) collective-permute-start(bf16[384,1024]{1,0:T(8,128)(2,1)S(1)} %dynamic-slice_bitcast_fusion), channel_id=1, source_target_pairs={{0,16},{16,0},{1,17},{17,1},{2,18},{18,2},{3,19},{19,3},{4,20},{20... | collective-permute-start | bytes 2359304 | tf_op jit(solution)/shard_map/ppermute | solution.py:176
  6.0 1.6 %collective-permute-start = (bf16[128,1024]{1,0:T(8,128)(2,1)S(1)}, bf16[128,1024]{1,0:T(8,128)(2,1)S(1)}, u32[]{:S(2)}, u32[]{:S(2)}) collective-permute-start(bf16[128,1024]{1,0:T(8,128)(2,1)S(1)} %pack.1.refs_0_), channel_id=1, source_target_pairs={{0,4},{2,6},{4,0},{6,2},{8,12},{10,14},{12,8},{14,10},{1,5},{3,7},... | collective-permute-start | bytes 786440 | tf_op jit(solution)/shard_map/ppermute | solution.py:185
  7.7 2.6 %collective-permute-start.4 = (bf16[128,1024]{1,0:T(8,128)(2,1)S(1)}, bf16[128,1024]{1,0:T(8,128)(2,1)S(1)}, u32[]{:S(2)}, u32[]{:S(2)}) collective-permute-start(bf16[128,1024]{1,0:T(8,128)(2,1)S(1)} %pack.1.refs_0_), channel_id=1, source_target_pairs={{0,8},{2,10},{4,12},{6,14},{8,0},{10,2},{12,4},{14,6},{1,9},{3,11}... | collective-permute-start | bytes 786440 | tf_op jit(solution)/shard_map/ppermute | solution.py:185
  10.5 1.5 %collective-permute-start.6 = (bf16[128,1024]{1,0:T(8,128)(2,1)S(1)}, bf16[128,1024]{1,0:T(8,128)(2,1)S(1)}, u32[]{:S(2)}, u32[]{:S(2)}) collective-permute-start(bf16[128,1024]{1,0:T(8,128)(2,1)S(1)} %pack.1.refs_0_), channel_id=1, source_target_pairs={{0,2},{2,0},{4,6},{6,4},{8,10},{10,8},{12,14},{14,12},{1,3},{3,1},... | collective-permute-start | bytes 786440 | tf_op jit(solution)/shard_map/ppermute | solution.py:182
  12.9 5.6 %collective-permute-done.refs_1_ = bf16[128,1024]{1,0:T(8,128)(2,1)S(1)} collective-permute-done((bf16[128,1024]{1,0:T(8,128)(2,1)S(1)}, bf16[128,1024]{1,0:T(8,128)(2,1)S(1)}, u32[]{:S(2)}, u32[]{:S(2)}) %collective-permute-start) | collective-permute-done | bytes 262176 | tf_op jit(solution)/shard_map/ppermute | solution.py:185
  18.6 1.5 %collective-permute-start.2 = (bf16[128,1024]{1,0:T(8,128)(2,1)S(1)}, bf16[128,1024]{1,0:T(8,128)(2,1)S(1)}, u32[]{:S(2)}, u32[]{:S(2)}) collective-permute-start(bf16[128,1024]{1,0:T(8,128)(2,1)S(1)} %collective-permute-done.refs_1_), channel_id=1, source_target_pairs={{0,2},{2,0},{4,6},{6,4},{8,10},{10,8},{12,14},{14,12},{1,3},{3,1},... | collective-permute-start | bytes 786440 | tf_op jit(solution)/shard_map/ppermute | solution.py:182
  21.8 3.4 %collective-permute-done.2.refs_5_ = bf16[128,1024]{1,0:T(8,128)(2,1)S(1)} collective-permute-done((bf16[128,1024]{1,0:T(8,128)(2,1)S(1)}, bf16[128,1024]{1,0:T(8,128)(2,1)S(1)}, u32[]{:S(2)}, u32[]{:S(2)}) %collective-permute-start.2) | collective-permute-done | bytes 262176 | tf_op jit(solution)/shard_map/ppermute | solution.py:182
  27.0 2.1 %collective-permute-done.4.refs_2_ = bf16[128,1024]{1,0:T(8,128)(2,1)S(1)} collective-permute-done((bf16[128,1024]{1,0:T(8,128)(2,1)S(1)}, bf16[128,1024]{1,0:T(8,128)(2,1)S(1)}, u32[]{:S(2)}, u32[]{:S(2)}) %collective-permute-start.4) | collective-permute-done | bytes 262176 | tf_op jit(solution)/shard_map/ppermute | solution.py:185
  29.0 1.5 %collective-permute-start.7 = (bf16[128,1024]{1,0:T(8,128)(2,1)S(1)}, bf16[128,1024]{1,0:T(8,128)(2,1)S(1)}, u32[]{:S(2)}, u32[]{:S(2)}) collective-permute-start(bf16[128,1024]{1,0:T(8,128)(2,1)S(1)} %collective-permute-done.4.refs_2_), channel_id=1, source_target_pairs={{0,2},{2,0},{4,6},{6,4},{8,10},{10,8},{12,14},{14,12},{1,3},{3,1},... | collective-permute-start | bytes 786440 | tf_op jit(solution)/shard_map/ppermute | solution.py:182
  31.3 2.9 %weights.1.weights_ref = bf16[4096,768]{1,0:T(8,128)(2,1)S(1)} custom-call(s32[1]{0:T(128)} %bitcast.6.sec_ref, bf16[4096,384]{1,0:T(8,128)(2,1)} %bitcast.39, bf16[4096,384]{1,0:T(8,128)(2,1)} %bitcast.40), custom_call_target="tpu_custom_call" | custom-call | tf_op jit(solution)/shard_map/weights/pallas_call | solution.py:231
  34.2 1.4 stage.1
  35.7 2.6 %collective-permute-done.7.refs_6_ = bf16[128,1024]{1,0:T(8,128)(2,1)S(1)} collective-permute-done((bf16[128,1024]{1,0:T(8,128)(2,1)S(1)}, bf16[128,1024]{1,0:T(8,128)(2,1)S(1)}, u32[]{:S(2)}, u32[]{:S(2)}) %collective-permute-start.7) | collective-permute-done | bytes 262176 | tf_op jit(solution)/shard_map/ppermute | solution.py:182
  38.3 3.1 %collective-permute-done.8.refs_7_ = bf16[128,1024]{1,0:T(8,128)(2,1)S(1)} collective-permute-done((bf16[128,1024]{1,0:T(8,128)(2,1)S(1)}, bf16[128,1024]{1,0:T(8,128)(2,1)S(1)}, u32[]{:S(2)}, u32[]{:S(2)}) %collective-permute-start.8) | collective-permute-done | bytes 262176 | tf_op jit(solution)/shard_map/ppermute | solution.py:182
  41.4 4.3 %attend.1 = (f32[128,2048]{1,0:T(8,128)}, bf16[80,2048]{1,0:T(8,128)(2,1)S(1)}, bf16[80,2048]{1,0:T(8,128)(2,1)S(1)}, bf16[80,2048]{1,0:T(8,128)(2,1)S(1)}, bf16[80,2048]{1,0:T(8,128)(2,1)S(1)}) custom-call(bf16[128,2048]{1,0:T(8,128)(2,1)S(1)} %get-tuple-element.45.q_ref, bf16[128,2048]{1,0:T(8,128)(2,1)S(1)} %get-tuple-element.46.resid_ref, ...), custom_call_target="tpu_custom_call" | custom-call | flops 1073741824 | bytes 4194304 | tf_op jit(solution)/shard_map/attend/pallas_call | solution.py:248
  45.7 2.4 %down_weights.1.w_ref = bf16[768,2048]{1,0:T(8,128)(2,1)S(1)} custom-call(s32[2]{0:T(128)S(1)} %pad_add_fusion.index_ref, bf16[384,4096]{1,0:T(8,128)(2,1)} %bitcast.38, bf16[384,1024]{1,0:T(8,128)(2,1)} %copy-done.3, bf16[384,1024]{1,0:T(8,128)(2,1)} %collective-permute-done.3.far_ref), custom_call_target="tpu_custom_call" | custom-call | tf_op jit(solution)/shard_map/down_weights/pallas_call | solution.py:259
  48.1 1.6 %collective-permute-start.9 = (bf16[80,2048]{1,0:T(8,128)(2,1)S(1)}, bf16[80,2048]{1,0:T(8,128)(2,1)S(1)}, u32[]{:S(2)}, u32[]{:S(2)}) collective-permute-start(bf16[80,2048]{1,0:T(8,128)(2,1)S(1)} %get-tuple-element.57.own_ref), channel_id=1, source_target_pairs={{0,2},{2,0},{4,6},{6,4},{8,10},{10,8},{12,14},{14,12},{1,3},{3,1},... | collective-permute-start | bytes 983048 | tf_op jit(solution)/shard_map/ppermute | solution.py:182
  50.2 4.0 %collective-permute-start.21 = (bf16[80,2048]{1,0:T(8,128)(2,1)S(1)}, bf16[80,2048]{1,0:T(8,128)(2,1)S(1)}, u32[]{:S(2)}, u32[]{:S(2)}) collective-permute-start(bf16[80,2048]{1,0:T(8,128)(2,1)S(1)} %get-tuple-element.67), channel_id=1, source_target_pairs={{0,8},{2,10},{4,12},{6,14},{8,0},{10,2},{12,4},{14,6},{1,9},{3,11}... | collective-permute-start | bytes 983048 | tf_op jit(solution)/shard_map/ppermute | solution.py:185
  55.4 1.4 collective-permute-done.10.x_ref
  56.8 6.9 %collective-permute-done.14.own_ref = bf16[80,2048]{1,0:T(8,128)(2,1)S(1)} collective-permute-done((bf16[80,2048]{1,0:T(8,128)(2,1)S(1)}, bf16[80,2048]{1,0:T(8,128)(2,1)S(1)}, u32[]{:S(2)}, u32[]{:S(2)}) %collective-permute-start.14) | collective-permute-done | bytes 327712 | tf_op jit(solution)/shard_map/ppermute | solution.py:185
  65.7 1.5 %collective-permute-start.28 = (bf16[80,2048]{1,0:T(8,128)(2,1)S(1)}, bf16[80,2048]{1,0:T(8,128)(2,1)S(1)}, u32[]{:S(2)}, u32[]{:S(2)}) collective-permute-start(bf16[80,2048]{1,0:T(8,128)(2,1)S(1)} %get-tuple-element.71), channel_id=1, source_target_pairs={{0,12},{2,14},{4,8},{6,10},{8,4},{10,6},{12,0},{14,2},{1,13},{3,15... | collective-permute-start | bytes 983048 | tf_op jit(solution)/shard_map/ppermute | solution.py:185
  67.2 3.4 %collective-permute-done.21.own_ref = bf16[80,2048]{1,0:T(8,128)(2,1)S(1)} collective-permute-done((bf16[80,2048]{1,0:T(8,128)(2,1)S(1)}, bf16[80,2048]{1,0:T(8,128)(2,1)S(1)}, u32[]{:S(2)}, u32[]{:S(2)}) %collective-permute-start.21) | collective-permute-done | bytes 327712 | tf_op jit(solution)/shard_map/ppermute | solution.py:185
  70.5 1.4 collective-permute-done.15.y_ref
  72.0 1.9 %collective-permute-done.16.x_ref = bf16[80,2048]{1,0:T(8,128)(2,1)S(1)} collective-permute-done((bf16[80,2048]{1,0:T(8,128)(2,1)S(1)}, bf16[80,2048]{1,0:T(8,128)(2,1)S(1)}, u32[]{:S(2)}, u32[]{:S(2)}) %collective-permute-start.16) | collective-permute-done | bytes 327712 | tf_op jit(solution)/shard_map/ppermute | solution.py:176
  74.6 2.5 %collective-permute-start.23 = (bf16[80,2048]{1,0:T(8,128)(2,1)S(1)}, bf16[80,2048]{1,0:T(8,128)(2,1)S(1)}, u32[]{:S(2)}, u32[]{:S(2)}) collective-permute-start(bf16[80,2048]{1,0:T(8,128)(2,1)S(1)} %collective-permute-done.21.own_ref), channel_id=1, source_target_pairs={{0,16},{16,0},{1,17},{17,1},{2,18},{18,2},{3,19},{19,3},{4,20},{20... | collective-permute-start | bytes 983048 | tf_op jit(solution)/shard_map/ppermute | solution.py:176
  77.2 7.1 %collective-permute-done.22.y_ref = bf16[80,2048]{1,0:T(8,128)(2,1)S(1)} collective-permute-done((bf16[80,2048]{1,0:T(8,128)(2,1)S(1)}, bf16[80,2048]{1,0:T(8,128)(2,1)S(1)}, u32[]{:S(2)}, u32[]{:S(2)}) %collective-permute-start.22) | collective-permute-done | bytes 327712 | tf_op jit(solution)/shard_map/ppermute | solution.py:182
  84.7 1.6 %collective-permute-start.11 = (bf16[80,2048]{1,0:T(8,128)(2,1)S(1)}, bf16[80,2048]{1,0:T(8,128)(2,1)S(1)}, u32[]{:S(2)}, u32[]{:S(2)}) collective-permute-start(bf16[80,2048]{1,0:T(8,128)(2,1)S(1)} %collective-permute-done.10.x_ref), channel_id=1, source_target_pairs={{0,2},{2,0},{4,6},{6,4},{8,10},{10,8},{12,14},{14,12},{1,3},{3,1},... | collective-permute-start | bytes 983048 | tf_op jit(solution)/shard_map/ppermute | solution.py:182
  86.7 2.2 %collective-permute-done.17.both_ref = bf16[80,2048]{1,0:T(8,128)(2,1)S(1)} collective-permute-done((bf16[80,2048]{1,0:T(8,128)(2,1)S(1)}, bf16[80,2048]{1,0:T(8,128)(2,1)S(1)}, u32[]{:S(2)}, u32[]{:S(2)}) %collective-permute-start.17) | collective-permute-done | bytes 327712 | tf_op jit(solution)/shard_map/ppermute | solution.py:176
  88.9 1.4 hidden.5.own_act
  90.3 2.6 %collective-permute-start.18 = (bf16[160,384]{1,0:T(8,128)(2,1)S(1)}, bf16[160,384]{1,0:T(8,128)(2,1)S(1)}, u32[]{:S(2)}, u32[]{:S(2)}) collective-permute-start(bf16[160,384]{1,0:T(8,128)(2,1)S(1)} %hidden.5.own_act), channel_id=1, source_target_pairs={{0,16},{16,0},{1,17},{17,1},{2,18},{18,2},{3,19},{19,3},{4,20},{20... | collective-permute-start | bytes 368648 | tf_op jit(solution)/shard_map/ppermute | solution.py:176
  92.9 2.0 %collective-permute-done.29.y_ref = bf16[80,2048]{1,0:T(8,128)(2,1)S(1)} collective-permute-done((bf16[80,2048]{1,0:T(8,128)(2,1)S(1)}, bf16[80,2048]{1,0:T(8,128)(2,1)S(1)}, u32[]{:S(2)}, u32[]{:S(2)}) %collective-permute-start.29) | collective-permute-done | bytes 327712 | tf_op jit(solution)/shard_map/ppermute | solution.py:182
  94.9 1.8 %collective-permute-start.31 = (bf16[80,2048]{1,0:T(8,128)(2,1)S(1)}, bf16[80,2048]{1,0:T(8,128)(2,1)S(1)}, u32[]{:S(2)}, u32[]{:S(2)}) collective-permute-start(bf16[80,2048]{1,0:T(8,128)(2,1)S(1)} %collective-permute-done.29.y_ref), channel_id=1, source_target_pairs={{0,16},{16,0},{1,17},{17,1},{2,18},{18,2},{3,19},{19,3},{4,20},{20... | collective-permute-start | bytes 983048 | tf_op jit(solution)/shard_map/ppermute | solution.py:176
  96.7 5.2 %collective-permute-done.11.both_ref = bf16[80,2048]{1,0:T(8,128)(2,1)S(1)} collective-permute-done((bf16[80,2048]{1,0:T(8,128)(2,1)S(1)}, bf16[80,2048]{1,0:T(8,128)(2,1)S(1)}, u32[]{:S(2)}, u32[]{:S(2)}) %collective-permute-start.11) | collective-permute-done | bytes 327712 | tf_op jit(solution)/shard_map/ppermute | solution.py:182
  101.9 1.4 hidden.4.own_act
  103.4 1.9 %collective-permute-start.12 = (bf16[160,384]{1,0:T(8,128)(2,1)S(1)}, bf16[160,384]{1,0:T(8,128)(2,1)S(1)}, u32[]{:S(2)}, u32[]{:S(2)}) collective-permute-start(bf16[160,384]{1,0:T(8,128)(2,1)S(1)} %hidden.4.own_act), channel_id=1, source_target_pairs={{0,16},{16,0},{1,17},{17,1},{2,18},{18,2},{3,19},{19,3},{4,20},{20... | collective-permute-start | bytes 368648 | tf_op jit(solution)/shard_map/ppermute | solution.py:176
  105.9 1.6 %collective-permute-start.19 = (bf16[80,2048]{1,0:T(8,128)(2,1)S(1)}, bf16[80,2048]{1,0:T(8,128)(2,1)S(1)}, u32[]{:S(2)}, u32[]{:S(2)}) collective-permute-start(bf16[80,2048]{1,0:T(8,128)(2,1)S(1)} %get-tuple-element.66), channel_id=1, source_target_pairs={{0,2},{2,0},{4,6},{6,4},{8,10},{10,8},{12,14},{14,12},{1,3},{3,1},... | collective-permute-start | bytes 983048 | tf_op jit(solution)/shard_map/ppermute | solution.py:182
  107.6 1.4 collective-permute-done.24.both_ref
  109.0 1.4 hidden.6.own_act
  110.4 1.9 %collective-permute-start.25 = (bf16[160,384]{1,0:T(8,128)(2,1)S(1)}, bf16[160,384]{1,0:T(8,128)(2,1)S(1)}, u32[]{:S(2)}, u32[]{:S(2)}) collective-permute-start(bf16[160,384]{1,0:T(8,128)(2,1)S(1)} %hidden.6.own_act), channel_id=1, source_target_pairs={{0,16},{16,0},{1,17},{17,1},{2,18},{18,2},{3,19},{19,3},{4,20},{20... | collective-permute-start | bytes 368648 | tf_op jit(solution)/shard_map/ppermute | solution.py:176
  113.0 1.6 %collective-permute-start.13 = (bf16[80,2048]{1,0:T(8,128)(2,1)S(1)}, bf16[80,2048]{1,0:T(8,128)(2,1)S(1)}, u32[]{:S(2)}, u32[]{:S(2)}) collective-permute-start(bf16[80,2048]{1,0:T(8,128)(2,1)S(1)} %get-tuple-element.62), channel_id=1, source_target_pairs={{0,2},{2,0},{4,6},{6,4},{8,10},{10,8},{12,14},{14,12},{1,3},{3,1},... | collective-permute-start | bytes 983048 | tf_op jit(solution)/shard_map/ppermute | solution.py:182
  116.0 1.4 collective-permute-start.26
  117.5 1.4 hidden.7.own_act
  118.9 2.1 %collective-permute-start.32 = (bf16[160,384]{1,0:T(8,128)(2,1)S(1)}, bf16[160,384]{1,0:T(8,128)(2,1)S(1)}, u32[]{:S(2)}, u32[]{:S(2)}) collective-permute-start(bf16[160,384]{1,0:T(8,128)(2,1)S(1)} %hidden.7.own_act), channel_id=1, source_target_pairs={{0,16},{16,0},{1,17},{17,1},{2,18},{18,2},{3,19},{19,3},{4,20},{20... | collective-permute-start | bytes 368648 | tf_op jit(solution)/shard_map/ppermute | solution.py:176
  121.1 2.7 %collective-permute-done.32.other_act = bf16[160,384]{1,0:T(8,128)(2,1)S(1)} collective-permute-done((bf16[160,384]{1,0:T(8,128)(2,1)S(1)}, bf16[160,384]{1,0:T(8,128)(2,1)S(1)}, u32[]{:S(2)}, u32[]{:S(2)}) %collective-permute-start.32) | collective-permute-done | bytes 122912 | tf_op jit(solution)/shard_map/ppermute | solution.py:176
  126.6 2.1 %collective-permute-start.27 = (bf16[80,2048]{1,0:T(8,128)(2,1)S(1)}, bf16[80,2048]{1,0:T(8,128)(2,1)S(1)}, u32[]{:S(2)}, u32[]{:S(2)}) collective-permute-start(bf16[80,2048]{1,0:T(8,128)(2,1)S(1)} %add_convert_fusion.1), channel_id=1, source_target_pairs={{0,8},{2,10},{4,12},{6,14},{8,0},{10,2},{12,4},{14,6},{1,9},{3,11}... | collective-permute-start | bytes 983048 | tf_op jit(solution)/shard_map/ppermute | solution.py:185
  128.8 2.9 %collective-permute-done.33 = bf16[80,2048]{1,0:T(8,128)(2,1)S(1)} collective-permute-done((bf16[80,2048]{1,0:T(8,128)(2,1)S(1)}, bf16[80,2048]{1,0:T(8,128)(2,1)S(1)}, u32[]{:S(2)}, u32[]{:S(2)}) %collective-permute-start.33) | collective-permute-done | bytes 327712 | tf_op jit(solution)/shard_map/ppermute | solution.py:182
  131.7 3.4 %collective-permute-start.34 = (bf16[80,2048]{1,0:T(8,128)(2,1)S(1)}, bf16[80,2048]{1,0:T(8,128)(2,1)S(1)}, u32[]{:S(2)}, u32[]{:S(2)}) collective-permute-start(bf16[80,2048]{1,0:T(8,128)(2,1)S(1)} %add_convert_fusion), channel_id=1, source_target_pairs={{0,12},{2,14},{4,8},{6,10},{8,4},{10,6},{12,0},{14,2},{1,13},{3,15... | collective-permute-start | bytes 983048 | tf_op jit(solution)/shard_map/ppermute | solution.py:185
  135.2 13.9 %collective-permute-done.27.refs_2_ = bf16[80,2048]{1,0:T(8,128)(2,1)S(1)} collective-permute-done((bf16[80,2048]{1,0:T(8,128)(2,1)S(1)}, bf16[80,2048]{1,0:T(8,128)(2,1)S(1)}, u32[]{:S(2)}, u32[]{:S(2)}) %collective-permute-start.27) | collective-permute-done | bytes 327712 | tf_op jit(solution)/shard_map/ppermute | solution.py:185
  149.1 2.0 %combine.1 = bf16[128,2048]{1,0:T(8,128)(2,1)} custom-call(f32[128,2048]{1,0:T(8,128)S(1)} %copy-done, bf16[4,128,80]{2,1,0:T(8,128)(2,1)S(1)} %get-tuple-element.51.high_ref, bf16[4,128,80]{2,1,0:T(8,128)(2,1)S(1)} %get-tuple-element.52.low_ref, bf16[80,2048]{1,0:T(8,128)(2,1)S(1)} %add_convert_fusion.3.refs_0_, ...), custom_call_target="tpu_custom_call" | custom-call | flops 335544320 | bytes 2883584 | tf_op jit(solution)/shard_map/combine/pallas_call | solution.py:314
  (68 shorter events, 19.6 us)
Async XLA Ops:
  1.2 24.1 %collective-permute-start.1 = (bf16[384,1024]{1,0:T(8,128)(2,1)S(1)}, bf16[384,1024]{1,0:T(8,128)(2,1)S(1)}, u32[]{:S(2)}, u32[]{:S(2)}) collective-permute-start(bf16[384,1024]{1,0:T(8,128)(2,1)S(1)} %dynamic-slice_bitcast_fusion), channel_id=1, source_target_pairs={{0,16},{16,0},{1,17},{17,1},{2,18},{18,2},{3,19},{19,3},{4,20},{20... | collective-permute-start | bytes 2359304 | tf_op jit(solution)/shard_map/ppermute | solution.py:176
  4.2 0.9 copy-start.1
  5.1 0.9 copy-start.2
  6.0 12.5 %collective-permute-start = (bf16[128,1024]{1,0:T(8,128)(2,1)S(1)}, bf16[128,1024]{1,0:T(8,128)(2,1)S(1)}, u32[]{:S(2)}, u32[]{:S(2)}) collective-permute-start(bf16[128,1024]{1,0:T(8,128)(2,1)S(1)} %pack.1.refs_0_), channel_id=1, source_target_pairs={{0,4},{2,6},{4,0},{6,2},{8,12},{10,14},{12,8},{14,10},{1,5},{3,7},... | collective-permute-start | bytes 786440 | tf_op jit(solution)/shard_map/ppermute | solution.py:185
  7.7 21.4 %collective-permute-start.4 = (bf16[128,1024]{1,0:T(8,128)(2,1)S(1)}, bf16[128,1024]{1,0:T(8,128)(2,1)S(1)}, u32[]{:S(2)}, u32[]{:S(2)}) collective-permute-start(bf16[128,1024]{1,0:T(8,128)(2,1)S(1)} %pack.1.refs_0_), channel_id=1, source_target_pairs={{0,8},{2,10},{4,12},{6,14},{8,0},{10,2},{12,4},{14,6},{1,9},{3,11}... | collective-permute-start | bytes 786440 | tf_op jit(solution)/shard_map/ppermute | solution.py:185
  10.3 20.3 %collective-permute-start.5 = (bf16[128,1024]{1,0:T(8,128)(2,1)S(1)}, bf16[128,1024]{1,0:T(8,128)(2,1)S(1)}, u32[]{:S(2)}, u32[]{:S(2)}) collective-permute-start(bf16[128,1024]{1,0:T(8,128)(2,1)S(1)} %pack.1.refs_0_), channel_id=1, source_target_pairs={{0,12},{2,14},{4,8},{6,10},{8,4},{10,6},{12,0},{14,2},{1,13},{3,15... | collective-permute-start | bytes 786440 | tf_op jit(solution)/shard_map/ppermute | solution.py:185
  10.5 25.2 %collective-permute-start.6 = (bf16[128,1024]{1,0:T(8,128)(2,1)S(1)}, bf16[128,1024]{1,0:T(8,128)(2,1)S(1)}, u32[]{:S(2)}, u32[]{:S(2)}) collective-permute-start(bf16[128,1024]{1,0:T(8,128)(2,1)S(1)} %pack.1.refs_0_), channel_id=1, source_target_pairs={{0,2},{2,0},{4,6},{6,4},{8,10},{10,8},{12,14},{14,12},{1,3},{3,1},... | collective-permute-start | bytes 786440 | tf_op jit(solution)/shard_map/ppermute | solution.py:182
  18.6 6.7 %collective-permute-start.2 = (bf16[128,1024]{1,0:T(8,128)(2,1)S(1)}, bf16[128,1024]{1,0:T(8,128)(2,1)S(1)}, u32[]{:S(2)}, u32[]{:S(2)}) collective-permute-start(bf16[128,1024]{1,0:T(8,128)(2,1)S(1)} %collective-permute-done.refs_1_), channel_id=1, source_target_pairs={{0,2},{2,0},{4,6},{6,4},{8,10},{10,8},{12,14},{14,12},{1,3},{3,1},... | collective-permute-start | bytes 786440 | tf_op jit(solution)/shard_map/ppermute | solution.py:182
  25.3 8.9 %copy-start.3 = (bf16[384,1024]{1,0:T(8,128)(2,1)}, bf16[384,1024]{1,0:T(8,128)(2,1)S(1)}, u32[]{:S(2)}) copy-start(bf16[384,1024]{1,0:T(8,128)(2,1)S(1)} %collective-permute-done.1.near_ref) | copy-start | bytes 2359300
  25.3 10.4 %collective-permute-start.3 = (bf16[384,1024]{1,0:T(8,128)(2,1)S(1)}, bf16[384,1024]{1,0:T(8,128)(2,1)}, u32[]{:S(2)}, u32[]{:S(2)}) collective-permute-start(bf16[384,1024]{1,0:T(8,128)(2,1)S(1)} %collective-permute-done.1.near_ref), channel_id=1, source_target_pairs={{0,1},{1,0},{2,3},{3,2},{4,5},{5,4},{6,7},{7,6},{8,9},{9,8},{10,11... | collective-permute-start | bytes 2359304 | tf_op jit(solution)/shard_map/ppermute | solution.py:179
  29.0 9.2 %collective-permute-start.7 = (bf16[128,1024]{1,0:T(8,128)(2,1)S(1)}, bf16[128,1024]{1,0:T(8,128)(2,1)S(1)}, u32[]{:S(2)}, u32[]{:S(2)}) collective-permute-start(bf16[128,1024]{1,0:T(8,128)(2,1)S(1)} %collective-permute-done.4.refs_2_), channel_id=1, source_target_pairs={{0,2},{2,0},{4,6},{6,4},{8,10},{10,8},{12,14},{14,12},{1,3},{3,1},... | collective-permute-start | bytes 786440 | tf_op jit(solution)/shard_map/ppermute | solution.py:182
  30.6 10.8 %collective-permute-start.8 = (bf16[128,1024]{1,0:T(8,128)(2,1)S(1)}, bf16[128,1024]{1,0:T(8,128)(2,1)S(1)}, u32[]{:S(2)}, u32[]{:S(2)}) collective-permute-start(bf16[128,1024]{1,0:T(8,128)(2,1)S(1)} %collective-permute-done.5.refs_3_), channel_id=1, source_target_pairs={{0,2},{2,0},{4,6},{6,4},{8,10},{10,8},{12,14},{14,12},{1,3},{3,1},... | collective-permute-start | bytes 786440 | tf_op jit(solution)/shard_map/ppermute | solution.py:182
  48.1 7.3 %collective-permute-start.9 = (bf16[80,2048]{1,0:T(8,128)(2,1)S(1)}, bf16[80,2048]{1,0:T(8,128)(2,1)S(1)}, u32[]{:S(2)}, u32[]{:S(2)}) collective-permute-start(bf16[80,2048]{1,0:T(8,128)(2,1)S(1)} %get-tuple-element.57.own_ref), channel_id=1, source_target_pairs={{0,2},{2,0},{4,6},{6,4},{8,10},{10,8},{12,14},{14,12},{1,3},{3,1},... | collective-permute-start | bytes 983048 | tf_op jit(solution)/shard_map/ppermute | solution.py:182
  49.7 7.1 %collective-permute-start.10 = (bf16[80,2048]{1,0:T(8,128)(2,1)S(1)}, bf16[80,2048]{1,0:T(8,128)(2,1)S(1)}, u32[]{:S(2)}, u32[]{:S(2)}) collective-permute-start(bf16[80,2048]{1,0:T(8,128)(2,1)S(1)} %get-tuple-element.57.own_ref), channel_id=1, source_target_pairs={{0,16},{16,0},{1,17},{17,1},{2,18},{18,2},{3,19},{19,3},{4,20},{20... | collective-permute-start | bytes 983048 | tf_op jit(solution)/shard_map/ppermute | solution.py:176
  50.2 13.4 %collective-permute-start.14 = (bf16[80,2048]{1,0:T(8,128)(2,1)S(1)}, bf16[80,2048]{1,0:T(8,128)(2,1)S(1)}, u32[]{:S(2)}, u32[]{:S(2)}) collective-permute-start(bf16[80,2048]{1,0:T(8,128)(2,1)S(1)} %get-tuple-element.63), channel_id=1, source_target_pairs={{0,4},{2,6},{4,0},{6,2},{8,12},{10,14},{12,8},{14,10},{1,5},{3,7},... | collective-permute-start | bytes 983048 | tf_op jit(solution)/shard_map/ppermute | solution.py:185
  50.2 20.3 %collective-permute-start.21 = (bf16[80,2048]{1,0:T(8,128)(2,1)S(1)}, bf16[80,2048]{1,0:T(8,128)(2,1)S(1)}, u32[]{:S(2)}, u32[]{:S(2)}) collective-permute-start(bf16[80,2048]{1,0:T(8,128)(2,1)S(1)} %get-tuple-element.67), channel_id=1, source_target_pairs={{0,8},{2,10},{4,12},{6,14},{8,0},{10,2},{12,4},{14,6},{1,9},{3,11}... | collective-permute-start | bytes 983048 | tf_op jit(solution)/shard_map/ppermute | solution.py:185
  63.7 8.3 %collective-permute-start.15 = (bf16[80,2048]{1,0:T(8,128)(2,1)S(1)}, bf16[80,2048]{1,0:T(8,128)(2,1)S(1)}, u32[]{:S(2)}, u32[]{:S(2)}) collective-permute-start(bf16[80,2048]{1,0:T(8,128)(2,1)S(1)} %collective-permute-done.14.own_ref), channel_id=1, source_target_pairs={{0,2},{2,0},{4,6},{6,4},{8,10},{10,8},{12,14},{14,12},{1,3},{3,1},... | collective-permute-start | bytes 983048 | tf_op jit(solution)/shard_map/ppermute | solution.py:182
  64.6 9.3 %collective-permute-start.16 = (bf16[80,2048]{1,0:T(8,128)(2,1)S(1)}, bf16[80,2048]{1,0:T(8,128)(2,1)S(1)}, u32[]{:S(2)}, u32[]{:S(2)}) collective-permute-start(bf16[80,2048]{1,0:T(8,128)(2,1)S(1)} %collective-permute-done.14.own_ref), channel_id=1, source_target_pairs={{0,16},{16,0},{1,17},{17,1},{2,18},{18,2},{3,19},{19,3},{4,20},{20... | collective-permute-start | bytes 983048 | tf_op jit(solution)/shard_map/ppermute | solution.py:176
  65.7 11.5 %collective-permute-start.28 = (bf16[80,2048]{1,0:T(8,128)(2,1)S(1)}, bf16[80,2048]{1,0:T(8,128)(2,1)S(1)}, u32[]{:S(2)}, u32[]{:S(2)}) collective-permute-start(bf16[80,2048]{1,0:T(8,128)(2,1)S(1)} %get-tuple-element.71), channel_id=1, source_target_pairs={{0,12},{2,14},{4,8},{6,10},{8,4},{10,6},{12,0},{14,2},{1,13},{3,15... | collective-permute-start | bytes 983048 | tf_op jit(solution)/shard_map/ppermute | solution.py:185
  73.9 10.4 %collective-permute-start.22 = (bf16[80,2048]{1,0:T(8,128)(2,1)S(1)}, bf16[80,2048]{1,0:T(8,128)(2,1)S(1)}, u32[]{:S(2)}, u32[]{:S(2)}) collective-permute-start(bf16[80,2048]{1,0:T(8,128)(2,1)S(1)} %collective-permute-done.21.own_ref), channel_id=1, source_target_pairs={{0,2},{2,0},{4,6},{6,4},{8,10},{10,8},{12,14},{14,12},{1,3},{3,1},... | collective-permute-start | bytes 983048 | tf_op jit(solution)/shard_map/ppermute | solution.py:182
  74.6 9.6 %collective-permute-start.23 = (bf16[80,2048]{1,0:T(8,128)(2,1)S(1)}, bf16[80,2048]{1,0:T(8,128)(2,1)S(1)}, u32[]{:S(2)}, u32[]{:S(2)}) collective-permute-start(bf16[80,2048]{1,0:T(8,128)(2,1)S(1)} %collective-permute-done.21.own_ref), channel_id=1, source_target_pairs={{0,16},{16,0},{1,17},{17,1},{2,18},{18,2},{3,19},{19,3},{4,20},{20... | collective-permute-start | bytes 983048 | tf_op jit(solution)/shard_map/ppermute | solution.py:176
  77.1 11.8 %collective-permute-start.17 = (bf16[80,2048]{1,0:T(8,128)(2,1)S(1)}, bf16[80,2048]{1,0:T(8,128)(2,1)S(1)}, u32[]{:S(2)}, u32[]{:S(2)}) collective-permute-start(bf16[80,2048]{1,0:T(8,128)(2,1)S(1)} %collective-permute-done.15.y_ref), channel_id=1, source_target_pairs={{0,16},{16,0},{1,17},{17,1},{2,18},{18,2},{3,19},{19,3},{4,20},{20... | collective-permute-start | bytes 983048 | tf_op jit(solution)/shard_map/ppermute | solution.py:176
  84.3 10.7 %collective-permute-start.29 = (bf16[80,2048]{1,0:T(8,128)(2,1)S(1)}, bf16[80,2048]{1,0:T(8,128)(2,1)S(1)}, u32[]{:S(2)}, u32[]{:S(2)}) collective-permute-start(bf16[80,2048]{1,0:T(8,128)(2,1)S(1)} %collective-permute-done.28.own_ref), channel_id=1, source_target_pairs={{0,2},{2,0},{4,6},{6,4},{8,10},{10,8},{12,14},{14,12},{1,3},{3,1},... | collective-permute-start | bytes 983048 | tf_op jit(solution)/shard_map/ppermute | solution.py:182
  84.7 17.3 %collective-permute-start.11 = (bf16[80,2048]{1,0:T(8,128)(2,1)S(1)}, bf16[80,2048]{1,0:T(8,128)(2,1)S(1)}, u32[]{:S(2)}, u32[]{:S(2)}) collective-permute-start(bf16[80,2048]{1,0:T(8,128)(2,1)S(1)} %collective-permute-done.10.x_ref), channel_id=1, source_target_pairs={{0,2},{2,0},{4,6},{6,4},{8,10},{10,8},{12,14},{14,12},{1,3},{3,1},... | collective-permute-start | bytes 983048 | tf_op jit(solution)/shard_map/ppermute | solution.py:182
  86.3 22.7 %collective-permute-start.24 = (bf16[80,2048]{1,0:T(8,128)(2,1)S(1)}, bf16[80,2048]{1,0:T(8,128)(2,1)S(1)}, u32[]{:S(2)}, u32[]{:S(2)}) collective-permute-start(bf16[80,2048]{1,0:T(8,128)(2,1)S(1)} %collective-permute-done.23.x_ref), channel_id=1, source_target_pairs={{0,2},{2,0},{4,6},{6,4},{8,10},{10,8},{12,14},{14,12},{1,3},{3,1},... | collective-permute-start | bytes 983048 | tf_op jit(solution)/shard_map/ppermute | solution.py:182
  90.3 14.9 %collective-permute-start.18 = (bf16[160,384]{1,0:T(8,128)(2,1)S(1)}, bf16[160,384]{1,0:T(8,128)(2,1)S(1)}, u32[]{:S(2)}, u32[]{:S(2)}) collective-permute-start(bf16[160,384]{1,0:T(8,128)(2,1)S(1)} %hidden.5.own_act), channel_id=1, source_target_pairs={{0,16},{16,0},{1,17},{17,1},{2,18},{18,2},{3,19},{19,3},{4,20},{20... | collective-permute-start | bytes 368648 | tf_op jit(solution)/shard_map/ppermute | solution.py:176
  92.9 24.6 %collective-permute-start.30 = (bf16[80,2048]{1,0:T(8,128)(2,1)S(1)}, bf16[80,2048]{1,0:T(8,128)(2,1)S(1)}, u32[]{:S(2)}, u32[]{:S(2)}) collective-permute-start(bf16[80,2048]{1,0:T(8,128)(2,1)S(1)} %collective-permute-done.28.own_ref), channel_id=1, source_target_pairs={{0,16},{16,0},{1,17},{17,1},{2,18},{18,2},{3,19},{19,3},{4,20},{20... | collective-permute-start | bytes 983048 | tf_op jit(solution)/shard_map/ppermute | solution.py:176
  94.9 22.5 %collective-permute-start.31 = (bf16[80,2048]{1,0:T(8,128)(2,1)S(1)}, bf16[80,2048]{1,0:T(8,128)(2,1)S(1)}, u32[]{:S(2)}, u32[]{:S(2)}) collective-permute-start(bf16[80,2048]{1,0:T(8,128)(2,1)S(1)} %collective-permute-done.29.y_ref), channel_id=1, source_target_pairs={{0,16},{16,0},{1,17},{17,1},{2,18},{18,2},{3,19},{19,3},{4,20},{20... | collective-permute-start | bytes 983048 | tf_op jit(solution)/shard_map/ppermute | solution.py:176
  103.4 8.9 %collective-permute-start.12 = (bf16[160,384]{1,0:T(8,128)(2,1)S(1)}, bf16[160,384]{1,0:T(8,128)(2,1)S(1)}, u32[]{:S(2)}, u32[]{:S(2)}) collective-permute-start(bf16[160,384]{1,0:T(8,128)(2,1)S(1)} %hidden.4.own_act), channel_id=1, source_target_pairs={{0,16},{16,0},{1,17},{17,1},{2,18},{18,2},{3,19},{19,3},{4,20},{20... | collective-permute-start | bytes 368648 | tf_op jit(solution)/shard_map/ppermute | solution.py:176
  105.9 15.1 %collective-permute-start.19 = (bf16[80,2048]{1,0:T(8,128)(2,1)S(1)}, bf16[80,2048]{1,0:T(8,128)(2,1)S(1)}, u32[]{:S(2)}, u32[]{:S(2)}) collective-permute-start(bf16[80,2048]{1,0:T(8,128)(2,1)S(1)} %get-tuple-element.66), channel_id=1, source_target_pairs={{0,2},{2,0},{4,6},{6,4},{8,10},{10,8},{12,14},{14,12},{1,3},{3,1},... | collective-permute-start | bytes 983048 | tf_op jit(solution)/shard_map/ppermute | solution.py:182
  110.4 4.9 %collective-permute-start.25 = (bf16[160,384]{1,0:T(8,128)(2,1)S(1)}, bf16[160,384]{1,0:T(8,128)(2,1)S(1)}, u32[]{:S(2)}, u32[]{:S(2)}) collective-permute-start(bf16[160,384]{1,0:T(8,128)(2,1)S(1)} %hidden.6.own_act), channel_id=1, source_target_pairs={{0,16},{16,0},{1,17},{17,1},{2,18},{18,2},{3,19},{19,3},{4,20},{20... | collective-permute-start | bytes 368648 | tf_op jit(solution)/shard_map/ppermute | solution.py:176
  113.0 22.2 %collective-permute-start.13 = (bf16[80,2048]{1,0:T(8,128)(2,1)S(1)}, bf16[80,2048]{1,0:T(8,128)(2,1)S(1)}, u32[]{:S(2)}, u32[]{:S(2)}) collective-permute-start(bf16[80,2048]{1,0:T(8,128)(2,1)S(1)} %get-tuple-element.62), channel_id=1, source_target_pairs={{0,2},{2,0},{4,6},{6,4},{8,10},{10,8},{12,14},{14,12},{1,3},{3,1},... | collective-permute-start | bytes 983048 | tf_op jit(solution)/shard_map/ppermute | solution.py:182
  116.0 10.5 %collective-permute-start.26 = (bf16[80,2048]{1,0:T(8,128)(2,1)S(1)}, bf16[80,2048]{1,0:T(8,128)(2,1)S(1)}, u32[]{:S(2)}, u32[]{:S(2)}) collective-permute-start(bf16[80,2048]{1,0:T(8,128)(2,1)S(1)} %get-tuple-element.70), channel_id=1, source_target_pairs={{0,2},{2,0},{4,6},{6,4},{8,10},{10,8},{12,14},{14,12},{1,3},{3,1},... | collective-permute-start | bytes 983048 | tf_op jit(solution)/shard_map/ppermute | solution.py:182
  118.9 4.9 %collective-permute-start.32 = (bf16[160,384]{1,0:T(8,128)(2,1)S(1)}, bf16[160,384]{1,0:T(8,128)(2,1)S(1)}, u32[]{:S(2)}, u32[]{:S(2)}) collective-permute-start(bf16[160,384]{1,0:T(8,128)(2,1)S(1)} %hidden.7.own_act), channel_id=1, source_target_pairs={{0,16},{16,0},{1,17},{17,1},{2,18},{18,2},{3,19},{19,3},{4,20},{20... | collective-permute-start | bytes 368648 | tf_op jit(solution)/shard_map/ppermute | solution.py:176
  121.0 28.1 %copy-start = (f32[128,2048]{1,0:T(8,128)S(1)}, f32[128,2048]{1,0:T(8,128)}, u32[]{:S(2)}) copy-start(f32[128,2048]{1,0:T(8,128)} %get-tuple-element.50.stream_ref) | copy-start | bytes 3145732
  121.1 14.1 %collective-permute-start.20 = (bf16[80,2048]{1,0:T(8,128)(2,1)S(1)}, bf16[80,2048]{1,0:T(8,128)(2,1)S(1)}, u32[]{:S(2)}, u32[]{:S(2)}) collective-permute-start(bf16[80,2048]{1,0:T(8,128)(2,1)S(1)} %add_convert_fusion.2), channel_id=1, source_target_pairs={{0,4},{2,6},{4,0},{6,2},{8,12},{10,14},{12,8},{14,10},{1,5},{3,7},... | collective-permute-start | bytes 983048 | tf_op jit(solution)/shard_map/ppermute | solution.py:185
  124.5 7.1 %collective-permute-start.33 = (bf16[80,2048]{1,0:T(8,128)(2,1)S(1)}, bf16[80,2048]{1,0:T(8,128)(2,1)S(1)}, u32[]{:S(2)}, u32[]{:S(2)}) collective-permute-start(bf16[80,2048]{1,0:T(8,128)(2,1)S(1)} %get-tuple-element.74), channel_id=1, source_target_pairs={{0,2},{2,0},{4,6},{6,4},{8,10},{10,8},{12,14},{14,12},{1,3},{3,1},... | collective-permute-start | bytes 983048 | tf_op jit(solution)/shard_map/ppermute | solution.py:182
  126.6 22.5 %collective-permute-start.27 = (bf16[80,2048]{1,0:T(8,128)(2,1)S(1)}, bf16[80,2048]{1,0:T(8,128)(2,1)S(1)}, u32[]{:S(2)}, u32[]{:S(2)}) collective-permute-start(bf16[80,2048]{1,0:T(8,128)(2,1)S(1)} %add_convert_fusion.1), channel_id=1, source_target_pairs={{0,8},{2,10},{4,12},{6,14},{8,0},{10,2},{12,4},{14,6},{1,9},{3,11}... | collective-permute-start | bytes 983048 | tf_op jit(solution)/shard_map/ppermute | solution.py:185
  131.7 17.4 %collective-permute-start.34 = (bf16[80,2048]{1,0:T(8,128)(2,1)S(1)}, bf16[80,2048]{1,0:T(8,128)(2,1)S(1)}, u32[]{:S(2)}, u32[]{:S(2)}) collective-permute-start(bf16[80,2048]{1,0:T(8,128)(2,1)S(1)} %add_convert_fusion), channel_id=1, source_target_pairs={{0,12},{2,14},{4,8},{6,10},{8,4},{10,6},{12,0},{14,2},{1,13},{3,15... | collective-permute-start | bytes 983048 | tf_op jit(solution)/shard_map/ppermute | solution.py:185

commit v3 on v2

--- a/solution.py
+++ b/solution.py
@@ -16,40 +16,43 @@
 
 
 def params():
-    return pltpu.CompilerParams(vmem_limit_bytes=20 * 1024 * 1024)
+    return pltpu.CompilerParams(vmem_limit_bytes=28 * 1024 * 1024)
 
 
 def cost(flops, moved):
     return pl.CostEstimate(flops=int(flops), bytes_accessed=int(moved), transcendentals=0)
 
 
-def pack_kernel(keys_ref, values_ref, out_ref):
-    size = keys_ref.shape[1]
-    out_ref[:, :size] = keys_ref[...]
-    out_ref[:, size:] = values_ref[...]
-
-
-def stage_kernel(sec_ref, q_ref, resid_ref, gain_ref, q_out, resid_out, gain_out, inverse_out):
-    half = q_out.shape[1]
-    q_out[...] = q_ref[...]
-    low = pl.multiple_of(sec_ref[0] * half, half)
-    resid_out[...] = resid_ref[:, pl.ds(low, half)]
-    gain_out[...] = gain_ref[:, pl.ds(low, half)]
-    inverse_out[:, :half] = 1.0 / gain_ref[:, pl.ds(low, half)]
-    inverse_out[:, half:] = 1.0 / gain_ref[:, pl.ds(pl.multiple_of(half - low, half), half)]
-
-
-def weights_kernel(sec_ref, gate_ref, up_ref, out_ref, sems):
-    half, hidden = gate_ref.shape[0] // 2, gate_ref.shape[1]
-    copies = []
-    for c in range(2):
-        low = pl.multiple_of(lax.rem(sec_ref[0] + c, 2) * half, half)
-        for n, ref in enumerate((gate_ref, up_ref)):
-            target = out_ref.at[c * half : (c + 1) * half, n * hidden : (n + 1) * hidden]
-            copies.append(pltpu.make_async_copy(ref.at[pl.ds(low, half)], target, sems.at[2 * c + n]))
-            copies[-1].start()
+def copy_all(pairs, sems):
+    copies = [pltpu.make_async_copy(source, target, sems.at[i]) for i, (source, target) in enumerate(pairs)]
+    for copy in copies:
+        copy.start()
     for copy in copies:
         copy.wait()
+
+
+def pack_kernel(keys_ref, values_ref, kv_out, sems):
+    size = keys_ref.shape[1]
+    copy_all([(keys_ref, kv_out.at[:, :size]), (values_ref, kv_out.at[:, size:])], sems)
+
+
+def stage_kernel(sec_ref, q_ref, resid_ref, gain_ref, gate_ref, up_ref, down_ref, *refs):
+    q_out, resid_out, gain_out, columns_out, down_out, sems = refs
+    half, hidden = q_out.shape[1], gate_ref.shape[1]
+    low = pl.multiple_of(sec_ref[0] * half, half)
+    rest = pl.multiple_of((1 - sec_ref[0]) * half, half)
+    pairs = [
+        (q_ref, q_out),
+        (resid_ref.at[:, pl.ds(low, half)], resid_out),
+        (gain_ref.at[:, pl.ds(low, half)], gain_out.at[:, :half]),
+        (gain_ref.at[:, pl.ds(rest, half)], gain_out.at[:, half:]),
+        (down_ref.at[:, pl.ds(low, half)], down_out),
+    ]
+    for c, start in enumerate((low, rest)):
+        for n, ref in enumerate((gate_ref, up_ref)):
+            target = columns_out.at[c * half : (c + 1) * half, n * hidden : (n + 1) * hidden]
+            pairs.append((ref.at[pl.ds(start, half)], target))
+    copy_all(pairs, sems)
 
 
 def attend_kernel(n_pieces, q_ref, resid_ref, gain_ref, pick_ref, *refs):
@@ -71,7 +74,7 @@
         for r in range(group_size):
             low = (g * group_size + r) * HD
             stream_ref[:, low : low + HD] = resid_ref[:, low : low + HD].astype(F32) + attended[r * rows : (r + 1) * rows]
-    scaled = (stream_ref[...] * gain_ref[...]).astype(BF16)
+    scaled = (stream_ref[...] * gain_ref[:, : q_ref.shape[1]]).astype(BF16)
     for k, out_ref in enumerate(outs):
         out_ref[...] = jnp.dot(pick_ref[k], scaled, preferred_element_type=F32).astype(BF16)
 
@@ -95,46 +98,32 @@
         state = (new_max, total, mixed)
     attended = (state[2] / state[1]).transpose(2, 0, 1, 3).reshape(rows, -1).astype(BF16)
     stream = resid.astype(F32) + attended.astype(F32)
-    scaled = (stream * gain).astype(BF16)
+    scaled = (stream * gain[:, : queries.shape[1]]).astype(BF16)
     return [stream] + [jnp.dot(p, scaled, preferred_element_type=F32).astype(BF16) for p in pick]
 
 
-def down_weights_kernel(index_ref, own_ref, near_ref, far_ref, out_ref, sems):
-    hidden, quarter = near_ref.shape
-    low = pl.multiple_of(index_ref[0] * 2 * quarter, quarter)
-    near = pl.multiple_of(index_ref[1] * quarter, quarter)
-    other = pl.multiple_of((1 - index_ref[1]) * quarter, quarter)
-    copies = [
-        pltpu.make_async_copy(own_ref.at[:, pl.ds(low, 2 * quarter)], out_ref.at[:hidden, :], sems.at[0]),
-        pltpu.make_async_copy(near_ref, out_ref.at[hidden:, pl.ds(near, quarter)], sems.at[1]),
-        pltpu.make_async_copy(far_ref, out_ref.at[hidden:, pl.ds(other, quarter)], sems.at[2]),
-    ]
-    for copy in copies:
-        copy.start()
-    for copy in copies:
-        copy.wait()
-
-
-def hidden_kernel(width, own_ref, y_ref, x_ref, both_ref, weights_ref, inverse_ref, act_ref):
+def hidden_kernel(width, own_ref, y_ref, x_ref, both_ref, weights_ref, gain_ref, act_ref):
     half, hidden = own_ref.shape[1], act_ref.shape[1]
     total = square = 0.0
     for c, refs in enumerate(((own_ref, y_ref), (x_ref, both_ref))):
         rows = jnp.concatenate([ref[...] for ref in refs], axis=0)
         columns = slice(c * half, (c + 1) * half)
         total = total + jnp.dot(rows, weights_ref[columns, :], preferred_element_type=F32)
-        stream = rows.astype(F32) * inverse_ref[:, columns]
+        stream = rows.astype(F32) * (1.0 / gain_ref[:, columns])
         square = square + jnp.sum(stream * stream, axis=1, keepdims=True)
     total = total * lax.rsqrt(square / width + 1e-06)
     gate, up = total[:, :hidden], total[:, hidden:]
     act_ref[...] = (gate / (1.0 + jnp.exp(-gate)) * up).astype(BF16)
 
 
-def down_kernel(own_act, other_act, w_ref, keep_ref, send_ref):
-    rows = keep_ref.shape[0]
-    act = jnp.concatenate([own_act[...], other_act[...]], axis=1)
-    total = jnp.dot(act, w_ref[...], preferred_element_type=F32)
-    keep_ref[...] = total[:rows]
-    send_ref[...] = total[rows:].astype(BF16)
+def down_kernel(rep_ref, own_act, other_act, own_ref, near_ref, far_ref, keep_ref, send_ref, total_ref):
+    rows, quarter = keep_ref.shape[0], near_ref.shape[1]
+    total_ref[...] = jnp.dot(own_act[...], own_ref[...], preferred_element_type=F32)
+    for place, ref in ((rep_ref[0], near_ref), (1 - rep_ref[0], far_ref)):
+        columns = pl.ds(pl.multiple_of(place * quarter, quarter), quarter)
+        total_ref[:, columns] += jnp.dot(other_act[...], ref[...], preferred_element_type=F32)
+    keep_ref[...] = total_ref[:rows]
+    send_ref[...] = total_ref[rows:].astype(BF16)
 
 
 def combine_kernel(stream_ref, high_ref, low_ref, *refs):
@@ -187,18 +176,17 @@
     own_kv = pl.pallas_call(
         pack_kernel,
         out_shape=jax.ShapeDtypeStruct((rows, 2 * keys.shape[1]), BF16),
-        in_specs=[VMEM] * 2,
+        in_specs=[ANY] * 2,
         out_specs=VMEM,
+        scratch_shapes=[pltpu.SemaphoreType.DMA((2,))],
         compiler_params=params(),
-        cost_estimate=cost(0, 4 * keys.size * 2),
         name="pack",
-    )(keys, values)
+    )(*far([keys, values]))
     planes = [own_kv] + [over_z(own_kv, k) for k in range(1, n_exp)]
     pieces = planes + [over_y(a) for a in planes]
 
     part = lax.dynamic_slice_in_dim(w_down[0], ((1 - sec) * 2 + rep) * quarter, quarter, 1)
-    down_near = over_sec(part)
-    down_far = over_rep(after(down_near, pieces[n_exp + 1]))
+    down_near = over_sec(after(part, planes[1]))
 
     experts = jnp.arange(n_exp, dtype=jnp.int32)
     onehot = (expert_ids[:, :, None] == experts[None, None, :]).astype(jnp.int32)
@@ -212,34 +200,25 @@
     weight = weight.reshape(rows, n_exp, cap).transpose(1, 0, 2)
     weight_high = weight.astype(BF16)
     weight_low = (weight - weight_high.astype(F32)).astype(BF16)
-    gain = norm_gain.reshape(1, width)
-    index = jnp.stack([sec, rep])
     smem = pl.BlockSpec(memory_space=pltpu.SMEM)
     staged = pl.pallas_call(
         stage_kernel,
         out_shape=[
             pltpu.VMEM((rows, half), BF16),
             pltpu.VMEM((rows, half), BF16),
-            pltpu.VMEM((1, half), F32),
             pltpu.VMEM((1, width), F32),
+            pltpu.VMEM((width, 2 * hidden), BF16),
+            pltpu.VMEM((hidden, half), BF16),
         ],
-        in_specs=[smem] + [VMEM] * 3,
-        out_specs=[VMEM] * 4,
+        in_specs=[smem] + [ANY] * 6,
+        out_specs=[VMEM] * 5,
+        scratch_shapes=[pltpu.SemaphoreType.DMA((9,))],
         compiler_params=params(),
         name="stage",
-    )(sec.reshape(1), *far([queries, resid, gain]))
-    weights = pl.pallas_call(
-        weights_kernel,
-        out_shape=pltpu.VMEM((width, 2 * hidden), BF16),
-        in_specs=[smem] + [ANY] * 2,
-        out_specs=VMEM,
-        scratch_shapes=[pltpu.SemaphoreType.DMA((4,))],
-        compiler_params=params(),
-        name="weights",
-    )(sec.reshape(1), *far([w_gate[0], w_up[0]]))
-    tied = lax.optimization_barrier((pieces[1], pick, weight_high, weight_low, index, weights, down_far, *staged))
-    pieces[1], pick, weight_high, weight_low, index, weights, down_far, *staged = tied
-    queries, resid, gain, inverse = staged
+    )(sec.reshape(1), *far([queries, resid, norm_gain.reshape(1, width), w_gate[0], w_up[0], w_down[0]]))
+    tied = lax.optimization_barrier((pieces[1], pick, weight_high, weight_low, *staged))
+    pieces[1], pick, weight_high, weight_low, *staged = tied
+    queries, resid, gain, columns, down_own = staged
 
     if n_dev > 8:
         stream, *sent = attend_long(queries, resid, gain, pick, pieces)
@@ -255,31 +234,25 @@
             name="attend",
         )(queries, resid, gain, pick, *pieces)
 
-    arrived = [sent[0]] + [over_z(sent[k], k) for k in range(1, n_exp)]
-    down_weights = pl.pallas_call(
-        down_weights_kernel,
-        out_shape=pltpu.VMEM((2 * hidden, half), BF16),
-        in_specs=[smem] + [ANY] * 3,
-        out_specs=VMEM,
-        scratch_shapes=[pltpu.SemaphoreType.DMA((3,))],
-        compiler_params=params(),
-        name="down_weights",
-    )(after(index, stream), *far([w_down[0], down_near, down_far]))
-    arrived[0], down_weights = lax.optimization_barrier((arrived[0], down_weights))
+    arrived = [sent[0]] + [None] * (n_exp - 1)
+    for k in range(1, n_exp):
+        arrived[k] = over_z(after(sent[k], arrived[1]) if k == 3 else sent[k], k)
+    down_far = over_rep(after(down_near, stream))
+    arrived[1] = after(arrived[1], down_far)
     each = max(1, n_exp // 4)
     if each > 1:
         arrived = [jnp.concatenate(arrived[i : i + each], axis=0) for i in range(0, n_exp, each)]
 
     def plane_gather(number, own):
-        if number % 2 == 0:
+        if number < 2:
             from_x, from_y = over_sec(own), over_y(own)
             return own, from_y, from_x, over_y(from_x)
         from_y, from_x = over_y(own), over_sec(own)
         return own, from_y, from_x, over_sec(from_y)
 
-    def experts_of(gathered):
+    def hidden_of(gathered):
         count = gathered[0].shape[0]
-        act = pl.pallas_call(
+        return pl.pallas_call(
             functools.partial(hidden_kernel, width),
             in_specs=[VMEM] * 6,
             out_specs=VMEM,
@@ -287,28 +260,35 @@
             compiler_params=params(),
             cost_estimate=cost(8 * count * width * hidden, 4 * width * hidden),
             name="hidden",
-        )(*gathered, weights, inverse)
-        keep, send = pl.pallas_call(
+        )(*gathered, columns, gain)
+
+    def down_of(act, other_act):
+        count = act.shape[0] // 2
+        return pl.pallas_call(
             down_kernel,
-            in_specs=[VMEM] * 3,
+            in_specs=[smem] + [VMEM] * 5,
             out_specs=[VMEM] * 2,
             out_shape=[jax.ShapeDtypeStruct((count, half), F32), jax.ShapeDtypeStruct((count, half), BF16)],
+            scratch_shapes=[pltpu.VMEM((2 * count, half), F32)],
             compiler_params=params(),
             cost_estimate=cost(8 * count * half * hidden, 4 * half * hidden),
             name="down",
-        )(act, over_sec(act), down_weights)
-        return (keep + over_y(send).astype(F32)).astype(BF16)
-
-    returned = [None] * n_exp
-    gathered = []
-    for g, block in enumerate(arrived):
-        if g > 0:
-            block = after(block, *gathered[-1][1:3])
-        gathered.append(plane_gather(g, block))
-    for g in range(len(arrived)):
-        result = experts_of(gathered[g])
+        )(rep.reshape(1), act, other_act, down_own, down_near, down_far)
+
+    acts, sends, results, returned = [], [], [], [None] * n_exp
+    gathered = [plane_gather(g, block) for g, block in enumerate(arrived)]
+    for g, (own, *others) in enumerate(gathered):
+        if g > 1:
+            own = after(own, sends[g - 2])
+        acts.append(hidden_of((own, *others)))
+        other_act = over_sec(acts[g])
+        if g > 1:
+            other_act = after(other_act, results[g - 2])
+        keep, send = down_of(acts[g], other_act)
+        sends.append(send)
+        results.append((keep + over_y(send).astype(F32)).astype(BF16))
         for n, k in enumerate(range(g * each, (g + 1) * each)):
-            back = result if each == 1 else result[n * cap : (n + 1) * cap]
+            back = results[g] if each == 1 else results[g][n * cap : (n + 1) * cap]
             returned[k] = back if k == 0 else over_z(back, k)
 
     return pl.pallas_call(

time: 153 us -> 141 us (0.922)
  waiting for transfers between devices: 72.5 us -> 59.8 us
  starting transfers between devices: 49.1 us -> 52.3 us
    ppermute x14, waiting for transfers between devices: 31.6 us -> 16.9 us  [over_y(): return lax.ppermute(a, 'dev', [(i, i ^ 1) for i in range(n_dev)])]
    ppermute x11, waiting for transfers between devices: 8.94 us -> 14.4 us  [over_sec(): return lax.ppermute(a, 'sec', [(0, 1), (1, 0)])]
    pallas_call x10 -> x8, Pallas kernels: 13.7 us -> 9.14 us  [the longest x4 5.44 us: hidden_of(): pl.pallas_call(functools.partial(hidden_kernel, width), in_specs=[VMEM] *...]
    ppermute x14, starting transfers between devices: 16.2 us -> 20.7 us  [over_y(): return lax.ppermute(a, 'dev', [(i, i ^ 1) for i in range(n_dev)])]
    ppermute x11, starting transfers between devices: 17.3 us -> 12.9 us  [over_sec(): return lax.ppermute(a, 'sec', [(0, 1), (1, 0)])]
    ppermute x9, waiting for transfers between devices: 31.9 us -> 28.5 us  [over_z(): lax.ppermute(a, 'dev', [(i, (i // 2 ^ k) * 2 + i % 2) for i in range(n_de...]
    ppermute x9, starting transfers between devices: 15.6 us -> 18.7 us  [over_z(): lax.ppermute(a, 'dev', [(i, (i // 2 ^ k) * 2 + i % 2) for i in range(n_de...]
    pallas_call x1, Pallas kernels: 1.44 us -> 3.72 us  [body(): pl.pallas_call(stage_kernel, out_shape=[pltpu.VMEM((rows, half), BF16), p...]
  transfers between devices with their start and end apart: 35 -> 35, of which waited for: 21 -> 16; matrix products, arithmetic and copies ran while one was open for 3% -> 5% of each run, Pallas kernels for 8% -> 12%
where the time goes in v3:
time: 141 us; the launch traced here: 139 us
  waiting for transfers between devices  59.8 us (42%)
  starting transfers between devices  52.3 us (37%)
  Pallas kernels  20.1 us (14%)
  local copies, waits for them, and re-layouts  3.73 us (3%)
  other arithmetic  3.1 us (2%)
    ppermute x9, waiting for transfers between devices, over_z(): lax.ppermute(a, 'dev', [(i, (i // 2 ^ k) * 2 + i % 2) for i in range(n_de...  28.5 us
    ppermute x14, starting transfers between devices, over_y(): return lax.ppermute(a, 'dev', [(i, i ^ 1) for i in range(n_dev)])  20.7 us
    ppermute x9, starting transfers between devices, over_z(): lax.ppermute(a, 'dev', [(i, (i // 2 ^ k) * 2 + i % 2) for i in range(n_de...  18.7 us
    ppermute x14, waiting for transfers between devices, over_y(): return lax.ppermute(a, 'dev', [(i, i ^ 1) for i in range(n_dev)])  16.9 us
    ppermute x11, waiting for transfers between devices, over_sec(): return lax.ppermute(a, 'sec', [(0, 1), (1, 0)])  14.4 us
    ppermute x11, starting transfers between devices, over_sec(): return lax.ppermute(a, 'sec', [(0, 1), (1, 0)])  12.9 us
    pallas_call x4, Pallas kernels, hidden_of(): pl.pallas_call(functools.partial(hidden_kernel, width), in_specs=[VMEM] *...  5.44 us
    pallas_call x1, Pallas kernels, body(): pl.pallas_call(functools.partial(attend_kernel, len(pieces)), in_specs=[V...  4.23 us
  transfers between devices with their start and end apart: 35, of which 16 were waited for; matrix products, arithmetic and copies ran while one was open for 5% of the time, Pallas kernels for 12%

profile of v3, /device:TPU:0, one launch (start us, length us, event | category | flops | bytes accessed | tf_op | source)
XLA Modules:
  0.0 139.3 jit_solution(763724136547818270)
XLA Ops:
  1.0 3.1 %collective-permute-start = (bf16[128,1024]{1,0:T(8,128)(2,1)S(1)}, bf16[128,1024]{1,0:T(8,128)(2,1)S(1)}, u32[]{:S(2)}, u32[]{:S(2)}) collective-permute-start(bf16[128,1024]{1,0:T(8,128)(2,1)S(1)} %pack.1.refs_0_), channel_id=1, source_target_pairs={{0,4},{2,6},{4,0},{6,2},{8,12},{10,14},{12,8},{14,10},{1,5},{3,7},... | collective-permute-start | bytes 786440 | tf_op jit(solution)/shard_map/ppermute | solution.py:174
  4.1 2.6 %collective-permute-start.1 = (bf16[128,1024]{1,0:T(8,128)(2,1)S(1)}, bf16[128,1024]{1,0:T(8,128)(2,1)S(1)}, u32[]{:S(2)}, u32[]{:S(2)}) collective-permute-start(bf16[128,1024]{1,0:T(8,128)(2,1)S(1)} %pack.1.refs_0_), channel_id=1, source_target_pairs={{0,8},{2,10},{4,12},{6,14},{8,0},{10,2},{12,4},{14,6},{1,9},{3,11}... | collective-permute-start | bytes 786440 | tf_op jit(solution)/shard_map/ppermute | solution.py:174
  6.7 1.7 %collective-permute-start.3 = (bf16[128,1024]{1,0:T(8,128)(2,1)S(1)}, bf16[128,1024]{1,0:T(8,128)(2,1)S(1)}, u32[]{:S(2)}, u32[]{:S(2)}) collective-permute-start(bf16[128,1024]{1,0:T(8,128)(2,1)S(1)} %pack.1.refs_0_), channel_id=1, source_target_pairs={{0,2},{2,0},{4,6},{6,4},{8,10},{10,8},{12,14},{14,12},{1,3},{3,1},... | collective-permute-start | bytes 786440 | tf_op jit(solution)/shard_map/ppermute | solution.py:171
  9.4 2.1 %dynamic-slice_bitcast_fusion = bf16[384,1024]{1,0:T(8,128)(2,1)} fusion(bf16[1,384,4096]{2,1,0:T(8,128)(2,1)} %param.19, s32[]{:T(128)S(6)} %select_n.14), kind=kLoop, calls=%fused_computation | loop fusion | bytes 1572868 | tf_op jit(solution)/shard_map/dynamic_slice | solution.py:188
  11.6 1.2 reduce-window.6
  13.2 2.0 %collective-permute-done.refs_1_ = bf16[128,1024]{1,0:T(8,128)(2,1)S(1)} collective-permute-done((bf16[128,1024]{1,0:T(8,128)(2,1)S(1)}, bf16[128,1024]{1,0:T(8,128)(2,1)S(1)}, u32[]{:S(2)}, u32[]{:S(2)}) %collective-permute-start) | collective-permute-done | bytes 262176 | tf_op jit(solution)/shard_map/ppermute | solution.py:174
  15.2 1.7 %collective-permute-start.11 = (bf16[384,1024]{1,0:T(8,128)(2,1)}, bf16[384,1024]{1,0:T(8,128)(2,1)S(1)}, u32[]{:S(2)}, u32[]{:S(2)}) collective-permute-start(bf16[384,1024]{1,0:T(8,128)(2,1)} %dynamic-slice_bitcast_fusion), channel_id=1, source_target_pairs={{0,16},{16,0},{1,17},{17,1},{2,18},{18,2},{3,19},{19,3},{4,20},{20... | collective-permute-start | bytes 2359304 | tf_op jit(solution)/shard_map/ppermute | solution.py:165
  17.8 1.5 %collective-permute-start.4 = (bf16[128,1024]{1,0:T(8,128)(2,1)S(1)}, bf16[128,1024]{1,0:T(8,128)(2,1)S(1)}, u32[]{:S(2)}, u32[]{:S(2)}) collective-permute-start(bf16[128,1024]{1,0:T(8,128)(2,1)S(1)} %collective-permute-done.refs_1_), channel_id=1, source_target_pairs={{0,2},{2,0},{4,6},{6,4},{8,10},{10,8},{12,14},{14,12},{1,3},{3,1},... | collective-permute-start | bytes 786440 | tf_op jit(solution)/shard_map/ppermute | solution.py:171
  19.3 6.1 %collective-permute-done.1.refs_2_ = bf16[128,1024]{1,0:T(8,128)(2,1)S(1)} collective-permute-done((bf16[128,1024]{1,0:T(8,128)(2,1)S(1)}, bf16[128,1024]{1,0:T(8,128)(2,1)S(1)}, u32[]{:S(2)}, u32[]{:S(2)}) %collective-permute-start.1) | collective-permute-done | bytes 262176 | tf_op jit(solution)/shard_map/ppermute | solution.py:174
  25.5 1.5 %collective-permute-start.5 = (bf16[128,1024]{1,0:T(8,128)(2,1)S(1)}, bf16[128,1024]{1,0:T(8,128)(2,1)S(1)}, u32[]{:S(2)}, u32[]{:S(2)}) collective-permute-start(bf16[128,1024]{1,0:T(8,128)(2,1)S(1)} %collective-permute-done.1.refs_2_), channel_id=1, source_target_pairs={{0,2},{2,0},{4,6},{6,4},{8,10},{10,8},{12,14},{14,12},{1,3},{3,1},... | collective-permute-start | bytes 786440 | tf_op jit(solution)/shard_map/ppermute | solution.py:171
  28.4 3.7 %stage.1 = (bf16[128,2048]{1,0:T(8,128)(2,1)S(1)}, bf16[128,2048]{1,0:T(8,128)(2,1)S(1)}, f32[1,4096]{1,0:T(1,128)S(1)}, bf16[4096,768]{1,0:T(8,128)(2,1)S(1)}, bf16[384,2048]{1,0:T(8,128)(2,1)S(1)}) custom-call(s32[1]{0:T(128)} %bitcast.6.sec_ref, bf16[128,2048]{1,0:T(8,128)(2,1)} %q_ref.1, bf16[128,4096]{1,0:T(8,128)(2,1)} %resid_ref.1, ...), custom_call_target="tpu_custom_call" | custom-call | tf_op jit(solution)/shard_map/stage/pallas_call | solution.py:204
  33.1 2.8 %collective-permute-done.6.refs_7_ = bf16[128,1024]{1,0:T(8,128)(2,1)S(1)} collective-permute-done((bf16[128,1024]{1,0:T(8,128)(2,1)S(1)}, bf16[128,1024]{1,0:T(8,128)(2,1)S(1)}, u32[]{:S(2)}, u32[]{:S(2)}) %collective-permute-start.6) | collective-permute-done | bytes 262176 | tf_op jit(solution)/shard_map/ppermute | solution.py:171
  36.0 4.2 %attend.1 = (f32[128,2048]{1,0:T(8,128)}, bf16[80,2048]{1,0:T(8,128)(2,1)S(1)}, bf16[80,2048]{1,0:T(8,128)(2,1)S(1)}, bf16[80,2048]{1,0:T(8,128)(2,1)S(1)}, bf16[80,2048]{1,0:T(8,128)(2,1)S(1)}) custom-call(bf16[128,2048]{1,0:T(8,128)(2,1)S(1)} %get-tuple-element.45.q_ref, bf16[128,2048]{1,0:T(8,128)(2,1)S(1)} %get-tuple-element.46.resid_ref, ...), custom_call_target="tpu_custom_call" | custom-call | flops 1073741824 | bytes 4194304 | tf_op jit(solution)/shard_map/attend/pallas_call | solution.py:227
  40.9 2.0 %collective-permute-start.14 = (bf16[80,2048]{1,0:T(8,128)(2,1)S(1)}, bf16[80,2048]{1,0:T(8,128)(2,1)S(1)}, u32[]{:S(2)}, u32[]{:S(2)}) collective-permute-start(bf16[80,2048]{1,0:T(8,128)(2,1)S(1)} %get-tuple-element.60), channel_id=1, source_target_pairs={{0,4},{2,6},{4,0},{6,2},{8,12},{10,14},{12,8},{14,10},{1,5},{3,7},... | collective-permute-start | bytes 983048 | tf_op jit(solution)/shard_map/ppermute | solution.py:174
  42.8 1.5 %collective-permute-start.21 = (bf16[80,2048]{1,0:T(8,128)(2,1)S(1)}, bf16[80,2048]{1,0:T(8,128)(2,1)S(1)}, u32[]{:S(2)}, u32[]{:S(2)}) collective-permute-start(bf16[80,2048]{1,0:T(8,128)(2,1)S(1)} %get-tuple-element.64), channel_id=1, source_target_pairs={{0,8},{2,10},{4,12},{6,14},{8,0},{10,2},{12,4},{14,6},{1,9},{3,11}... | collective-permute-start | bytes 983048 | tf_op jit(solution)/shard_map/ppermute | solution.py:174
  44.3 1.5 %collective-permute-start.7 = (bf16[80,2048]{1,0:T(8,128)(2,1)S(1)}, bf16[80,2048]{1,0:T(8,128)(2,1)S(1)}, u32[]{:S(2)}, u32[]{:S(2)}) collective-permute-start(bf16[80,2048]{1,0:T(8,128)(2,1)S(1)} %get-tuple-element.53.own_ref), channel_id=1, source_target_pairs={{0,2},{2,0},{4,6},{6,4},{8,10},{10,8},{12,14},{14,12},{1,3},{3,1},... | collective-permute-start | bytes 983048 | tf_op jit(solution)/shard_map/ppermute | solution.py:171
  45.9 4.5 %collective-permute-done.8.x_ref = bf16[80,2048]{1,0:T(8,128)(2,1)S(1)} collective-permute-done((bf16[80,2048]{1,0:T(8,128)(2,1)S(1)}, bf16[80,2048]{1,0:T(8,128)(2,1)S(1)}, u32[]{:S(2)}, u32[]{:S(2)}) %collective-permute-start.8) | collective-permute-done | bytes 327712 | tf_op jit(solution)/shard_map/ppermute | solution.py:165
  50.3 1.5 %collective-permute-start.9 = (bf16[80,2048]{1,0:T(8,128)(2,1)S(1)}, bf16[80,2048]{1,0:T(8,128)(2,1)S(1)}, u32[]{:S(2)}, u32[]{:S(2)}) collective-permute-start(bf16[80,2048]{1,0:T(8,128)(2,1)S(1)} %collective-permute-done.8.x_ref), channel_id=1, source_target_pairs={{0,2},{2,0},{4,6},{6,4},{8,10},{10,8},{12,14},{14,12},{1,3},{3,1},... | collective-permute-start | bytes 983048 | tf_op jit(solution)/shard_map/ppermute | solution.py:171
  51.8 6.0 %collective-permute-done.14.own_ref = bf16[80,2048]{1,0:T(8,128)(2,1)S(1)} collective-permute-done((bf16[80,2048]{1,0:T(8,128)(2,1)S(1)}, bf16[80,2048]{1,0:T(8,128)(2,1)S(1)}, u32[]{:S(2)}, u32[]{:S(2)}) %collective-permute-start.14) | collective-permute-done | bytes 327712 | tf_op jit(solution)/shard_map/ppermute | solution.py:174
  57.8 1.1 collective-permute-start.16
  59.0 1.4 %collective-permute-done.21.own_ref = bf16[80,2048]{1,0:T(8,128)(2,1)S(1)} collective-permute-done((bf16[80,2048]{1,0:T(8,128)(2,1)S(1)}, bf16[80,2048]{1,0:T(8,128)(2,1)S(1)}, u32[]{:S(2)}, u32[]{:S(2)}) %collective-permute-start.21) | collective-permute-done | bytes 327712 | tf_op jit(solution)/shard_map/ppermute | solution.py:174
  60.4 1.5 %collective-permute-start.22 = (bf16[80,2048]{1,0:T(8,128)(2,1)S(1)}, bf16[80,2048]{1,0:T(8,128)(2,1)S(1)}, u32[]{:S(2)}, u32[]{:S(2)}) collective-permute-start(bf16[80,2048]{1,0:T(8,128)(2,1)S(1)} %collective-permute-done.21.own_ref), channel_id=1, source_target_pairs={{0,2},{2,0},{4,6},{6,4},{8,10},{10,8},{12,14},{14,12},{1,3},{3,1},... | collective-permute-start | bytes 983048 | tf_op jit(solution)/shard_map/ppermute | solution.py:171
  61.9 2.5 %collective-permute-start.28 = (bf16[80,2048]{1,0:T(8,128)(2,1)S(1)}, bf16[80,2048]{1,0:T(8,128)(2,1)S(1)}, u32[]{:S(2)}, u32[]{:S(2)}) collective-permute-start(bf16[80,2048]{1,0:T(8,128)(2,1)S(1)} %get-tuple-element.70), channel_id=1, source_target_pairs={{0,12},{2,14},{4,8},{6,10},{8,4},{10,6},{12,0},{14,2},{1,13},{3,15... | collective-permute-start | bytes 983048 | tf_op jit(solution)/shard_map/ppermute | solution.py:174
  64.9 1.3 hidden.4.own_act
  67.1 1.6 %collective-permute-start.17 = (bf16[80,2048]{1,0:T(8,128)(2,1)S(1)}, bf16[80,2048]{1,0:T(8,128)(2,1)S(1)}, u32[]{:S(2)}, u32[]{:S(2)}) collective-permute-start(bf16[80,2048]{1,0:T(8,128)(2,1)S(1)} %collective-permute-done.16.x_ref), channel_id=1, source_target_pairs={{0,2},{2,0},{4,6},{6,4},{8,10},{10,8},{12,14},{14,12},{1,3},{3,1},... | collective-permute-start | bytes 983048 | tf_op jit(solution)/shard_map/ppermute | solution.py:171
  68.7 1.2 collective-permute-done.22.y_ref
  70.0 1.6 %collective-permute-start.23 = (bf16[80,2048]{1,0:T(8,128)(2,1)S(1)}, bf16[80,2048]{1,0:T(8,128)(2,1)S(1)}, u32[]{:S(2)}, u32[]{:S(2)}) collective-permute-start(bf16[80,2048]{1,0:T(8,128)(2,1)S(1)} %collective-permute-done.21.own_ref), channel_id=1, source_target_pairs={{0,16},{16,0},{1,17},{17,1},{2,18},{18,2},{3,19},{19,3},{4,20},{20... | collective-permute-start | bytes 983048 | tf_op jit(solution)/shard_map/ppermute | solution.py:165
  71.6 1.5 %collective-permute-start.29 = (bf16[80,2048]{1,0:T(8,128)(2,1)S(1)}, bf16[80,2048]{1,0:T(8,128)(2,1)S(1)}, u32[]{:S(2)}, u32[]{:S(2)}) collective-permute-start(bf16[80,2048]{1,0:T(8,128)(2,1)S(1)} %collective-permute-done.28.own_ref), channel_id=1, source_target_pairs={{0,2},{2,0},{4,6},{6,4},{8,10},{10,8},{12,14},{14,12},{1,3},{3,1},... | collective-permute-start | bytes 983048 | tf_op jit(solution)/shard_map/ppermute | solution.py:171
  73.1 1.4 %collective-permute-start.24 = (bf16[80,2048]{1,0:T(8,128)(2,1)S(1)}, bf16[80,2048]{1,0:T(8,128)(2,1)S(1)}, u32[]{:S(2)}, u32[]{:S(2)}) collective-permute-start(bf16[80,2048]{1,0:T(8,128)(2,1)S(1)} %collective-permute-done.22.y_ref), channel_id=1, source_target_pairs={{0,16},{16,0},{1,17},{17,1},{2,18},{18,2},{3,19},{19,3},{4,20},{20... | collective-permute-start | bytes 983048 | tf_op jit(solution)/shard_map/ppermute | solution.py:165
  75.4 1.6 %collective-permute-done.15.y_ref = bf16[80,2048]{1,0:T(8,128)(2,1)S(1)} collective-permute-done((bf16[80,2048]{1,0:T(8,128)(2,1)S(1)}, bf16[80,2048]{1,0:T(8,128)(2,1)S(1)}, u32[]{:S(2)}, u32[]{:S(2)}) %collective-permute-start.15) | collective-permute-done | bytes 327712 | tf_op jit(solution)/shard_map/ppermute | solution.py:171
  77.0 2.5 %collective-permute-start.13 = (bf16[80,2048]{1,0:T(8,128)(2,1)S(1)}, bf16[80,2048]{1,0:T(8,128)(2,1)S(1)}, u32[]{:S(2)}, u32[]{:S(2)}) collective-permute-start(bf16[80,2048]{1,0:T(8,128)(2,1)S(1)} %get-tuple-element.59), channel_id=1, source_target_pairs={{0,2},{2,0},{4,6},{6,4},{8,10},{10,8},{12,14},{14,12},{1,3},{3,1},... | collective-permute-start | bytes 983048 | tf_op jit(solution)/shard_map/ppermute | solution.py:171
  79.5 4.5 %collective-permute-done.17.both_ref = bf16[80,2048]{1,0:T(8,128)(2,1)S(1)} collective-permute-done((bf16[80,2048]{1,0:T(8,128)(2,1)S(1)}, bf16[80,2048]{1,0:T(8,128)(2,1)S(1)}, u32[]{:S(2)}, u32[]{:S(2)}) %collective-permute-start.17) | collective-permute-done | bytes 327712 | tf_op jit(solution)/shard_map/ppermute | solution.py:171
  84.0 1.3 hidden.5.own_act
  85.3 1.7 %collective-permute-start.18 = (bf16[160,384]{1,0:T(8,128)(2,1)S(1)}, bf16[160,384]{1,0:T(8,128)(2,1)S(1)}, u32[]{:S(2)}, u32[]{:S(2)}) collective-permute-start(bf16[160,384]{1,0:T(8,128)(2,1)S(1)} %hidden.5.own_act), channel_id=1, source_target_pairs={{0,16},{16,0},{1,17},{17,1},{2,18},{18,2},{3,19},{19,3},{4,20},{20... | collective-permute-start | bytes 368648 | tf_op jit(solution)/shard_map/ppermute | solution.py:165
  87.4 3.6 %collective-permute-done.29.y_ref = bf16[80,2048]{1,0:T(8,128)(2,1)S(1)} collective-permute-done((bf16[80,2048]{1,0:T(8,128)(2,1)S(1)}, bf16[80,2048]{1,0:T(8,128)(2,1)S(1)}, u32[]{:S(2)}, u32[]{:S(2)}) %collective-permute-start.29) | collective-permute-done | bytes 327712 | tf_op jit(solution)/shard_map/ppermute | solution.py:171
  91.0 1.6 %collective-permute-start.31 = (bf16[80,2048]{1,0:T(8,128)(2,1)S(1)}, bf16[80,2048]{1,0:T(8,128)(2,1)S(1)}, u32[]{:S(2)}, u32[]{:S(2)}) collective-permute-start(bf16[80,2048]{1,0:T(8,128)(2,1)S(1)} %collective-permute-done.29.y_ref), channel_id=1, source_target_pairs={{0,16},{16,0},{1,17},{17,1},{2,18},{18,2},{3,19},{19,3},{4,20},{20... | collective-permute-start | bytes 983048 | tf_op jit(solution)/shard_map/ppermute | solution.py:165
  92.6 1.3 hidden.6.own_act
  95.4 2.6 %collective-permute-start.19 = (bf16[80,2048]{1,0:T(8,128)(2,1)S(1)}, bf16[80,2048]{1,0:T(8,128)(2,1)S(1)}, u32[]{:S(2)}, u32[]{:S(2)}) collective-permute-start(bf16[80,2048]{1,0:T(8,128)(2,1)S(1)} %get-tuple-element.63), channel_id=1, source_target_pairs={{0,2},{2,0},{4,6},{6,4},{8,10},{10,8},{12,14},{14,12},{1,3},{3,1},... | collective-permute-start | bytes 983048 | tf_op jit(solution)/shard_map/ppermute | solution.py:171
  98.0 6.5 %collective-permute-done.25.other_act = bf16[160,384]{1,0:T(8,128)(2,1)S(1)} collective-permute-done((bf16[160,384]{1,0:T(8,128)(2,1)S(1)}, bf16[160,384]{1,0:T(8,128)(2,1)S(1)}, u32[]{:S(2)}, u32[]{:S(2)}) %collective-permute-start.25) | collective-permute-done | bytes 122912 | tf_op jit(solution)/shard_map/ppermute | solution.py:165
  105.9 1.5 %hidden.7.own_act = bf16[160,384]{1,0:T(8,128)(2,1)S(1)} custom-call(bf16[80,2048]{1,0:T(8,128)(2,1)S(1)} %collective-permute-done.28.own_ref, bf16[80,2048]{1,0:T(8,128)(2,1)S(1)} %collective-permute-done.29.y_ref, bf16[80,2048]{1,0:T(8,128)(2,1)S(1)} %collective-permute-done.30.x_ref, bf16[80,2048]{1,0:T(8,128)(2,1)S(1)} %collective-permute-done.31.both_ref, ...), custom_call_target="tpu_custom_call" | custom-call | flops 1006632960 | bytes 6291456 | tf_op jit(solution)/shard_map/hidden/pallas_call | solution.py:255
  107.4 1.7 %collective-permute-start.32 = (bf16[160,384]{1,0:T(8,128)(2,1)S(1)}, bf16[160,384]{1,0:T(8,128)(2,1)S(1)}, u32[]{:S(2)}, u32[]{:S(2)}) collective-permute-start(bf16[160,384]{1,0:T(8,128)(2,1)S(1)} %hidden.7.own_act), channel_id=1, source_target_pairs={{0,16},{16,0},{1,17},{17,1},{2,18},{18,2},{3,19},{19,3},{4,20},{20... | collective-permute-start | bytes 368648 | tf_op jit(solution)/shard_map/ppermute | solution.py:165
  109.2 3.1 %collective-permute-done.32.other_act = bf16[160,384]{1,0:T(8,128)(2,1)S(1)} collective-permute-done((bf16[160,384]{1,0:T(8,128)(2,1)S(1)}, bf16[160,384]{1,0:T(8,128)(2,1)S(1)}, u32[]{:S(2)}, u32[]{:S(2)}) %collective-permute-start.32) | collective-permute-done | bytes 122912 | tf_op jit(solution)/shard_map/ppermute | solution.py:165
  113.3 1.7 %collective-permute-start.33 = (bf16[80,2048]{1,0:T(8,128)(2,1)S(1)}, bf16[80,2048]{1,0:T(8,128)(2,1)S(1)}, u32[]{:S(2)}, u32[]{:S(2)}) collective-permute-start(bf16[80,2048]{1,0:T(8,128)(2,1)S(1)} %get-tuple-element.74), channel_id=1, source_target_pairs={{0,2},{2,0},{4,6},{6,4},{8,10},{10,8},{12,14},{14,12},{1,3},{3,1},... | collective-permute-start | bytes 983048 | tf_op jit(solution)/shard_map/ppermute | solution.py:171
  116.2 2.2 %collective-permute-start.20 = (bf16[80,2048]{1,0:T(8,128)(2,1)S(1)}, bf16[80,2048]{1,0:T(8,128)(2,1)S(1)}, u32[]{:S(2)}, u32[]{:S(2)}) collective-permute-start(bf16[80,2048]{1,0:T(8,128)(2,1)S(1)} %add_convert_fusion.2), channel_id=1, source_target_pairs={{0,4},{2,6},{4,0},{6,2},{8,12},{10,14},{12,8},{14,10},{1,5},{3,7},... | collective-permute-start | bytes 983048 | tf_op jit(solution)/shard_map/ppermute | solution.py:174
  118.3 2.1 %collective-permute-done.33 = bf16[80,2048]{1,0:T(8,128)(2,1)S(1)} collective-permute-done((bf16[80,2048]{1,0:T(8,128)(2,1)S(1)}, bf16[80,2048]{1,0:T(8,128)(2,1)S(1)}, u32[]{:S(2)}, u32[]{:S(2)}) %collective-permute-start.33) | collective-permute-done | bytes 327712 | tf_op jit(solution)/shard_map/ppermute | solution.py:171
  120.5 3.8 %collective-permute-start.34 = (bf16[80,2048]{1,0:T(8,128)(2,1)S(1)}, bf16[80,2048]{1,0:T(8,128)(2,1)S(1)}, u32[]{:S(2)}, u32[]{:S(2)}) collective-permute-start(bf16[80,2048]{1,0:T(8,128)(2,1)S(1)} %add_convert_fusion), channel_id=1, source_target_pairs={{0,12},{2,14},{4,8},{6,10},{8,4},{10,6},{12,0},{14,2},{1,13},{3,15... | collective-permute-start | bytes 983048 | tf_op jit(solution)/shard_map/ppermute | solution.py:174
  124.3 12.9 %collective-permute-done.27.refs_2_ = bf16[80,2048]{1,0:T(8,128)(2,1)S(1)} collective-permute-done((bf16[80,2048]{1,0:T(8,128)(2,1)S(1)}, bf16[80,2048]{1,0:T(8,128)(2,1)S(1)}, u32[]{:S(2)}, u32[]{:S(2)}) %collective-permute-start.27) | collective-permute-done | bytes 327712 | tf_op jit(solution)/shard_map/ppermute | solution.py:174
  137.2 2.0 %combine.1 = bf16[128,2048]{1,0:T(8,128)(2,1)} custom-call(f32[128,2048]{1,0:T(8,128)S(1)} %copy-done, bf16[4,128,80]{2,1,0:T(8,128)(2,1)S(1)} %get-tuple-element.51.high_ref, bf16[4,128,80]{2,1,0:T(8,128)(2,1)S(1)} %get-tuple-element.52.low_ref, bf16[80,2048]{1,0:T(8,128)(2,1)S(1)} %add_convert_fusion.3.refs_0_, ...), custom_call_target="tpu_custom_call" | custom-call | flops 335544320 | bytes 2883584 | tf_op jit(solution)/shard_map/combine/pallas_call | solution.py:294
  (59 shorter events, 14.3 us)
Async XLA Ops:
  1.0 14.2 %collective-permute-start = (bf16[128,1024]{1,0:T(8,128)(2,1)S(1)}, bf16[128,1024]{1,0:T(8,128)(2,1)S(1)}, u32[]{:S(2)}, u32[]{:S(2)}) collective-permute-start(bf16[128,1024]{1,0:T(8,128)(2,1)S(1)} %pack.1.refs_0_), channel_id=1, source_target_pairs={{0,4},{2,6},{4,0},{6,2},{8,12},{10,14},{12,8},{14,10},{1,5},{3,7},... | collective-permute-start | bytes 786440 | tf_op jit(solution)/shard_map/ppermute | solution.py:174
  4.1 21.4 %collective-permute-start.1 = (bf16[128,1024]{1,0:T(8,128)(2,1)S(1)}, bf16[128,1024]{1,0:T(8,128)(2,1)S(1)}, u32[]{:S(2)}, u32[]{:S(2)}) collective-permute-start(bf16[128,1024]{1,0:T(8,128)(2,1)S(1)} %pack.1.refs_0_), channel_id=1, source_target_pairs={{0,8},{2,10},{4,12},{6,14},{8,0},{10,2},{12,4},{14,6},{1,9},{3,11}... | collective-permute-start | bytes 786440 | tf_op jit(solution)/shard_map/ppermute | solution.py:174
  6.7 20.3 %collective-permute-start.2 = (bf16[128,1024]{1,0:T(8,128)(2,1)S(1)}, bf16[128,1024]{1,0:T(8,128)(2,1)S(1)}, u32[]{:S(2)}, u32[]{:S(2)}) collective-permute-start(bf16[128,1024]{1,0:T(8,128)(2,1)S(1)} %pack.1.refs_0_), channel_id=1, source_target_pairs={{0,12},{2,14},{4,8},{6,10},{8,4},{10,6},{12,0},{14,2},{1,13},{3,15... | collective-permute-start | bytes 786440 | tf_op jit(solution)/shard_map/ppermute | solution.py:174
  6.7 25.5 %collective-permute-start.3 = (bf16[128,1024]{1,0:T(8,128)(2,1)S(1)}, bf16[128,1024]{1,0:T(8,128)(2,1)S(1)}, u32[]{:S(2)}, u32[]{:S(2)}) collective-permute-start(bf16[128,1024]{1,0:T(8,128)(2,1)S(1)} %pack.1.refs_0_), channel_id=1, source_target_pairs={{0,2},{2,0},{4,6},{6,4},{8,10},{10,8},{12,14},{14,12},{1,3},{3,1},... | collective-permute-start | bytes 786440 | tf_op jit(solution)/shard_map/ppermute | solution.py:171
  15.2 24.9 %collective-permute-start.11 = (bf16[384,1024]{1,0:T(8,128)(2,1)}, bf16[384,1024]{1,0:T(8,128)(2,1)S(1)}, u32[]{:S(2)}, u32[]{:S(2)}) collective-permute-start(bf16[384,1024]{1,0:T(8,128)(2,1)} %dynamic-slice_bitcast_fusion), channel_id=1, source_target_pairs={{0,16},{16,0},{1,17},{17,1},{2,18},{18,2},{3,19},{19,3},{4,20},{20... | collective-permute-start | bytes 2359304 | tf_op jit(solution)/shard_map/ppermute | solution.py:165
  17.8 14.3 %collective-permute-start.4 = (bf16[128,1024]{1,0:T(8,128)(2,1)S(1)}, bf16[128,1024]{1,0:T(8,128)(2,1)S(1)}, u32[]{:S(2)}, u32[]{:S(2)}) collective-permute-start(bf16[128,1024]{1,0:T(8,128)(2,1)S(1)} %collective-permute-done.refs_1_), channel_id=1, source_target_pairs={{0,2},{2,0},{4,6},{6,4},{8,10},{10,8},{12,14},{14,12},{1,3},{3,1},... | collective-permute-start | bytes 786440 | tf_op jit(solution)/shard_map/ppermute | solution.py:171
  25.5 7.7 %collective-permute-start.5 = (bf16[128,1024]{1,0:T(8,128)(2,1)S(1)}, bf16[128,1024]{1,0:T(8,128)(2,1)S(1)}, u32[]{:S(2)}, u32[]{:S(2)}) collective-permute-start(bf16[128,1024]{1,0:T(8,128)(2,1)S(1)} %collective-permute-done.1.refs_2_), channel_id=1, source_target_pairs={{0,2},{2,0},{4,6},{6,4},{8,10},{10,8},{12,14},{14,12},{1,3},{3,1},... | collective-permute-start | bytes 786440 | tf_op jit(solution)/shard_map/ppermute | solution.py:171
  27.0 9.0 %collective-permute-start.6 = (bf16[128,1024]{1,0:T(8,128)(2,1)S(1)}, bf16[128,1024]{1,0:T(8,128)(2,1)S(1)}, u32[]{:S(2)}, u32[]{:S(2)}) collective-permute-start(bf16[128,1024]{1,0:T(8,128)(2,1)S(1)} %collective-permute-done.2.refs_3_), channel_id=1, source_target_pairs={{0,2},{2,0},{4,6},{6,4},{8,10},{10,8},{12,14},{14,12},{1,3},{3,1},... | collective-permute-start | bytes 786440 | tf_op jit(solution)/shard_map/ppermute | solution.py:171
  40.2 17.7 %collective-permute-start.12 = (bf16[384,1024]{1,0:T(8,128)(2,1)S(1)}, bf16[384,1024]{1,0:T(8,128)(2,1)S(1)}, u32[]{:S(2)}, u32[]{:S(2)}) collective-permute-start(bf16[384,1024]{1,0:T(8,128)(2,1)S(1)} %collective-permute-done.11.near_ref), channel_id=1, source_target_pairs={{0,1},{1,0},{2,3},{3,2},{4,5},{5,4},{6,7},{7,6},{8,9},{9,8},{10,11... | collective-permute-start | bytes 2359304 | tf_op jit(solution)/shard_map/ppermute | solution.py:168
  40.2 10.1 %collective-permute-start.8 = (bf16[80,2048]{1,0:T(8,128)(2,1)S(1)}, bf16[80,2048]{1,0:T(8,128)(2,1)S(1)}, u32[]{:S(2)}, u32[]{:S(2)}) collective-permute-start(bf16[80,2048]{1,0:T(8,128)(2,1)S(1)} %get-tuple-element.53.own_ref), channel_id=1, source_target_pairs={{0,16},{16,0},{1,17},{17,1},{2,18},{18,2},{3,19},{19,3},{4,20},{20... | collective-permute-start | bytes 983048 | tf_op jit(solution)/shard_map/ppermute | solution.py:165
  40.9 17.0 %collective-permute-start.14 = (bf16[80,2048]{1,0:T(8,128)(2,1)S(1)}, bf16[80,2048]{1,0:T(8,128)(2,1)S(1)}, u32[]{:S(2)}, u32[]{:S(2)}) collective-permute-start(bf16[80,2048]{1,0:T(8,128)(2,1)S(1)} %get-tuple-element.60), channel_id=1, source_target_pairs={{0,4},{2,6},{4,0},{6,2},{8,12},{10,14},{12,8},{14,10},{1,5},{3,7},... | collective-permute-start | bytes 983048 | tf_op jit(solution)/shard_map/ppermute | solution.py:174
  42.8 17.5 %collective-permute-start.21 = (bf16[80,2048]{1,0:T(8,128)(2,1)S(1)}, bf16[80,2048]{1,0:T(8,128)(2,1)S(1)}, u32[]{:S(2)}, u32[]{:S(2)}) collective-permute-start(bf16[80,2048]{1,0:T(8,128)(2,1)S(1)} %get-tuple-element.64), channel_id=1, source_target_pairs={{0,8},{2,10},{4,12},{6,14},{8,0},{10,2},{12,4},{14,6},{1,9},{3,11}... | collective-permute-start | bytes 983048 | tf_op jit(solution)/shard_map/ppermute | solution.py:174
  44.3 20.0 %collective-permute-start.7 = (bf16[80,2048]{1,0:T(8,128)(2,1)S(1)}, bf16[80,2048]{1,0:T(8,128)(2,1)S(1)}, u32[]{:S(2)}, u32[]{:S(2)}) collective-permute-start(bf16[80,2048]{1,0:T(8,128)(2,1)S(1)} %get-tuple-element.53.own_ref), channel_id=1, source_target_pairs={{0,2},{2,0},{4,6},{6,4},{8,10},{10,8},{12,14},{14,12},{1,3},{3,1},... | collective-permute-start | bytes 983048 | tf_op jit(solution)/shard_map/ppermute | solution.py:171
  50.3 14.6 %collective-permute-start.9 = (bf16[80,2048]{1,0:T(8,128)(2,1)S(1)}, bf16[80,2048]{1,0:T(8,128)(2,1)S(1)}, u32[]{:S(2)}, u32[]{:S(2)}) collective-permute-start(bf16[80,2048]{1,0:T(8,128)(2,1)S(1)} %collective-permute-done.8.x_ref), channel_id=1, source_target_pairs={{0,2},{2,0},{4,6},{6,4},{8,10},{10,8},{12,14},{14,12},{1,3},{3,1},... | collective-permute-start | bytes 983048 | tf_op jit(solution)/shard_map/ppermute | solution.py:171
  57.8 9.3 %collective-permute-start.16 = (bf16[80,2048]{1,0:T(8,128)(2,1)S(1)}, bf16[80,2048]{1,0:T(8,128)(2,1)S(1)}, u32[]{:S(2)}, u32[]{:S(2)}) collective-permute-start(bf16[80,2048]{1,0:T(8,128)(2,1)S(1)} %collective-permute-done.14.own_ref), channel_id=1, source_target_pairs={{0,16},{16,0},{1,17},{17,1},{2,18},{18,2},{3,19},{19,3},{4,20},{20... | collective-permute-start | bytes 983048 | tf_op jit(solution)/shard_map/ppermute | solution.py:165
  60.4 9.6 %collective-permute-start.22 = (bf16[80,2048]{1,0:T(8,128)(2,1)S(1)}, bf16[80,2048]{1,0:T(8,128)(2,1)S(1)}, u32[]{:S(2)}, u32[]{:S(2)}) collective-permute-start(bf16[80,2048]{1,0:T(8,128)(2,1)S(1)} %collective-permute-done.21.own_ref), channel_id=1, source_target_pairs={{0,2},{2,0},{4,6},{6,4},{8,10},{10,8},{12,14},{14,12},{1,3},{3,1},... | collective-permute-start | bytes 983048 | tf_op jit(solution)/shard_map/ppermute | solution.py:171
  61.9 9.7 %collective-permute-start.28 = (bf16[80,2048]{1,0:T(8,128)(2,1)S(1)}, bf16[80,2048]{1,0:T(8,128)(2,1)S(1)}, u32[]{:S(2)}, u32[]{:S(2)}) collective-permute-start(bf16[80,2048]{1,0:T(8,128)(2,1)S(1)} %get-tuple-element.70), channel_id=1, source_target_pairs={{0,12},{2,14},{4,8},{6,10},{8,4},{10,6},{12,0},{14,2},{1,13},{3,15... | collective-permute-start | bytes 983048 | tf_op jit(solution)/shard_map/ppermute | solution.py:174
  64.4 12.6 %collective-permute-start.15 = (bf16[80,2048]{1,0:T(8,128)(2,1)S(1)}, bf16[80,2048]{1,0:T(8,128)(2,1)S(1)}, u32[]{:S(2)}, u32[]{:S(2)}) collective-permute-start(bf16[80,2048]{1,0:T(8,128)(2,1)S(1)} %collective-permute-done.14.own_ref), channel_id=1, source_target_pairs={{0,2},{2,0},{4,6},{6,4},{8,10},{10,8},{12,14},{14,12},{1,3},{3,1},... | collective-permute-start | bytes 983048 | tf_op jit(solution)/shard_map/ppermute | solution.py:171
  66.2 6.9 %collective-permute-start.10 = (bf16[160,384]{1,0:T(8,128)(2,1)S(1)}, bf16[160,384]{1,0:T(8,128)(2,1)S(1)}, u32[]{:S(2)}, u32[]{:S(2)}) collective-permute-start(bf16[160,384]{1,0:T(8,128)(2,1)S(1)} %hidden.4.own_act), channel_id=1, source_target_pairs={{0,16},{16,0},{1,17},{17,1},{2,18},{18,2},{3,19},{19,3},{4,20},{20... | collective-permute-start | bytes 368648 | tf_op jit(solution)/shard_map/ppermute | solution.py:165
  67.1 16.9 %collective-permute-start.17 = (bf16[80,2048]{1,0:T(8,128)(2,1)S(1)}, bf16[80,2048]{1,0:T(8,128)(2,1)S(1)}, u32[]{:S(2)}, u32[]{:S(2)}) collective-permute-start(bf16[80,2048]{1,0:T(8,128)(2,1)S(1)} %collective-permute-done.16.x_ref), channel_id=1, source_target_pairs={{0,2},{2,0},{4,6},{6,4},{8,10},{10,8},{12,14},{14,12},{1,3},{3,1},... | collective-permute-start | bytes 983048 | tf_op jit(solution)/shard_map/ppermute | solution.py:171
  70.0 17.0 %collective-permute-start.23 = (bf16[80,2048]{1,0:T(8,128)(2,1)S(1)}, bf16[80,2048]{1,0:T(8,128)(2,1)S(1)}, u32[]{:S(2)}, u32[]{:S(2)}) collective-permute-start(bf16[80,2048]{1,0:T(8,128)(2,1)S(1)} %collective-permute-done.21.own_ref), channel_id=1, source_target_pairs={{0,16},{16,0},{1,17},{17,1},{2,18},{18,2},{3,19},{19,3},{4,20},{20... | collective-permute-start | bytes 983048 | tf_op jit(solution)/shard_map/ppermute | solution.py:165
  71.6 19.5 %collective-permute-start.29 = (bf16[80,2048]{1,0:T(8,128)(2,1)S(1)}, bf16[80,2048]{1,0:T(8,128)(2,1)S(1)}, u32[]{:S(2)}, u32[]{:S(2)}) collective-permute-start(bf16[80,2048]{1,0:T(8,128)(2,1)S(1)} %collective-permute-done.28.own_ref), channel_id=1, source_target_pairs={{0,2},{2,0},{4,6},{6,4},{8,10},{10,8},{12,14},{14,12},{1,3},{3,1},... | collective-permute-start | bytes 983048 | tf_op jit(solution)/shard_map/ppermute | solution.py:171
  73.1 19.5 %collective-permute-start.24 = (bf16[80,2048]{1,0:T(8,128)(2,1)S(1)}, bf16[80,2048]{1,0:T(8,128)(2,1)S(1)}, u32[]{:S(2)}, u32[]{:S(2)}) collective-permute-start(bf16[80,2048]{1,0:T(8,128)(2,1)S(1)} %collective-permute-done.22.y_ref), channel_id=1, source_target_pairs={{0,16},{16,0},{1,17},{17,1},{2,18},{18,2},{3,19},{19,3},{4,20},{20... | collective-permute-start | bytes 983048 | tf_op jit(solution)/shard_map/ppermute | solution.py:165
  77.0 20.9 %collective-permute-start.13 = (bf16[80,2048]{1,0:T(8,128)(2,1)S(1)}, bf16[80,2048]{1,0:T(8,128)(2,1)S(1)}, u32[]{:S(2)}, u32[]{:S(2)}) collective-permute-start(bf16[80,2048]{1,0:T(8,128)(2,1)S(1)} %get-tuple-element.59), channel_id=1, source_target_pairs={{0,2},{2,0},{4,6},{6,4},{8,10},{10,8},{12,14},{14,12},{1,3},{3,1},... | collective-permute-start | bytes 983048 | tf_op jit(solution)/shard_map/ppermute | solution.py:171
  85.3 9.1 %collective-permute-start.18 = (bf16[160,384]{1,0:T(8,128)(2,1)S(1)}, bf16[160,384]{1,0:T(8,128)(2,1)S(1)}, u32[]{:S(2)}, u32[]{:S(2)}) collective-permute-start(bf16[160,384]{1,0:T(8,128)(2,1)S(1)} %hidden.5.own_act), channel_id=1, source_target_pairs={{0,16},{16,0},{1,17},{17,1},{2,18},{18,2},{3,19},{19,3},{4,20},{20... | collective-permute-start | bytes 368648 | tf_op jit(solution)/shard_map/ppermute | solution.py:165
  87.0 18.9 %collective-permute-start.30 = (bf16[80,2048]{1,0:T(8,128)(2,1)S(1)}, bf16[80,2048]{1,0:T(8,128)(2,1)S(1)}, u32[]{:S(2)}, u32[]{:S(2)}) collective-permute-start(bf16[80,2048]{1,0:T(8,128)(2,1)S(1)} %collective-permute-done.28.own_ref), channel_id=1, source_target_pairs={{0,16},{16,0},{1,17},{17,1},{2,18},{18,2},{3,19},{19,3},{4,20},{20... | collective-permute-start | bytes 983048 | tf_op jit(solution)/shard_map/ppermute | solution.py:165
  91.0 14.9 %collective-permute-start.31 = (bf16[80,2048]{1,0:T(8,128)(2,1)S(1)}, bf16[80,2048]{1,0:T(8,128)(2,1)S(1)}, u32[]{:S(2)}, u32[]{:S(2)}) collective-permute-start(bf16[80,2048]{1,0:T(8,128)(2,1)S(1)} %collective-permute-done.29.y_ref), channel_id=1, source_target_pairs={{0,16},{16,0},{1,17},{17,1},{2,18},{18,2},{3,19},{19,3},{4,20},{20... | collective-permute-start | bytes 983048 | tf_op jit(solution)/shard_map/ppermute | solution.py:165
  93.9 10.6 %collective-permute-start.25 = (bf16[160,384]{1,0:T(8,128)(2,1)S(1)}, bf16[160,384]{1,0:T(8,128)(2,1)S(1)}, u32[]{:S(2)}, u32[]{:S(2)}) collective-permute-start(bf16[160,384]{1,0:T(8,128)(2,1)S(1)} %hidden.6.own_act), channel_id=1, source_target_pairs={{0,16},{16,0},{1,17},{17,1},{2,18},{18,2},{3,19},{19,3},{4,20},{20... | collective-permute-start | bytes 368648 | tf_op jit(solution)/shard_map/ppermute | solution.py:165
  95.4 13.7 %collective-permute-start.19 = (bf16[80,2048]{1,0:T(8,128)(2,1)S(1)}, bf16[80,2048]{1,0:T(8,128)(2,1)S(1)}, u32[]{:S(2)}, u32[]{:S(2)}) collective-permute-start(bf16[80,2048]{1,0:T(8,128)(2,1)S(1)} %get-tuple-element.63), channel_id=1, source_target_pairs={{0,2},{2,0},{4,6},{6,4},{8,10},{10,8},{12,14},{14,12},{1,3},{3,1},... | collective-permute-start | bytes 983048 | tf_op jit(solution)/shard_map/ppermute | solution.py:171
  105.4 9.6 %collective-permute-start.26 = (bf16[80,2048]{1,0:T(8,128)(2,1)S(1)}, bf16[80,2048]{1,0:T(8,128)(2,1)S(1)}, u32[]{:S(2)}, u32[]{:S(2)}) collective-permute-start(bf16[80,2048]{1,0:T(8,128)(2,1)S(1)} %get-tuple-element.68), channel_id=1, source_target_pairs={{0,2},{2,0},{4,6},{6,4},{8,10},{10,8},{12,14},{14,12},{1,3},{3,1},... | collective-permute-start | bytes 983048 | tf_op jit(solution)/shard_map/ppermute | solution.py:171
  107.4 4.9 %collective-permute-start.32 = (bf16[160,384]{1,0:T(8,128)(2,1)S(1)}, bf16[160,384]{1,0:T(8,128)(2,1)S(1)}, u32[]{:S(2)}, u32[]{:S(2)}) collective-permute-start(bf16[160,384]{1,0:T(8,128)(2,1)S(1)} %hidden.7.own_act), channel_id=1, source_target_pairs={{0,16},{16,0},{1,17},{17,1},{2,18},{18,2},{3,19},{19,3},{4,20},{20... | collective-permute-start | bytes 368648 | tf_op jit(solution)/shard_map/ppermute | solution.py:165
  109.2 28.1 %copy-start = (f32[128,2048]{1,0:T(8,128)S(1)}, f32[128,2048]{1,0:T(8,128)}, u32[]{:S(2)}) copy-start(f32[128,2048]{1,0:T(8,128)} %get-tuple-element.50.stream_ref) | copy-start | bytes 3145732
  113.3 7.1 %collective-permute-start.33 = (bf16[80,2048]{1,0:T(8,128)(2,1)S(1)}, bf16[80,2048]{1,0:T(8,128)(2,1)S(1)}, u32[]{:S(2)}, u32[]{:S(2)}) collective-permute-start(bf16[80,2048]{1,0:T(8,128)(2,1)S(1)} %get-tuple-element.74), channel_id=1, source_target_pairs={{0,2},{2,0},{4,6},{6,4},{8,10},{10,8},{12,14},{14,12},{1,3},{3,1},... | collective-permute-start | bytes 983048 | tf_op jit(solution)/shard_map/ppermute | solution.py:171
  115.1 22.1 %collective-permute-start.27 = (bf16[80,2048]{1,0:T(8,128)(2,1)S(1)}, bf16[80,2048]{1,0:T(8,128)(2,1)S(1)}, u32[]{:S(2)}, u32[]{:S(2)}) collective-permute-start(bf16[80,2048]{1,0:T(8,128)(2,1)S(1)} %add_convert_fusion.1), channel_id=1, source_target_pairs={{0,8},{2,10},{4,12},{6,14},{8,0},{10,2},{12,4},{14,6},{1,9},{3,11}... | collective-permute-start | bytes 983048 | tf_op jit(solution)/shard_map/ppermute | solution.py:174
  116.2 21.1 %collective-permute-start.20 = (bf16[80,2048]{1,0:T(8,128)(2,1)S(1)}, bf16[80,2048]{1,0:T(8,128)(2,1)S(1)}, u32[]{:S(2)}, u32[]{:S(2)}) collective-permute-start(bf16[80,2048]{1,0:T(8,128)(2,1)S(1)} %add_convert_fusion.2), channel_id=1, source_target_pairs={{0,4},{2,6},{4,0},{6,2},{8,12},{10,14},{12,8},{14,10},{1,5},{3,7},... | collective-permute-start | bytes 983048 | tf_op jit(solution)/shard_map/ppermute | solution.py:174
  120.5 16.8 %collective-permute-start.34 = (bf16[80,2048]{1,0:T(8,128)(2,1)S(1)}, bf16[80,2048]{1,0:T(8,128)(2,1)S(1)}, u32[]{:S(2)}, u32[]{:S(2)}) collective-permute-start(bf16[80,2048]{1,0:T(8,128)(2,1)S(1)} %add_convert_fusion), channel_id=1, source_target_pairs={{0,12},{2,14},{4,8},{6,10},{8,4},{10,6},{12,0},{14,2},{1,13},{3,15... | collective-permute-start | bytes 983048 | tf_op jit(solution)/shard_map/ppermute | solution.py:174

commit v4 on v3

--- a/solution.py
+++ b/solution.py
@@ -128,12 +128,15 @@
 
 def combine_kernel(stream_ref, high_ref, low_ref, *refs):
     returned, out_ref = refs[:-1], refs[-1]
+    rows = [ref[...] for ref in returned]
+    weights = [jnp.concatenate([high_ref[k], low_ref[k]], axis=0) for k in range(len(rows))]
+    if rows[0].shape[0] % 16 == 0:
+        rows, weights = [jnp.concatenate(rows, axis=0)], [jnp.concatenate(weights, axis=1)]
     total = stream_ref[...]
-    for k, ref in enumerate(returned):
-        rows = ref[...]
-        total = total + jnp.dot(high_ref[k], rows, preferred_element_type=F32)
-        total = total + jnp.dot(low_ref[k], rows, preferred_element_type=F32)
-    out_ref[...] = total.astype(BF16)
+    for weight, block in zip(weights, rows):
+        both = jnp.dot(weight, block, preferred_element_type=F32)
+        total = total + both[: total.shape[0]] + both[total.shape[0] :]
+    out_ref[...] = total.astype(out_ref.dtype)
 
 
 def near(values):
@@ -228,7 +231,7 @@
             functools.partial(attend_kernel, len(pieces)),
             in_specs=[VMEM] * (4 + len(pieces)),
             out_specs=[VMEM] * (1 + n_exp),
-            out_shape=[pltpu.HBM((rows, half), F32)] + [jax.ShapeDtypeStruct((cap, half), BF16)] * n_exp,
+            out_shape=[jax.ShapeDtypeStruct((rows, half), F32)] + [jax.ShapeDtypeStruct((cap, half), BF16)] * n_exp,
             compiler_params=params(),
             cost_estimate=cost(4 * rows * half * n_keys, n_keys * half * 2),
             name="attend",

time: 141 us -> 140 us (level)
  no operation moved by 1% of the time
where the time goes in v4:
time: 140 us; the launch traced here: 138 us
  waiting for transfers between devices  59.6 us (43%)
  starting transfers between devices  52.5 us (38%)
  Pallas kernels  19.1 us (14%)
  local copies, waits for them, and re-layouts  3.73 us (3%)
  other arithmetic  3.1 us (2%)
    ppermute x9, waiting for transfers between devices, over_z(): lax.ppermute(a, 'dev', [(i, (i // 2 ^ k) * 2 + i % 2) for i in range(n_de...  28.5 us
    ppermute x14, starting transfers between devices, over_y(): return lax.ppermute(a, 'dev', [(i, i ^ 1) for i in range(n_dev)])  20.7 us
    ppermute x9, starting transfers between devices, over_z(): lax.ppermute(a, 'dev', [(i, (i // 2 ^ k) * 2 + i % 2) for i in range(n_de...  18.6 us
    ppermute x14, waiting for transfers between devices, over_y(): return lax.ppermute(a, 'dev', [(i, i ^ 1) for i in range(n_dev)])  16.9 us
    ppermute x11, waiting for transfers between devices, over_sec(): return lax.ppermute(a, 'sec', [(0, 1), (1, 0)])  14.2 us
    ppermute x11, starting transfers between devices, over_sec(): return lax.ppermute(a, 'sec', [(0, 1), (1, 0)])  13.1 us
    pallas_call x4, Pallas kernels, hidden_of(): pl.pallas_call(functools.partial(hidden_kernel, width), in_specs=[VMEM] *...  5.45 us
    pallas_call x1, Pallas kernels, body(): pl.pallas_call(stage_kernel, out_shape=[pltpu.VMEM((rows, half), BF16), p...  3.72 us
  transfers between devices with their start and end apart: 35, of which 16 were waited for; matrix products, arithmetic and copies ran while one was open for 5% of the time, Pallas kernels for 12%

profile of v4, /device:TPU:0, one launch (start us, length us, event | category | flops | bytes accessed | tf_op | source)
XLA Modules:
  0.0 138.2 jit_solution(9228023542709491035)
XLA Ops:
  1.0 3.1 %collective-permute-start = (bf16[128,1024]{1,0:T(8,128)(2,1)S(1)}, bf16[128,1024]{1,0:T(8,128)(2,1)S(1)}, u32[]{:S(2)}, u32[]{:S(2)}) collective-permute-start(bf16[128,1024]{1,0:T(8,128)(2,1)S(1)} %pack.1.refs_0_), channel_id=1, source_target_pairs={{0,4},{2,6},{4,0},{6,2},{8,12},{10,14},{12,8},{14,10},{1,5},{3,7},... | collective-permute-start | bytes 786440 | tf_op jit(solution)/shard_map/ppermute | solution.py:177
  4.1 2.6 %collective-permute-start.1 = (bf16[128,1024]{1,0:T(8,128)(2,1)S(1)}, bf16[128,1024]{1,0:T(8,128)(2,1)S(1)}, u32[]{:S(2)}, u32[]{:S(2)}) collective-permute-start(bf16[128,1024]{1,0:T(8,128)(2,1)S(1)} %pack.1.refs_0_), channel_id=1, source_target_pairs={{0,8},{2,10},{4,12},{6,14},{8,0},{10,2},{12,4},{14,6},{1,9},{3,11}... | collective-permute-start | bytes 786440 | tf_op jit(solution)/shard_map/ppermute | solution.py:177
  6.7 1.7 %collective-permute-start.3 = (bf16[128,1024]{1,0:T(8,128)(2,1)S(1)}, bf16[128,1024]{1,0:T(8,128)(2,1)S(1)}, u32[]{:S(2)}, u32[]{:S(2)}) collective-permute-start(bf16[128,1024]{1,0:T(8,128)(2,1)S(1)} %pack.1.refs_0_), channel_id=1, source_target_pairs={{0,2},{2,0},{4,6},{6,4},{8,10},{10,8},{12,14},{14,12},{1,3},{3,1},... | collective-permute-start | bytes 786440 | tf_op jit(solution)/shard_map/ppermute | solution.py:174
  9.4 2.1 %dynamic-slice_bitcast_fusion = bf16[384,1024]{1,0:T(8,128)(2,1)} fusion(bf16[1,384,4096]{2,1,0:T(8,128)(2,1)} %param.19, s32[]{:T(128)S(6)} %select_n.14), kind=kLoop, calls=%fused_computation | loop fusion | bytes 1572868 | tf_op jit(solution)/shard_map/dynamic_slice | solution.py:191
  11.6 1.2 reduce-window.6
  13.2 2.0 %collective-permute-done.refs_1_ = bf16[128,1024]{1,0:T(8,128)(2,1)S(1)} collective-permute-done((bf16[128,1024]{1,0:T(8,128)(2,1)S(1)}, bf16[128,1024]{1,0:T(8,128)(2,1)S(1)}, u32[]{:S(2)}, u32[]{:S(2)}) %collective-permute-start) | collective-permute-done | bytes 262176 | tf_op jit(solution)/shard_map/ppermute | solution.py:177
  15.2 1.7 %collective-permute-start.11 = (bf16[384,1024]{1,0:T(8,128)(2,1)}, bf16[384,1024]{1,0:T(8,128)(2,1)S(1)}, u32[]{:S(2)}, u32[]{:S(2)}) collective-permute-start(bf16[384,1024]{1,0:T(8,128)(2,1)} %dynamic-slice_bitcast_fusion), channel_id=1, source_target_pairs={{0,16},{16,0},{1,17},{17,1},{2,18},{18,2},{3,19},{19,3},{4,20},{20... | collective-permute-start | bytes 2359304 | tf_op jit(solution)/shard_map/ppermute | solution.py:168
  17.8 1.5 %collective-permute-start.4 = (bf16[128,1024]{1,0:T(8,128)(2,1)S(1)}, bf16[128,1024]{1,0:T(8,128)(2,1)S(1)}, u32[]{:S(2)}, u32[]{:S(2)}) collective-permute-start(bf16[128,1024]{1,0:T(8,128)(2,1)S(1)} %collective-permute-done.refs_1_), channel_id=1, source_target_pairs={{0,2},{2,0},{4,6},{6,4},{8,10},{10,8},{12,14},{14,12},{1,3},{3,1},... | collective-permute-start | bytes 786440 | tf_op jit(solution)/shard_map/ppermute | solution.py:174
  19.3 6.1 %collective-permute-done.1.refs_2_ = bf16[128,1024]{1,0:T(8,128)(2,1)S(1)} collective-permute-done((bf16[128,1024]{1,0:T(8,128)(2,1)S(1)}, bf16[128,1024]{1,0:T(8,128)(2,1)S(1)}, u32[]{:S(2)}, u32[]{:S(2)}) %collective-permute-start.1) | collective-permute-done | bytes 262176 | tf_op jit(solution)/shard_map/ppermute | solution.py:177
  25.5 1.5 %collective-permute-start.5 = (bf16[128,1024]{1,0:T(8,128)(2,1)S(1)}, bf16[128,1024]{1,0:T(8,128)(2,1)S(1)}, u32[]{:S(2)}, u32[]{:S(2)}) collective-permute-start(bf16[128,1024]{1,0:T(8,128)(2,1)S(1)} %collective-permute-done.1.refs_2_), channel_id=1, source_target_pairs={{0,2},{2,0},{4,6},{6,4},{8,10},{10,8},{12,14},{14,12},{1,3},{3,1},... | collective-permute-start | bytes 786440 | tf_op jit(solution)/shard_map/ppermute | solution.py:174
  28.4 3.7 %stage.1 = (bf16[128,2048]{1,0:T(8,128)(2,1)S(1)}, bf16[128,2048]{1,0:T(8,128)(2,1)S(1)}, f32[1,4096]{1,0:T(1,128)S(1)}, bf16[4096,768]{1,0:T(8,128)(2,1)S(1)}, bf16[384,2048]{1,0:T(8,128)(2,1)S(1)}) custom-call(s32[1]{0:T(128)} %bitcast.6.sec_ref, bf16[128,2048]{1,0:T(8,128)(2,1)} %q_ref.1, bf16[128,4096]{1,0:T(8,128)(2,1)} %resid_ref.1, ...), custom_call_target="tpu_custom_call" | custom-call | tf_op jit(solution)/shard_map/stage/pallas_call | solution.py:207
  33.1 2.8 %collective-permute-done.6.refs_7_ = bf16[128,1024]{1,0:T(8,128)(2,1)S(1)} collective-permute-done((bf16[128,1024]{1,0:T(8,128)(2,1)S(1)}, bf16[128,1024]{1,0:T(8,128)(2,1)S(1)}, u32[]{:S(2)}, u32[]{:S(2)}) %collective-permute-start.6) | collective-permute-done | bytes 262176 | tf_op jit(solution)/shard_map/ppermute | solution.py:174
  36.0 3.7 %attend.1 = (f32[128,2048]{1,0:T(8,128)S(1)}, bf16[80,2048]{1,0:T(8,128)(2,1)S(1)}, bf16[80,2048]{1,0:T(8,128)(2,1)S(1)}, bf16[80,2048]{1,0:T(8,128)(2,1)S(1)}, bf16[80,2048]{1,0:T(8,128)(2,1)S(1)}) custom-call(bf16[128,2048]{1,0:T(8,128)(2,1)S(1)} %get-tuple-element.45.q_ref, bf16[128,2048]{1,0:T(8,128)(2,1)S(1)} %get-tuple-element.46.resid_ref, ...), custom_call_target="tpu_custom_call" | custom-call | flops 1073741824 | bytes 4194304 | tf_op jit(solution)/shard_map/attend/pallas_call | solution.py:230
  40.5 2.0 %collective-permute-start.14 = (bf16[80,2048]{1,0:T(8,128)(2,1)S(1)}, bf16[80,2048]{1,0:T(8,128)(2,1)S(1)}, u32[]{:S(2)}, u32[]{:S(2)}) collective-permute-start(bf16[80,2048]{1,0:T(8,128)(2,1)S(1)} %get-tuple-element.60), channel_id=1, source_target_pairs={{0,4},{2,6},{4,0},{6,2},{8,12},{10,14},{12,8},{14,10},{1,5},{3,7},... | collective-permute-start | bytes 983048 | tf_op jit(solution)/shard_map/ppermute | solution.py:177
  42.4 1.5 %collective-permute-start.21 = (bf16[80,2048]{1,0:T(8,128)(2,1)S(1)}, bf16[80,2048]{1,0:T(8,128)(2,1)S(1)}, u32[]{:S(2)}, u32[]{:S(2)}) collective-permute-start(bf16[80,2048]{1,0:T(8,128)(2,1)S(1)} %get-tuple-element.64), channel_id=1, source_target_pairs={{0,8},{2,10},{4,12},{6,14},{8,0},{10,2},{12,4},{14,6},{1,9},{3,11}... | collective-permute-start | bytes 983048 | tf_op jit(solution)/shard_map/ppermute | solution.py:177
  43.9 1.5 %collective-permute-start.7 = (bf16[80,2048]{1,0:T(8,128)(2,1)S(1)}, bf16[80,2048]{1,0:T(8,128)(2,1)S(1)}, u32[]{:S(2)}, u32[]{:S(2)}) collective-permute-start(bf16[80,2048]{1,0:T(8,128)(2,1)S(1)} %get-tuple-element.53.own_ref), channel_id=1, source_target_pairs={{0,2},{2,0},{4,6},{6,4},{8,10},{10,8},{12,14},{14,12},{1,3},{3,1},... | collective-permute-start | bytes 983048 | tf_op jit(solution)/shard_map/ppermute | solution.py:174
  45.4 4.4 %collective-permute-done.8.x_ref = bf16[80,2048]{1,0:T(8,128)(2,1)S(1)} collective-permute-done((bf16[80,2048]{1,0:T(8,128)(2,1)S(1)}, bf16[80,2048]{1,0:T(8,128)(2,1)S(1)}, u32[]{:S(2)}, u32[]{:S(2)}) %collective-permute-start.8) | collective-permute-done | bytes 327712 | tf_op jit(solution)/shard_map/ppermute | solution.py:168
  49.8 1.5 %collective-permute-start.9 = (bf16[80,2048]{1,0:T(8,128)(2,1)S(1)}, bf16[80,2048]{1,0:T(8,128)(2,1)S(1)}, u32[]{:S(2)}, u32[]{:S(2)}) collective-permute-start(bf16[80,2048]{1,0:T(8,128)(2,1)S(1)} %collective-permute-done.8.x_ref), channel_id=1, source_target_pairs={{0,2},{2,0},{4,6},{6,4},{8,10},{10,8},{12,14},{14,12},{1,3},{3,1},... | collective-permute-start | bytes 983048 | tf_op jit(solution)/shard_map/ppermute | solution.py:174
  51.4 6.0 %collective-permute-done.14.own_ref = bf16[80,2048]{1,0:T(8,128)(2,1)S(1)} collective-permute-done((bf16[80,2048]{1,0:T(8,128)(2,1)S(1)}, bf16[80,2048]{1,0:T(8,128)(2,1)S(1)}, u32[]{:S(2)}, u32[]{:S(2)}) %collective-permute-start.14) | collective-permute-done | bytes 327712 | tf_op jit(solution)/shard_map/ppermute | solution.py:177
  57.4 1.1 collective-permute-start.16
  58.5 1.4 %collective-permute-done.21.own_ref = bf16[80,2048]{1,0:T(8,128)(2,1)S(1)} collective-permute-done((bf16[80,2048]{1,0:T(8,128)(2,1)S(1)}, bf16[80,2048]{1,0:T(8,128)(2,1)S(1)}, u32[]{:S(2)}, u32[]{:S(2)}) %collective-permute-start.21) | collective-permute-done | bytes 327712 | tf_op jit(solution)/shard_map/ppermute | solution.py:177
  59.9 1.5 %collective-permute-start.22 = (bf16[80,2048]{1,0:T(8,128)(2,1)S(1)}, bf16[80,2048]{1,0:T(8,128)(2,1)S(1)}, u32[]{:S(2)}, u32[]{:S(2)}) collective-permute-start(bf16[80,2048]{1,0:T(8,128)(2,1)S(1)} %collective-permute-done.21.own_ref), channel_id=1, source_target_pairs={{0,2},{2,0},{4,6},{6,4},{8,10},{10,8},{12,14},{14,12},{1,3},{3,1},... | collective-permute-start | bytes 983048 | tf_op jit(solution)/shard_map/ppermute | solution.py:174
  61.4 2.5 %collective-permute-start.28 = (bf16[80,2048]{1,0:T(8,128)(2,1)S(1)}, bf16[80,2048]{1,0:T(8,128)(2,1)S(1)}, u32[]{:S(2)}, u32[]{:S(2)}) collective-permute-start(bf16[80,2048]{1,0:T(8,128)(2,1)S(1)} %get-tuple-element.70), channel_id=1, source_target_pairs={{0,12},{2,14},{4,8},{6,10},{8,4},{10,6},{12,0},{14,2},{1,13},{3,15... | collective-permute-start | bytes 983048 | tf_op jit(solution)/shard_map/ppermute | solution.py:177
  64.4 1.3 hidden.4.own_act
  66.6 1.6 %collective-permute-start.17 = (bf16[80,2048]{1,0:T(8,128)(2,1)S(1)}, bf16[80,2048]{1,0:T(8,128)(2,1)S(1)}, u32[]{:S(2)}, u32[]{:S(2)}) collective-permute-start(bf16[80,2048]{1,0:T(8,128)(2,1)S(1)} %collective-permute-done.16.x_ref), channel_id=1, source_target_pairs={{0,2},{2,0},{4,6},{6,4},{8,10},{10,8},{12,14},{14,12},{1,3},{3,1},... | collective-permute-start | bytes 983048 | tf_op jit(solution)/shard_map/ppermute | solution.py:174
  68.2 1.3 collective-permute-done.22.y_ref
  69.4 1.6 %collective-permute-start.23 = (bf16[80,2048]{1,0:T(8,128)(2,1)S(1)}, bf16[80,2048]{1,0:T(8,128)(2,1)S(1)}, u32[]{:S(2)}, u32[]{:S(2)}) collective-permute-start(bf16[80,2048]{1,0:T(8,128)(2,1)S(1)} %collective-permute-done.21.own_ref), channel_id=1, source_target_pairs={{0,16},{16,0},{1,17},{17,1},{2,18},{18,2},{3,19},{19,3},{4,20},{20... | collective-permute-start | bytes 983048 | tf_op jit(solution)/shard_map/ppermute | solution.py:168
  71.1 1.5 %collective-permute-start.29 = (bf16[80,2048]{1,0:T(8,128)(2,1)S(1)}, bf16[80,2048]{1,0:T(8,128)(2,1)S(1)}, u32[]{:S(2)}, u32[]{:S(2)}) collective-permute-start(bf16[80,2048]{1,0:T(8,128)(2,1)S(1)} %collective-permute-done.28.own_ref), channel_id=1, source_target_pairs={{0,2},{2,0},{4,6},{6,4},{8,10},{10,8},{12,14},{14,12},{1,3},{3,1},... | collective-permute-start | bytes 983048 | tf_op jit(solution)/shard_map/ppermute | solution.py:174
  72.6 1.4 collective-permute-start.24
  74.9 1.6 %collective-permute-done.15.y_ref = bf16[80,2048]{1,0:T(8,128)(2,1)S(1)} collective-permute-done((bf16[80,2048]{1,0:T(8,128)(2,1)S(1)}, bf16[80,2048]{1,0:T(8,128)(2,1)S(1)}, u32[]{:S(2)}, u32[]{:S(2)}) %collective-permute-start.15) | collective-permute-done | bytes 327712 | tf_op jit(solution)/shard_map/ppermute | solution.py:174
  76.5 2.5 %collective-permute-start.13 = (bf16[80,2048]{1,0:T(8,128)(2,1)S(1)}, bf16[80,2048]{1,0:T(8,128)(2,1)S(1)}, u32[]{:S(2)}, u32[]{:S(2)}) collective-permute-start(bf16[80,2048]{1,0:T(8,128)(2,1)S(1)} %get-tuple-element.59), channel_id=1, source_target_pairs={{0,2},{2,0},{4,6},{6,4},{8,10},{10,8},{12,14},{14,12},{1,3},{3,1},... | collective-permute-start | bytes 983048 | tf_op jit(solution)/shard_map/ppermute | solution.py:174
  79.0 4.5 %collective-permute-done.17.both_ref = bf16[80,2048]{1,0:T(8,128)(2,1)S(1)} collective-permute-done((bf16[80,2048]{1,0:T(8,128)(2,1)S(1)}, bf16[80,2048]{1,0:T(8,128)(2,1)S(1)}, u32[]{:S(2)}, u32[]{:S(2)}) %collective-permute-start.17) | collective-permute-done | bytes 327712 | tf_op jit(solution)/shard_map/ppermute | solution.py:174
  83.5 1.3 hidden.5.own_act
  84.8 1.7 %collective-permute-start.18 = (bf16[160,384]{1,0:T(8,128)(2,1)S(1)}, bf16[160,384]{1,0:T(8,128)(2,1)S(1)}, u32[]{:S(2)}, u32[]{:S(2)}) collective-permute-start(bf16[160,384]{1,0:T(8,128)(2,1)S(1)} %hidden.5.own_act), channel_id=1, source_target_pairs={{0,16},{16,0},{1,17},{17,1},{2,18},{18,2},{3,19},{19,3},{4,20},{20... | collective-permute-start | bytes 368648 | tf_op jit(solution)/shard_map/ppermute | solution.py:168
  86.9 3.6 %collective-permute-done.29.y_ref = bf16[80,2048]{1,0:T(8,128)(2,1)S(1)} collective-permute-done((bf16[80,2048]{1,0:T(8,128)(2,1)S(1)}, bf16[80,2048]{1,0:T(8,128)(2,1)S(1)}, u32[]{:S(2)}, u32[]{:S(2)}) %collective-permute-start.29) | collective-permute-done | bytes 327712 | tf_op jit(solution)/shard_map/ppermute | solution.py:174
  90.5 1.6 %collective-permute-start.31 = (bf16[80,2048]{1,0:T(8,128)(2,1)S(1)}, bf16[80,2048]{1,0:T(8,128)(2,1)S(1)}, u32[]{:S(2)}, u32[]{:S(2)}) collective-permute-start(bf16[80,2048]{1,0:T(8,128)(2,1)S(1)} %collective-permute-done.29.y_ref), channel_id=1, source_target_pairs={{0,16},{16,0},{1,17},{17,1},{2,18},{18,2},{3,19},{19,3},{4,20},{20... | collective-permute-start | bytes 983048 | tf_op jit(solution)/shard_map/ppermute | solution.py:168
  92.1 1.3 hidden.6.own_act
  94.9 2.6 %collective-permute-start.19 = (bf16[80,2048]{1,0:T(8,128)(2,1)S(1)}, bf16[80,2048]{1,0:T(8,128)(2,1)S(1)}, u32[]{:S(2)}, u32[]{:S(2)}) collective-permute-start(bf16[80,2048]{1,0:T(8,128)(2,1)S(1)} %get-tuple-element.63), channel_id=1, source_target_pairs={{0,2},{2,0},{4,6},{6,4},{8,10},{10,8},{12,14},{14,12},{1,3},{3,1},... | collective-permute-start | bytes 983048 | tf_op jit(solution)/shard_map/ppermute | solution.py:174
  97.5 6.4 %collective-permute-done.25.other_act = bf16[160,384]{1,0:T(8,128)(2,1)S(1)} collective-permute-done((bf16[160,384]{1,0:T(8,128)(2,1)S(1)}, bf16[160,384]{1,0:T(8,128)(2,1)S(1)}, u32[]{:S(2)}, u32[]{:S(2)}) %collective-permute-start.25) | collective-permute-done | bytes 122912 | tf_op jit(solution)/shard_map/ppermute | solution.py:168
  105.3 1.5 %hidden.7.own_act = bf16[160,384]{1,0:T(8,128)(2,1)S(1)} custom-call(bf16[80,2048]{1,0:T(8,128)(2,1)S(1)} %collective-permute-done.28.own_ref, bf16[80,2048]{1,0:T(8,128)(2,1)S(1)} %collective-permute-done.29.y_ref, bf16[80,2048]{1,0:T(8,128)(2,1)S(1)} %collective-permute-done.30.x_ref, bf16[80,2048]{1,0:T(8,128)(2,1)S(1)} %collective-permute-done.31.both_ref, ...), custom_call_target="tpu_custom_call" | custom-call | flops 1006632960 | bytes 6291456 | tf_op jit(solution)/shard_map/hidden/pallas_call | solution.py:258
  106.9 1.8 %collective-permute-start.32 = (bf16[160,384]{1,0:T(8,128)(2,1)S(1)}, bf16[160,384]{1,0:T(8,128)(2,1)S(1)}, u32[]{:S(2)}, u32[]{:S(2)}) collective-permute-start(bf16[160,384]{1,0:T(8,128)(2,1)S(1)} %hidden.7.own_act), channel_id=1, source_target_pairs={{0,16},{16,0},{1,17},{17,1},{2,18},{18,2},{3,19},{19,3},{4,20},{20... | collective-permute-start | bytes 368648 | tf_op jit(solution)/shard_map/ppermute | solution.py:168
  108.7 3.1 %collective-permute-done.32.other_act = bf16[160,384]{1,0:T(8,128)(2,1)S(1)} collective-permute-done((bf16[160,384]{1,0:T(8,128)(2,1)S(1)}, bf16[160,384]{1,0:T(8,128)(2,1)S(1)}, u32[]{:S(2)}, u32[]{:S(2)}) %collective-permute-start.32) | collective-permute-done | bytes 122912 | tf_op jit(solution)/shard_map/ppermute | solution.py:168
  112.7 1.7 %collective-permute-start.33 = (bf16[80,2048]{1,0:T(8,128)(2,1)S(1)}, bf16[80,2048]{1,0:T(8,128)(2,1)S(1)}, u32[]{:S(2)}, u32[]{:S(2)}) collective-permute-start(bf16[80,2048]{1,0:T(8,128)(2,1)S(1)} %get-tuple-element.74), channel_id=1, source_target_pairs={{0,2},{2,0},{4,6},{6,4},{8,10},{10,8},{12,14},{14,12},{1,3},{3,1},... | collective-permute-start | bytes 983048 | tf_op jit(solution)/shard_map/ppermute | solution.py:174
  115.6 2.1 %collective-permute-start.20 = (bf16[80,2048]{1,0:T(8,128)(2,1)S(1)}, bf16[80,2048]{1,0:T(8,128)(2,1)S(1)}, u32[]{:S(2)}, u32[]{:S(2)}) collective-permute-start(bf16[80,2048]{1,0:T(8,128)(2,1)S(1)} %add_convert_fusion.2), channel_id=1, source_target_pairs={{0,4},{2,6},{4,0},{6,2},{8,12},{10,14},{12,8},{14,10},{1,5},{3,7},... | collective-permute-start | bytes 983048 | tf_op jit(solution)/shard_map/ppermute | solution.py:177
  117.7 2.1 %collective-permute-done.33 = bf16[80,2048]{1,0:T(8,128)(2,1)S(1)} collective-permute-done((bf16[80,2048]{1,0:T(8,128)(2,1)S(1)}, bf16[80,2048]{1,0:T(8,128)(2,1)S(1)}, u32[]{:S(2)}, u32[]{:S(2)}) %collective-permute-start.33) | collective-permute-done | bytes 327712 | tf_op jit(solution)/shard_map/ppermute | solution.py:174
  119.9 3.8 %collective-permute-start.34 = (bf16[80,2048]{1,0:T(8,128)(2,1)S(1)}, bf16[80,2048]{1,0:T(8,128)(2,1)S(1)}, u32[]{:S(2)}, u32[]{:S(2)}) collective-permute-start(bf16[80,2048]{1,0:T(8,128)(2,1)S(1)} %add_convert_fusion), channel_id=1, source_target_pairs={{0,12},{2,14},{4,8},{6,10},{8,4},{10,6},{12,0},{14,2},{1,13},{3,15... | collective-permute-start | bytes 983048 | tf_op jit(solution)/shard_map/ppermute | solution.py:177
  123.7 12.9 %collective-permute-done.27.refs_2_ = bf16[80,2048]{1,0:T(8,128)(2,1)S(1)} collective-permute-done((bf16[80,2048]{1,0:T(8,128)(2,1)S(1)}, bf16[80,2048]{1,0:T(8,128)(2,1)S(1)}, u32[]{:S(2)}, u32[]{:S(2)}) %collective-permute-start.27) | collective-permute-done | bytes 327712 | tf_op jit(solution)/shard_map/ppermute | solution.py:177
  136.7 1.5 %combine.1 = bf16[128,2048]{1,0:T(8,128)(2,1)} custom-call(f32[128,2048]{1,0:T(8,128)S(1)} %get-tuple-element.50.stream_ref, bf16[4,128,80]{2,1,0:T(8,128)(2,1)S(1)} %get-tuple-element.51.high_ref, bf16[4,128,80]{2,1,0:T(8,128)(2,1)S(1)} %get-tuple-element.52.low_ref, bf16[80,2048]{1,0:T(8,128)(2,1)S(1)} %add_convert_fusion.3.refs_0_, ...), custom_call_target="tpu_custom_call" | custom-call | flops 335544320 | bytes 2883584 | tf_op jit(solution)/shard_map/combine/pallas_call | solution.py:297
  (57 shorter events, 14.4 us)
Async XLA Ops:
  1.0 14.2 %collective-permute-start = (bf16[128,1024]{1,0:T(8,128)(2,1)S(1)}, bf16[128,1024]{1,0:T(8,128)(2,1)S(1)}, u32[]{:S(2)}, u32[]{:S(2)}) collective-permute-start(bf16[128,1024]{1,0:T(8,128)(2,1)S(1)} %pack.1.refs_0_), channel_id=1, source_target_pairs={{0,4},{2,6},{4,0},{6,2},{8,12},{10,14},{12,8},{14,10},{1,5},{3,7},... | collective-permute-start | bytes 786440 | tf_op jit(solution)/shard_map/ppermute | solution.py:177
  4.1 21.4 %collective-permute-start.1 = (bf16[128,1024]{1,0:T(8,128)(2,1)S(1)}, bf16[128,1024]{1,0:T(8,128)(2,1)S(1)}, u32[]{:S(2)}, u32[]{:S(2)}) collective-permute-start(bf16[128,1024]{1,0:T(8,128)(2,1)S(1)} %pack.1.refs_0_), channel_id=1, source_target_pairs={{0,8},{2,10},{4,12},{6,14},{8,0},{10,2},{12,4},{14,6},{1,9},{3,11}... | collective-permute-start | bytes 786440 | tf_op jit(solution)/shard_map/ppermute | solution.py:177
  6.7 20.3 %collective-permute-start.2 = (bf16[128,1024]{1,0:T(8,128)(2,1)S(1)}, bf16[128,1024]{1,0:T(8,128)(2,1)S(1)}, u32[]{:S(2)}, u32[]{:S(2)}) collective-permute-start(bf16[128,1024]{1,0:T(8,128)(2,1)S(1)} %pack.1.refs_0_), channel_id=1, source_target_pairs={{0,12},{2,14},{4,8},{6,10},{8,4},{10,6},{12,0},{14,2},{1,13},{3,15... | collective-permute-start | bytes 786440 | tf_op jit(solution)/shard_map/ppermute | solution.py:177
  6.7 25.5 %collective-permute-start.3 = (bf16[128,1024]{1,0:T(8,128)(2,1)S(1)}, bf16[128,1024]{1,0:T(8,128)(2,1)S(1)}, u32[]{:S(2)}, u32[]{:S(2)}) collective-permute-start(bf16[128,1024]{1,0:T(8,128)(2,1)S(1)} %pack.1.refs_0_), channel_id=1, source_target_pairs={{0,2},{2,0},{4,6},{6,4},{8,10},{10,8},{12,14},{14,12},{1,3},{3,1},... | collective-permute-start | bytes 786440 | tf_op jit(solution)/shard_map/ppermute | solution.py:174
  15.2 24.4 %collective-permute-start.11 = (bf16[384,1024]{1,0:T(8,128)(2,1)}, bf16[384,1024]{1,0:T(8,128)(2,1)S(1)}, u32[]{:S(2)}, u32[]{:S(2)}) collective-permute-start(bf16[384,1024]{1,0:T(8,128)(2,1)} %dynamic-slice_bitcast_fusion), channel_id=1, source_target_pairs={{0,16},{16,0},{1,17},{17,1},{2,18},{18,2},{3,19},{19,3},{4,20},{20... | collective-permute-start | bytes 2359304 | tf_op jit(solution)/shard_map/ppermute | solution.py:168
  17.8 14.3 %collective-permute-start.4 = (bf16[128,1024]{1,0:T(8,128)(2,1)S(1)}, bf16[128,1024]{1,0:T(8,128)(2,1)S(1)}, u32[]{:S(2)}, u32[]{:S(2)}) collective-permute-start(bf16[128,1024]{1,0:T(8,128)(2,1)S(1)} %collective-permute-done.refs_1_), channel_id=1, source_target_pairs={{0,2},{2,0},{4,6},{6,4},{8,10},{10,8},{12,14},{14,12},{1,3},{3,1},... | collective-permute-start | bytes 786440 | tf_op jit(solution)/shard_map/ppermute | solution.py:174
  25.5 7.7 %collective-permute-start.5 = (bf16[128,1024]{1,0:T(8,128)(2,1)S(1)}, bf16[128,1024]{1,0:T(8,128)(2,1)S(1)}, u32[]{:S(2)}, u32[]{:S(2)}) collective-permute-start(bf16[128,1024]{1,0:T(8,128)(2,1)S(1)} %collective-permute-done.1.refs_2_), channel_id=1, source_target_pairs={{0,2},{2,0},{4,6},{6,4},{8,10},{10,8},{12,14},{14,12},{1,3},{3,1},... | collective-permute-start | bytes 786440 | tf_op jit(solution)/shard_map/ppermute | solution.py:174
  27.0 9.0 %collective-permute-start.6 = (bf16[128,1024]{1,0:T(8,128)(2,1)S(1)}, bf16[128,1024]{1,0:T(8,128)(2,1)S(1)}, u32[]{:S(2)}, u32[]{:S(2)}) collective-permute-start(bf16[128,1024]{1,0:T(8,128)(2,1)S(1)} %collective-permute-done.2.refs_3_), channel_id=1, source_target_pairs={{0,2},{2,0},{4,6},{6,4},{8,10},{10,8},{12,14},{14,12},{1,3},{3,1},... | collective-permute-start | bytes 786440 | tf_op jit(solution)/shard_map/ppermute | solution.py:174
  39.6 17.7 %collective-permute-start.12 = (bf16[384,1024]{1,0:T(8,128)(2,1)S(1)}, bf16[384,1024]{1,0:T(8,128)(2,1)S(1)}, u32[]{:S(2)}, u32[]{:S(2)}) collective-permute-start(bf16[384,1024]{1,0:T(8,128)(2,1)S(1)} %collective-permute-done.11.near_ref), channel_id=1, source_target_pairs={{0,1},{1,0},{2,3},{3,2},{4,5},{5,4},{6,7},{7,6},{8,9},{9,8},{10,11... | collective-permute-start | bytes 2359304 | tf_op jit(solution)/shard_map/ppermute | solution.py:171
  39.7 10.1 %collective-permute-start.8 = (bf16[80,2048]{1,0:T(8,128)(2,1)S(1)}, bf16[80,2048]{1,0:T(8,128)(2,1)S(1)}, u32[]{:S(2)}, u32[]{:S(2)}) collective-permute-start(bf16[80,2048]{1,0:T(8,128)(2,1)S(1)} %get-tuple-element.53.own_ref), channel_id=1, source_target_pairs={{0,16},{16,0},{1,17},{17,1},{2,18},{18,2},{3,19},{19,3},{4,20},{20... | collective-permute-start | bytes 983048 | tf_op jit(solution)/shard_map/ppermute | solution.py:168
  40.5 16.9 %collective-permute-start.14 = (bf16[80,2048]{1,0:T(8,128)(2,1)S(1)}, bf16[80,2048]{1,0:T(8,128)(2,1)S(1)}, u32[]{:S(2)}, u32[]{:S(2)}) collective-permute-start(bf16[80,2048]{1,0:T(8,128)(2,1)S(1)} %get-tuple-element.60), channel_id=1, source_target_pairs={{0,4},{2,6},{4,0},{6,2},{8,12},{10,14},{12,8},{14,10},{1,5},{3,7},... | collective-permute-start | bytes 983048 | tf_op jit(solution)/shard_map/ppermute | solution.py:177
  42.4 17.5 %collective-permute-start.21 = (bf16[80,2048]{1,0:T(8,128)(2,1)S(1)}, bf16[80,2048]{1,0:T(8,128)(2,1)S(1)}, u32[]{:S(2)}, u32[]{:S(2)}) collective-permute-start(bf16[80,2048]{1,0:T(8,128)(2,1)S(1)} %get-tuple-element.64), channel_id=1, source_target_pairs={{0,8},{2,10},{4,12},{6,14},{8,0},{10,2},{12,4},{14,6},{1,9},{3,11}... | collective-permute-start | bytes 983048 | tf_op jit(solution)/shard_map/ppermute | solution.py:177
  43.9 20.0 %collective-permute-start.7 = (bf16[80,2048]{1,0:T(8,128)(2,1)S(1)}, bf16[80,2048]{1,0:T(8,128)(2,1)S(1)}, u32[]{:S(2)}, u32[]{:S(2)}) collective-permute-start(bf16[80,2048]{1,0:T(8,128)(2,1)S(1)} %get-tuple-element.53.own_ref), channel_id=1, source_target_pairs={{0,2},{2,0},{4,6},{6,4},{8,10},{10,8},{12,14},{14,12},{1,3},{3,1},... | collective-permute-start | bytes 983048 | tf_op jit(solution)/shard_map/ppermute | solution.py:174
  49.8 14.6 %collective-permute-start.9 = (bf16[80,2048]{1,0:T(8,128)(2,1)S(1)}, bf16[80,2048]{1,0:T(8,128)(2,1)S(1)}, u32[]{:S(2)}, u32[]{:S(2)}) collective-permute-start(bf16[80,2048]{1,0:T(8,128)(2,1)S(1)} %collective-permute-done.8.x_ref), channel_id=1, source_target_pairs={{0,2},{2,0},{4,6},{6,4},{8,10},{10,8},{12,14},{14,12},{1,3},{3,1},... | collective-permute-start | bytes 983048 | tf_op jit(solution)/shard_map/ppermute | solution.py:174
  57.4 9.2 %collective-permute-start.16 = (bf16[80,2048]{1,0:T(8,128)(2,1)S(1)}, bf16[80,2048]{1,0:T(8,128)(2,1)S(1)}, u32[]{:S(2)}, u32[]{:S(2)}) collective-permute-start(bf16[80,2048]{1,0:T(8,128)(2,1)S(1)} %collective-permute-done.14.own_ref), channel_id=1, source_target_pairs={{0,16},{16,0},{1,17},{17,1},{2,18},{18,2},{3,19},{19,3},{4,20},{20... | collective-permute-start | bytes 983048 | tf_op jit(solution)/shard_map/ppermute | solution.py:168
  59.9 9.6 %collective-permute-start.22 = (bf16[80,2048]{1,0:T(8,128)(2,1)S(1)}, bf16[80,2048]{1,0:T(8,128)(2,1)S(1)}, u32[]{:S(2)}, u32[]{:S(2)}) collective-permute-start(bf16[80,2048]{1,0:T(8,128)(2,1)S(1)} %collective-permute-done.21.own_ref), channel_id=1, source_target_pairs={{0,2},{2,0},{4,6},{6,4},{8,10},{10,8},{12,14},{14,12},{1,3},{3,1},... | collective-permute-start | bytes 983048 | tf_op jit(solution)/shard_map/ppermute | solution.py:174
  61.4 9.7 %collective-permute-start.28 = (bf16[80,2048]{1,0:T(8,128)(2,1)S(1)}, bf16[80,2048]{1,0:T(8,128)(2,1)S(1)}, u32[]{:S(2)}, u32[]{:S(2)}) collective-permute-start(bf16[80,2048]{1,0:T(8,128)(2,1)S(1)} %get-tuple-element.70), channel_id=1, source_target_pairs={{0,12},{2,14},{4,8},{6,10},{8,4},{10,6},{12,0},{14,2},{1,13},{3,15... | collective-permute-start | bytes 983048 | tf_op jit(solution)/shard_map/ppermute | solution.py:177
  63.9 12.6 %collective-permute-start.15 = (bf16[80,2048]{1,0:T(8,128)(2,1)S(1)}, bf16[80,2048]{1,0:T(8,128)(2,1)S(1)}, u32[]{:S(2)}, u32[]{:S(2)}) collective-permute-start(bf16[80,2048]{1,0:T(8,128)(2,1)S(1)} %collective-permute-done.14.own_ref), channel_id=1, source_target_pairs={{0,2},{2,0},{4,6},{6,4},{8,10},{10,8},{12,14},{14,12},{1,3},{3,1},... | collective-permute-start | bytes 983048 | tf_op jit(solution)/shard_map/ppermute | solution.py:174
  65.7 6.9 %collective-permute-start.10 = (bf16[160,384]{1,0:T(8,128)(2,1)S(1)}, bf16[160,384]{1,0:T(8,128)(2,1)S(1)}, u32[]{:S(2)}, u32[]{:S(2)}) collective-permute-start(bf16[160,384]{1,0:T(8,128)(2,1)S(1)} %hidden.4.own_act), channel_id=1, source_target_pairs={{0,16},{16,0},{1,17},{17,1},{2,18},{18,2},{3,19},{19,3},{4,20},{20... | collective-permute-start | bytes 368648 | tf_op jit(solution)/shard_map/ppermute | solution.py:168
  66.6 16.9 %collective-permute-start.17 = (bf16[80,2048]{1,0:T(8,128)(2,1)S(1)}, bf16[80,2048]{1,0:T(8,128)(2,1)S(1)}, u32[]{:S(2)}, u32[]{:S(2)}) collective-permute-start(bf16[80,2048]{1,0:T(8,128)(2,1)S(1)} %collective-permute-done.16.x_ref), channel_id=1, source_target_pairs={{0,2},{2,0},{4,6},{6,4},{8,10},{10,8},{12,14},{14,12},{1,3},{3,1},... | collective-permute-start | bytes 983048 | tf_op jit(solution)/shard_map/ppermute | solution.py:174
  69.4 17.1 %collective-permute-start.23 = (bf16[80,2048]{1,0:T(8,128)(2,1)S(1)}, bf16[80,2048]{1,0:T(8,128)(2,1)S(1)}, u32[]{:S(2)}, u32[]{:S(2)}) collective-permute-start(bf16[80,2048]{1,0:T(8,128)(2,1)S(1)} %collective-permute-done.21.own_ref), channel_id=1, source_target_pairs={{0,16},{16,0},{1,17},{17,1},{2,18},{18,2},{3,19},{19,3},{4,20},{20... | collective-permute-start | bytes 983048 | tf_op jit(solution)/shard_map/ppermute | solution.py:168
  71.1 19.4 %collective-permute-start.29 = (bf16[80,2048]{1,0:T(8,128)(2,1)S(1)}, bf16[80,2048]{1,0:T(8,128)(2,1)S(1)}, u32[]{:S(2)}, u32[]{:S(2)}) collective-permute-start(bf16[80,2048]{1,0:T(8,128)(2,1)S(1)} %collective-permute-done.28.own_ref), channel_id=1, source_target_pairs={{0,2},{2,0},{4,6},{6,4},{8,10},{10,8},{12,14},{14,12},{1,3},{3,1},... | collective-permute-start | bytes 983048 | tf_op jit(solution)/shard_map/ppermute | solution.py:174
  72.6 19.5 %collective-permute-start.24 = (bf16[80,2048]{1,0:T(8,128)(2,1)S(1)}, bf16[80,2048]{1,0:T(8,128)(2,1)S(1)}, u32[]{:S(2)}, u32[]{:S(2)}) collective-permute-start(bf16[80,2048]{1,0:T(8,128)(2,1)S(1)} %collective-permute-done.22.y_ref), channel_id=1, source_target_pairs={{0,16},{16,0},{1,17},{17,1},{2,18},{18,2},{3,19},{19,3},{4,20},{20... | collective-permute-start | bytes 983048 | tf_op jit(solution)/shard_map/ppermute | solution.py:168
  76.5 20.9 %collective-permute-start.13 = (bf16[80,2048]{1,0:T(8,128)(2,1)S(1)}, bf16[80,2048]{1,0:T(8,128)(2,1)S(1)}, u32[]{:S(2)}, u32[]{:S(2)}) collective-permute-start(bf16[80,2048]{1,0:T(8,128)(2,1)S(1)} %get-tuple-element.59), channel_id=1, source_target_pairs={{0,2},{2,0},{4,6},{6,4},{8,10},{10,8},{12,14},{14,12},{1,3},{3,1},... | collective-permute-start | bytes 983048 | tf_op jit(solution)/shard_map/ppermute | solution.py:174
  84.8 9.1 %collective-permute-start.18 = (bf16[160,384]{1,0:T(8,128)(2,1)S(1)}, bf16[160,384]{1,0:T(8,128)(2,1)S(1)}, u32[]{:S(2)}, u32[]{:S(2)}) collective-permute-start(bf16[160,384]{1,0:T(8,128)(2,1)S(1)} %hidden.5.own_act), channel_id=1, source_target_pairs={{0,16},{16,0},{1,17},{17,1},{2,18},{18,2},{3,19},{19,3},{4,20},{20... | collective-permute-start | bytes 368648 | tf_op jit(solution)/shard_map/ppermute | solution.py:168
  86.5 18.8 %collective-permute-start.30 = (bf16[80,2048]{1,0:T(8,128)(2,1)S(1)}, bf16[80,2048]{1,0:T(8,128)(2,1)S(1)}, u32[]{:S(2)}, u32[]{:S(2)}) collective-permute-start(bf16[80,2048]{1,0:T(8,128)(2,1)S(1)} %collective-permute-done.28.own_ref), channel_id=1, source_target_pairs={{0,16},{16,0},{1,17},{17,1},{2,18},{18,2},{3,19},{19,3},{4,20},{20... | collective-permute-start | bytes 983048 | tf_op jit(solution)/shard_map/ppermute | solution.py:168
  90.5 14.8 %collective-permute-start.31 = (bf16[80,2048]{1,0:T(8,128)(2,1)S(1)}, bf16[80,2048]{1,0:T(8,128)(2,1)S(1)}, u32[]{:S(2)}, u32[]{:S(2)}) collective-permute-start(bf16[80,2048]{1,0:T(8,128)(2,1)S(1)} %collective-permute-done.29.y_ref), channel_id=1, source_target_pairs={{0,16},{16,0},{1,17},{17,1},{2,18},{18,2},{3,19},{19,3},{4,20},{20... | collective-permute-start | bytes 983048 | tf_op jit(solution)/shard_map/ppermute | solution.py:168
  93.5 10.5 %collective-permute-start.25 = (bf16[160,384]{1,0:T(8,128)(2,1)S(1)}, bf16[160,384]{1,0:T(8,128)(2,1)S(1)}, u32[]{:S(2)}, u32[]{:S(2)}) collective-permute-start(bf16[160,384]{1,0:T(8,128)(2,1)S(1)} %hidden.6.own_act), channel_id=1, source_target_pairs={{0,16},{16,0},{1,17},{17,1},{2,18},{18,2},{3,19},{19,3},{4,20},{20... | collective-permute-start | bytes 368648 | tf_op jit(solution)/shard_map/ppermute | solution.py:168
  94.9 13.8 %collective-permute-start.19 = (bf16[80,2048]{1,0:T(8,128)(2,1)S(1)}, bf16[80,2048]{1,0:T(8,128)(2,1)S(1)}, u32[]{:S(2)}, u32[]{:S(2)}) collective-permute-start(bf16[80,2048]{1,0:T(8,128)(2,1)S(1)} %get-tuple-element.63), channel_id=1, source_target_pairs={{0,2},{2,0},{4,6},{6,4},{8,10},{10,8},{12,14},{14,12},{1,3},{3,1},... | collective-permute-start | bytes 983048 | tf_op jit(solution)/shard_map/ppermute | solution.py:174
  104.9 9.6 %collective-permute-start.26 = (bf16[80,2048]{1,0:T(8,128)(2,1)S(1)}, bf16[80,2048]{1,0:T(8,128)(2,1)S(1)}, u32[]{:S(2)}, u32[]{:S(2)}) collective-permute-start(bf16[80,2048]{1,0:T(8,128)(2,1)S(1)} %get-tuple-element.68), channel_id=1, source_target_pairs={{0,2},{2,0},{4,6},{6,4},{8,10},{10,8},{12,14},{14,12},{1,3},{3,1},... | collective-permute-start | bytes 983048 | tf_op jit(solution)/shard_map/ppermute | solution.py:174
  106.9 4.9 %collective-permute-start.32 = (bf16[160,384]{1,0:T(8,128)(2,1)S(1)}, bf16[160,384]{1,0:T(8,128)(2,1)S(1)}, u32[]{:S(2)}, u32[]{:S(2)}) collective-permute-start(bf16[160,384]{1,0:T(8,128)(2,1)S(1)} %hidden.7.own_act), channel_id=1, source_target_pairs={{0,16},{16,0},{1,17},{17,1},{2,18},{18,2},{3,19},{19,3},{4,20},{20... | collective-permute-start | bytes 368648 | tf_op jit(solution)/shard_map/ppermute | solution.py:168
  112.7 7.1 %collective-permute-start.33 = (bf16[80,2048]{1,0:T(8,128)(2,1)S(1)}, bf16[80,2048]{1,0:T(8,128)(2,1)S(1)}, u32[]{:S(2)}, u32[]{:S(2)}) collective-permute-start(bf16[80,2048]{1,0:T(8,128)(2,1)S(1)} %get-tuple-element.74), channel_id=1, source_target_pairs={{0,2},{2,0},{4,6},{6,4},{8,10},{10,8},{12,14},{14,12},{1,3},{3,1},... | collective-permute-start | bytes 983048 | tf_op jit(solution)/shard_map/ppermute | solution.py:174
  114.5 22.1 %collective-permute-start.27 = (bf16[80,2048]{1,0:T(8,128)(2,1)S(1)}, bf16[80,2048]{1,0:T(8,128)(2,1)S(1)}, u32[]{:S(2)}, u32[]{:S(2)}) collective-permute-start(bf16[80,2048]{1,0:T(8,128)(2,1)S(1)} %add_convert_fusion.1), channel_id=1, source_target_pairs={{0,8},{2,10},{4,12},{6,14},{8,0},{10,2},{12,4},{14,6},{1,9},{3,11}... | collective-permute-start | bytes 983048 | tf_op jit(solution)/shard_map/ppermute | solution.py:177
  115.6 21.1 %collective-permute-start.20 = (bf16[80,2048]{1,0:T(8,128)(2,1)S(1)}, bf16[80,2048]{1,0:T(8,128)(2,1)S(1)}, u32[]{:S(2)}, u32[]{:S(2)}) collective-permute-start(bf16[80,2048]{1,0:T(8,128)(2,1)S(1)} %add_convert_fusion.2), channel_id=1, source_target_pairs={{0,4},{2,6},{4,0},{6,2},{8,12},{10,14},{12,8},{14,10},{1,5},{3,7},... | collective-permute-start | bytes 983048 | tf_op jit(solution)/shard_map/ppermute | solution.py:177
  119.9 16.7 %collective-permute-start.34 = (bf16[80,2048]{1,0:T(8,128)(2,1)S(1)}, bf16[80,2048]{1,0:T(8,128)(2,1)S(1)}, u32[]{:S(2)}, u32[]{:S(2)}) collective-permute-start(bf16[80,2048]{1,0:T(8,128)(2,1)S(1)} %add_convert_fusion), channel_id=1, source_target_pairs={{0,12},{2,14},{4,8},{6,10},{8,4},{10,6},{12,0},{14,2},{1,13},{3,15... | collective-permute-start | bytes 983048 | tf_op jit(solution)/shard_map/ppermute | solution.py:177

commit v5 on v4

--- a/solution.py
+++ b/solution.py
@@ -233,7 +233,7 @@
             out_specs=[VMEM] * (1 + n_exp),
             out_shape=[jax.ShapeDtypeStruct((rows, half), F32)] + [jax.ShapeDtypeStruct((cap, half), BF16)] * n_exp,
             compiler_params=params(),
-            cost_estimate=cost(4 * rows * half * n_keys, n_keys * half * 2),
+            cost_estimate=cost(2 * rows * half * n_keys, n_keys * half),
             name="attend",
         )(queries, resid, gain, pick, *pieces)
 
@@ -261,7 +261,7 @@
             out_specs=VMEM,
             out_shape=jax.ShapeDtypeStruct((2 * count, hidden), BF16),
             compiler_params=params(),
-            cost_estimate=cost(8 * count * width * hidden, 4 * width * hidden),
+            cost_estimate=cost(4 * count * width * hidden, 2 * width * hidden),
             name="hidden",
         )(*gathered, columns, gain)
 
@@ -274,7 +274,7 @@
             out_shape=[jax.ShapeDtypeStruct((count, half), F32), jax.ShapeDtypeStruct((count, half), BF16)],
             scratch_shapes=[pltpu.VMEM((2 * count, half), F32)],
             compiler_params=params(),
-            cost_estimate=cost(8 * count * half * hidden, 4 * half * hidden),
+            cost_estimate=cost(4.8 * count * half * hidden, 2.4 * half * hidden),
             name="down",
         )(rep.reshape(1), act, other_act, down_own, down_near, down_far)
 

time: 140 us -> 139 us (level)
    ppermute x14, waiting for transfers between devices: 16.9 us -> 18.8 us  [over_y(): return lax.ppermute(a, 'dev', [(i, i ^ 1) for i in range(n_dev)])]
  transfers between devices with their start and end apart: 35 -> 35, of which waited for: 16 -> 18; matrix products, arithmetic and copies ran while one was open for 5% -> 5% of each run, Pallas kernels for 12% -> 12%
where the time goes in v5:
time: 139 us; the launch traced here: 137 us
  waiting for transfers between devices  59.6 us (43%)
  starting transfers between devices  51.8 us (37%)
  Pallas kernels  18.9 us (14%)
  local copies, waits for them, and re-layouts  3.73 us (3%)
  other arithmetic  3.1 us (2%)
    ppermute x9, waiting for transfers between devices, over_z(): lax.ppermute(a, 'dev', [(i, (i // 2 ^ k) * 2 + i % 2) for i in range(n_de...  27.3 us
    ppermute x14, starting transfers between devices, over_y(): return lax.ppermute(a, 'dev', [(i, i ^ 1) for i in range(n_dev)])  20.5 us
    ppermute x14, waiting for transfers between devices, over_y(): return lax.ppermute(a, 'dev', [(i, i ^ 1) for i in range(n_dev)])  18.8 us
    ppermute x9, starting transfers between devices, over_z(): lax.ppermute(a, 'dev', [(i, (i // 2 ^ k) * 2 + i % 2) for i in range(n_de...  18.5 us
    ppermute x11, waiting for transfers between devices, over_sec(): return lax.ppermute(a, 'sec', [(0, 1), (1, 0)])  13.5 us
    ppermute x11, starting transfers between devices, over_sec(): return lax.ppermute(a, 'sec', [(0, 1), (1, 0)])  12.7 us
    pallas_call x4, Pallas kernels, hidden_of(): pl.pallas_call(functools.partial(hidden_kernel, width), in_specs=[VMEM] *...  5.24 us
    pallas_call x4, Pallas kernels, down_of(): pl.pallas_call(down_kernel, in_specs=[smem] + [VMEM] * 5, out_specs=[VMEM...  3.72 us
  transfers between devices with their start and end apart: 35, of which 18 were waited for; matrix products, arithmetic and copies ran while one was open for 5% of the time, Pallas kernels for 12%

profile of v5, /device:TPU:0, one launch (start us, length us, event | category | flops | bytes accessed | tf_op | source)
XLA Modules:
  0.0 137.4 jit_solution(7098118173708437912)
XLA Ops:
  1.0 3.1 %collective-permute-start = (bf16[128,1024]{1,0:T(8,128)(2,1)S(1)}, bf16[128,1024]{1,0:T(8,128)(2,1)S(1)}, u32[]{:S(2)}, u32[]{:S(2)}) collective-permute-start(bf16[128,1024]{1,0:T(8,128)(2,1)S(1)} %pack.1.refs_0_), channel_id=1, source_target_pairs={{0,4},{2,6},{4,0},{6,2},{8,12},{10,14},{12,8},{14,10},{1,5},{3,7},... | collective-permute-start | bytes 786440 | tf_op jit(solution)/shard_map/ppermute | solution.py:177
  4.1 2.6 %collective-permute-start.1 = (bf16[128,1024]{1,0:T(8,128)(2,1)S(1)}, bf16[128,1024]{1,0:T(8,128)(2,1)S(1)}, u32[]{:S(2)}, u32[]{:S(2)}) collective-permute-start(bf16[128,1024]{1,0:T(8,128)(2,1)S(1)} %pack.1.refs_0_), channel_id=1, source_target_pairs={{0,8},{2,10},{4,12},{6,14},{8,0},{10,2},{12,4},{14,6},{1,9},{3,11}... | collective-permute-start | bytes 786440 | tf_op jit(solution)/shard_map/ppermute | solution.py:177
  6.7 1.7 %collective-permute-start.3 = (bf16[128,1024]{1,0:T(8,128)(2,1)S(1)}, bf16[128,1024]{1,0:T(8,128)(2,1)S(1)}, u32[]{:S(2)}, u32[]{:S(2)}) collective-permute-start(bf16[128,1024]{1,0:T(8,128)(2,1)S(1)} %pack.1.refs_0_), channel_id=1, source_target_pairs={{0,2},{2,0},{4,6},{6,4},{8,10},{10,8},{12,14},{14,12},{1,3},{3,1},... | collective-permute-start | bytes 786440 | tf_op jit(solution)/shard_map/ppermute | solution.py:174
  10.9 2.1 %dynamic-slice_bitcast_fusion = bf16[384,1024]{1,0:T(8,128)(2,1)} fusion(bf16[1,384,4096]{2,1,0:T(8,128)(2,1)} %param.19, s32[]{:T(128)S(6)} %select_n.14), kind=kLoop, calls=%fused_computation | loop fusion | bytes 1572868 | tf_op jit(solution)/shard_map/dynamic_slice | solution.py:191
  13.0 2.3 %collective-permute-done.refs_1_ = bf16[128,1024]{1,0:T(8,128)(2,1)S(1)} collective-permute-done((bf16[128,1024]{1,0:T(8,128)(2,1)S(1)}, bf16[128,1024]{1,0:T(8,128)(2,1)S(1)}, u32[]{:S(2)}, u32[]{:S(2)}) %collective-permute-start) | collective-permute-done | bytes 262176 | tf_op jit(solution)/shard_map/ppermute | solution.py:177
  15.2 1.7 %collective-permute-start.11 = (bf16[384,1024]{1,0:T(8,128)(2,1)}, bf16[384,1024]{1,0:T(8,128)(2,1)S(1)}, u32[]{:S(2)}, u32[]{:S(2)}) collective-permute-start(bf16[384,1024]{1,0:T(8,128)(2,1)} %dynamic-slice_bitcast_fusion), channel_id=1, source_target_pairs={{0,16},{16,0},{1,17},{17,1},{2,18},{18,2},{3,19},{19,3},{4,20},{20... | collective-permute-start | bytes 2359304 | tf_op jit(solution)/shard_map/ppermute | solution.py:168
  18.0 1.5 %collective-permute-start.4 = (bf16[128,1024]{1,0:T(8,128)(2,1)S(1)}, bf16[128,1024]{1,0:T(8,128)(2,1)S(1)}, u32[]{:S(2)}, u32[]{:S(2)}) collective-permute-start(bf16[128,1024]{1,0:T(8,128)(2,1)S(1)} %collective-permute-done.refs_1_), channel_id=1, source_target_pairs={{0,2},{2,0},{4,6},{6,4},{8,10},{10,8},{12,14},{14,12},{1,3},{3,1},... | collective-permute-start | bytes 786440 | tf_op jit(solution)/shard_map/ppermute | solution.py:174
  19.6 5.9 %collective-permute-done.1.refs_2_ = bf16[128,1024]{1,0:T(8,128)(2,1)S(1)} collective-permute-done((bf16[128,1024]{1,0:T(8,128)(2,1)S(1)}, bf16[128,1024]{1,0:T(8,128)(2,1)S(1)}, u32[]{:S(2)}, u32[]{:S(2)}) %collective-permute-start.1) | collective-permute-done | bytes 262176 | tf_op jit(solution)/shard_map/ppermute | solution.py:177
  25.5 1.5 %collective-permute-start.5 = (bf16[128,1024]{1,0:T(8,128)(2,1)S(1)}, bf16[128,1024]{1,0:T(8,128)(2,1)S(1)}, u32[]{:S(2)}, u32[]{:S(2)}) collective-permute-start(bf16[128,1024]{1,0:T(8,128)(2,1)S(1)} %collective-permute-done.1.refs_2_), channel_id=1, source_target_pairs={{0,2},{2,0},{4,6},{6,4},{8,10},{10,8},{12,14},{14,12},{1,3},{3,1},... | collective-permute-start | bytes 786440 | tf_op jit(solution)/shard_map/ppermute | solution.py:174
  28.4 3.7 %stage.1 = (bf16[128,2048]{1,0:T(8,128)(2,1)S(1)}, bf16[128,2048]{1,0:T(8,128)(2,1)S(1)}, f32[1,4096]{1,0:T(1,128)S(1)}, bf16[4096,768]{1,0:T(8,128)(2,1)S(1)}, bf16[384,2048]{1,0:T(8,128)(2,1)S(1)}) custom-call(s32[1]{0:T(128)} %bitcast.6.sec_ref, bf16[128,2048]{1,0:T(8,128)(2,1)} %q_ref.1, bf16[128,4096]{1,0:T(8,128)(2,1)} %resid_ref.1, ...), custom_call_target="tpu_custom_call" | custom-call | tf_op jit(solution)/shard_map/stage/pallas_call | solution.py:207
  33.4 2.8 %collective-permute-done.6.refs_7_ = bf16[128,1024]{1,0:T(8,128)(2,1)S(1)} collective-permute-done((bf16[128,1024]{1,0:T(8,128)(2,1)S(1)}, bf16[128,1024]{1,0:T(8,128)(2,1)S(1)}, u32[]{:S(2)}, u32[]{:S(2)}) %collective-permute-start.6) | collective-permute-done | bytes 262176 | tf_op jit(solution)/shard_map/ppermute | solution.py:174
  36.2 3.7 %attend.1 = (f32[128,2048]{1,0:T(8,128)S(1)}, bf16[80,2048]{1,0:T(8,128)(2,1)S(1)}, bf16[80,2048]{1,0:T(8,128)(2,1)S(1)}, bf16[80,2048]{1,0:T(8,128)(2,1)S(1)}, bf16[80,2048]{1,0:T(8,128)(2,1)S(1)}) custom-call(bf16[128,2048]{1,0:T(8,128)(2,1)S(1)} %get-tuple-element.45.q_ref, bf16[128,2048]{1,0:T(8,128)(2,1)S(1)} %get-tuple-element.46.resid_ref, ...), custom_call_target="tpu_custom_call" | custom-call | flops 536870912 | bytes 2097152 | tf_op jit(solution)/shard_map/attend/pallas_call | solution.py:230
  40.7 1.7 %collective-permute-start.14 = (bf16[80,2048]{1,0:T(8,128)(2,1)S(1)}, bf16[80,2048]{1,0:T(8,128)(2,1)S(1)}, u32[]{:S(2)}, u32[]{:S(2)}) collective-permute-start(bf16[80,2048]{1,0:T(8,128)(2,1)S(1)} %get-tuple-element.60), channel_id=1, source_target_pairs={{0,4},{2,6},{4,0},{6,2},{8,12},{10,14},{12,8},{14,10},{1,5},{3,7},... | collective-permute-start | bytes 983048 | tf_op jit(solution)/shard_map/ppermute | solution.py:177
  42.4 1.7 %collective-permute-start.21 = (bf16[80,2048]{1,0:T(8,128)(2,1)S(1)}, bf16[80,2048]{1,0:T(8,128)(2,1)S(1)}, u32[]{:S(2)}, u32[]{:S(2)}) collective-permute-start(bf16[80,2048]{1,0:T(8,128)(2,1)S(1)} %get-tuple-element.64), channel_id=1, source_target_pairs={{0,8},{2,10},{4,12},{6,14},{8,0},{10,2},{12,4},{14,6},{1,9},{3,11}... | collective-permute-start | bytes 983048 | tf_op jit(solution)/shard_map/ppermute | solution.py:177
  44.1 1.5 %collective-permute-start.7 = (bf16[80,2048]{1,0:T(8,128)(2,1)S(1)}, bf16[80,2048]{1,0:T(8,128)(2,1)S(1)}, u32[]{:S(2)}, u32[]{:S(2)}) collective-permute-start(bf16[80,2048]{1,0:T(8,128)(2,1)S(1)} %get-tuple-element.53.own_ref), channel_id=1, source_target_pairs={{0,2},{2,0},{4,6},{6,4},{8,10},{10,8},{12,14},{14,12},{1,3},{3,1},... | collective-permute-start | bytes 983048 | tf_op jit(solution)/shard_map/ppermute | solution.py:174
  45.7 4.4 %collective-permute-done.8.x_ref = bf16[80,2048]{1,0:T(8,128)(2,1)S(1)} collective-permute-done((bf16[80,2048]{1,0:T(8,128)(2,1)S(1)}, bf16[80,2048]{1,0:T(8,128)(2,1)S(1)}, u32[]{:S(2)}, u32[]{:S(2)}) %collective-permute-start.8) | collective-permute-done | bytes 327712 | tf_op jit(solution)/shard_map/ppermute | solution.py:168
  50.1 1.5 %collective-permute-start.9 = (bf16[80,2048]{1,0:T(8,128)(2,1)S(1)}, bf16[80,2048]{1,0:T(8,128)(2,1)S(1)}, u32[]{:S(2)}, u32[]{:S(2)}) collective-permute-start(bf16[80,2048]{1,0:T(8,128)(2,1)S(1)} %collective-permute-done.8.x_ref), channel_id=1, source_target_pairs={{0,2},{2,0},{4,6},{6,4},{8,10},{10,8},{12,14},{14,12},{1,3},{3,1},... | collective-permute-start | bytes 983048 | tf_op jit(solution)/shard_map/ppermute | solution.py:174
  51.6 5.8 %collective-permute-done.14.own_ref = bf16[80,2048]{1,0:T(8,128)(2,1)S(1)} collective-permute-done((bf16[80,2048]{1,0:T(8,128)(2,1)S(1)}, bf16[80,2048]{1,0:T(8,128)(2,1)S(1)}, u32[]{:S(2)}, u32[]{:S(2)}) %collective-permute-start.14) | collective-permute-done | bytes 327712 | tf_op jit(solution)/shard_map/ppermute | solution.py:177
  57.4 1.3 collective-permute-start.16
  59.9 1.5 %collective-permute-start.22 = (bf16[80,2048]{1,0:T(8,128)(2,1)S(1)}, bf16[80,2048]{1,0:T(8,128)(2,1)S(1)}, u32[]{:S(2)}, u32[]{:S(2)}) collective-permute-start(bf16[80,2048]{1,0:T(8,128)(2,1)S(1)} %collective-permute-done.21.own_ref), channel_id=1, source_target_pairs={{0,2},{2,0},{4,6},{6,4},{8,10},{10,8},{12,14},{14,12},{1,3},{3,1},... | collective-permute-start | bytes 983048 | tf_op jit(solution)/shard_map/ppermute | solution.py:174
  61.4 2.5 %collective-permute-start.28 = (bf16[80,2048]{1,0:T(8,128)(2,1)S(1)}, bf16[80,2048]{1,0:T(8,128)(2,1)S(1)}, u32[]{:S(2)}, u32[]{:S(2)}) collective-permute-start(bf16[80,2048]{1,0:T(8,128)(2,1)S(1)} %get-tuple-element.70), channel_id=1, source_target_pairs={{0,12},{2,14},{4,8},{6,10},{8,4},{10,6},{12,0},{14,2},{1,13},{3,15... | collective-permute-start | bytes 983048 | tf_op jit(solution)/shard_map/ppermute | solution.py:177
  64.4 1.3 hidden.4.own_act
  66.3 1.7 %collective-permute-start.17 = (bf16[80,2048]{1,0:T(8,128)(2,1)S(1)}, bf16[80,2048]{1,0:T(8,128)(2,1)S(1)}, u32[]{:S(2)}, u32[]{:S(2)}) collective-permute-start(bf16[80,2048]{1,0:T(8,128)(2,1)S(1)} %collective-permute-done.16.x_ref), channel_id=1, source_target_pairs={{0,2},{2,0},{4,6},{6,4},{8,10},{10,8},{12,14},{14,12},{1,3},{3,1},... | collective-permute-start | bytes 983048 | tf_op jit(solution)/shard_map/ppermute | solution.py:174
  68.0 1.7 %collective-permute-done.22.y_ref = bf16[80,2048]{1,0:T(8,128)(2,1)S(1)} collective-permute-done((bf16[80,2048]{1,0:T(8,128)(2,1)S(1)}, bf16[80,2048]{1,0:T(8,128)(2,1)S(1)}, u32[]{:S(2)}, u32[]{:S(2)}) %collective-permute-start.22) | collective-permute-done | bytes 327712 | tf_op jit(solution)/shard_map/ppermute | solution.py:174
  69.8 1.4 collective-permute-start.23
  71.1 1.5 %collective-permute-start.29 = (bf16[80,2048]{1,0:T(8,128)(2,1)S(1)}, bf16[80,2048]{1,0:T(8,128)(2,1)S(1)}, u32[]{:S(2)}, u32[]{:S(2)}) collective-permute-start(bf16[80,2048]{1,0:T(8,128)(2,1)S(1)} %collective-permute-done.28.own_ref), channel_id=1, source_target_pairs={{0,2},{2,0},{4,6},{6,4},{8,10},{10,8},{12,14},{14,12},{1,3},{3,1},... | collective-permute-start | bytes 983048 | tf_op jit(solution)/shard_map/ppermute | solution.py:174
  72.6 1.5 %collective-permute-start.24 = (bf16[80,2048]{1,0:T(8,128)(2,1)S(1)}, bf16[80,2048]{1,0:T(8,128)(2,1)S(1)}, u32[]{:S(2)}, u32[]{:S(2)}) collective-permute-start(bf16[80,2048]{1,0:T(8,128)(2,1)S(1)} %collective-permute-done.22.y_ref), channel_id=1, source_target_pairs={{0,16},{16,0},{1,17},{17,1},{2,18},{18,2},{3,19},{19,3},{4,20},{20... | collective-permute-start | bytes 983048 | tf_op jit(solution)/shard_map/ppermute | solution.py:168
  75.0 1.8 %collective-permute-done.15.y_ref = bf16[80,2048]{1,0:T(8,128)(2,1)S(1)} collective-permute-done((bf16[80,2048]{1,0:T(8,128)(2,1)S(1)}, bf16[80,2048]{1,0:T(8,128)(2,1)S(1)}, u32[]{:S(2)}, u32[]{:S(2)}) %collective-permute-start.15) | collective-permute-done | bytes 327712 | tf_op jit(solution)/shard_map/ppermute | solution.py:174
  76.8 2.3 %collective-permute-start.13 = (bf16[80,2048]{1,0:T(8,128)(2,1)S(1)}, bf16[80,2048]{1,0:T(8,128)(2,1)S(1)}, u32[]{:S(2)}, u32[]{:S(2)}) collective-permute-start(bf16[80,2048]{1,0:T(8,128)(2,1)S(1)} %get-tuple-element.59), channel_id=1, source_target_pairs={{0,2},{2,0},{4,6},{6,4},{8,10},{10,8},{12,14},{14,12},{1,3},{3,1},... | collective-permute-start | bytes 983048 | tf_op jit(solution)/shard_map/ppermute | solution.py:174
  79.1 4.7 %collective-permute-done.17.both_ref = bf16[80,2048]{1,0:T(8,128)(2,1)S(1)} collective-permute-done((bf16[80,2048]{1,0:T(8,128)(2,1)S(1)}, bf16[80,2048]{1,0:T(8,128)(2,1)S(1)}, u32[]{:S(2)}, u32[]{:S(2)}) %collective-permute-start.17) | collective-permute-done | bytes 327712 | tf_op jit(solution)/shard_map/ppermute | solution.py:174
  83.8 1.3 hidden.5.own_act
  85.1 1.4 %collective-permute-start.18 = (bf16[160,384]{1,0:T(8,128)(2,1)S(1)}, bf16[160,384]{1,0:T(8,128)(2,1)S(1)}, u32[]{:S(2)}, u32[]{:S(2)}) collective-permute-start(bf16[160,384]{1,0:T(8,128)(2,1)S(1)} %hidden.5.own_act), channel_id=1, source_target_pairs={{0,16},{16,0},{1,17},{17,1},{2,18},{18,2},{3,19},{19,3},{4,20},{20... | collective-permute-start | bytes 368648 | tf_op jit(solution)/shard_map/ppermute | solution.py:168
  87.2 3.6 %collective-permute-done.29.y_ref = bf16[80,2048]{1,0:T(8,128)(2,1)S(1)} collective-permute-done((bf16[80,2048]{1,0:T(8,128)(2,1)S(1)}, bf16[80,2048]{1,0:T(8,128)(2,1)S(1)}, u32[]{:S(2)}, u32[]{:S(2)}) %collective-permute-start.29) | collective-permute-done | bytes 327712 | tf_op jit(solution)/shard_map/ppermute | solution.py:174
  90.8 1.4 collective-permute-start.31
  92.2 1.3 hidden.6.own_act
  95.2 2.4 %collective-permute-start.19 = (bf16[80,2048]{1,0:T(8,128)(2,1)S(1)}, bf16[80,2048]{1,0:T(8,128)(2,1)S(1)}, u32[]{:S(2)}, u32[]{:S(2)}) collective-permute-start(bf16[80,2048]{1,0:T(8,128)(2,1)S(1)} %get-tuple-element.63), channel_id=1, source_target_pairs={{0,2},{2,0},{4,6},{6,4},{8,10},{10,8},{12,14},{14,12},{1,3},{3,1},... | collective-permute-start | bytes 983048 | tf_op jit(solution)/shard_map/ppermute | solution.py:174
  97.9 5.7 %collective-permute-done.25.other_act = bf16[160,384]{1,0:T(8,128)(2,1)S(1)} collective-permute-done((bf16[160,384]{1,0:T(8,128)(2,1)S(1)}, bf16[160,384]{1,0:T(8,128)(2,1)S(1)}, u32[]{:S(2)}, u32[]{:S(2)}) %collective-permute-start.25) | collective-permute-done | bytes 122912 | tf_op jit(solution)/shard_map/ppermute | solution.py:168
  104.5 1.4 collective-permute-start.26
  105.9 1.3 hidden.7.own_act
  107.2 1.4 %collective-permute-start.32 = (bf16[160,384]{1,0:T(8,128)(2,1)S(1)}, bf16[160,384]{1,0:T(8,128)(2,1)S(1)}, u32[]{:S(2)}, u32[]{:S(2)}) collective-permute-start(bf16[160,384]{1,0:T(8,128)(2,1)S(1)} %hidden.7.own_act), channel_id=1, source_target_pairs={{0,16},{16,0},{1,17},{17,1},{2,18},{18,2},{3,19},{19,3},{4,20},{20... | collective-permute-start | bytes 368648 | tf_op jit(solution)/shard_map/ppermute | solution.py:168
  108.7 3.4 %collective-permute-done.32.other_act = bf16[160,384]{1,0:T(8,128)(2,1)S(1)} collective-permute-done((bf16[160,384]{1,0:T(8,128)(2,1)S(1)}, bf16[160,384]{1,0:T(8,128)(2,1)S(1)}, u32[]{:S(2)}, u32[]{:S(2)}) %collective-permute-start.32) | collective-permute-done | bytes 122912 | tf_op jit(solution)/shard_map/ppermute | solution.py:168
  114.2 1.4 collective-permute-start.27
  115.6 2.1 %collective-permute-start.20 = (bf16[80,2048]{1,0:T(8,128)(2,1)S(1)}, bf16[80,2048]{1,0:T(8,128)(2,1)S(1)}, u32[]{:S(2)}, u32[]{:S(2)}) collective-permute-start(bf16[80,2048]{1,0:T(8,128)(2,1)S(1)} %add_convert_fusion.2), channel_id=1, source_target_pairs={{0,4},{2,6},{4,0},{6,2},{8,12},{10,14},{12,8},{14,10},{1,5},{3,7},... | collective-permute-start | bytes 983048 | tf_op jit(solution)/shard_map/ppermute | solution.py:177
  117.7 2.6 %collective-permute-done.33 = bf16[80,2048]{1,0:T(8,128)(2,1)S(1)} collective-permute-done((bf16[80,2048]{1,0:T(8,128)(2,1)S(1)}, bf16[80,2048]{1,0:T(8,128)(2,1)S(1)}, u32[]{:S(2)}, u32[]{:S(2)}) %collective-permute-start.33) | collective-permute-done | bytes 327712 | tf_op jit(solution)/shard_map/ppermute | solution.py:174
  120.3 3.4 %collective-permute-start.34 = (bf16[80,2048]{1,0:T(8,128)(2,1)S(1)}, bf16[80,2048]{1,0:T(8,128)(2,1)S(1)}, u32[]{:S(2)}, u32[]{:S(2)}) collective-permute-start(bf16[80,2048]{1,0:T(8,128)(2,1)S(1)} %add_convert_fusion), channel_id=1, source_target_pairs={{0,12},{2,14},{4,8},{6,10},{8,4},{10,6},{12,0},{14,2},{1,13},{3,15... | collective-permute-start | bytes 983048 | tf_op jit(solution)/shard_map/ppermute | solution.py:177
  123.7 8.1 %collective-permute-done.27.refs_2_ = bf16[80,2048]{1,0:T(8,128)(2,1)S(1)} collective-permute-done((bf16[80,2048]{1,0:T(8,128)(2,1)S(1)}, bf16[80,2048]{1,0:T(8,128)(2,1)S(1)}, u32[]{:S(2)}, u32[]{:S(2)}) %collective-permute-start.27) | collective-permute-done | bytes 327712 | tf_op jit(solution)/shard_map/ppermute | solution.py:177
  131.8 4.0 %collective-permute-done.34.refs_3_ = bf16[80,2048]{1,0:T(8,128)(2,1)S(1)} collective-permute-done((bf16[80,2048]{1,0:T(8,128)(2,1)S(1)}, bf16[80,2048]{1,0:T(8,128)(2,1)S(1)}, u32[]{:S(2)}, u32[]{:S(2)}) %collective-permute-start.34) | collective-permute-done | bytes 327712 | tf_op jit(solution)/shard_map/ppermute | solution.py:177
  135.8 1.5 %combine.1 = bf16[128,2048]{1,0:T(8,128)(2,1)} custom-call(f32[128,2048]{1,0:T(8,128)S(1)} %get-tuple-element.50.stream_ref, bf16[4,128,80]{2,1,0:T(8,128)(2,1)S(1)} %get-tuple-element.51.high_ref, bf16[4,128,80]{2,1,0:T(8,128)(2,1)S(1)} %get-tuple-element.52.low_ref, bf16[80,2048]{1,0:T(8,128)(2,1)S(1)} %add_convert_fusion.3.refs_0_, ...), custom_call_target="tpu_custom_call" | custom-call | flops 335544320 | bytes 2883584 | tf_op jit(solution)/shard_map/combine/pallas_call | solution.py:297
  (57 shorter events, 17.1 us)
Async XLA Ops:
  1.0 14.2 %collective-permute-start = (bf16[128,1024]{1,0:T(8,128)(2,1)S(1)}, bf16[128,1024]{1,0:T(8,128)(2,1)S(1)}, u32[]{:S(2)}, u32[]{:S(2)}) collective-permute-start(bf16[128,1024]{1,0:T(8,128)(2,1)S(1)} %pack.1.refs_0_), channel_id=1, source_target_pairs={{0,4},{2,6},{4,0},{6,2},{8,12},{10,14},{12,8},{14,10},{1,5},{3,7},... | collective-permute-start | bytes 786440 | tf_op jit(solution)/shard_map/ppermute | solution.py:177
  4.1 21.4 %collective-permute-start.1 = (bf16[128,1024]{1,0:T(8,128)(2,1)S(1)}, bf16[128,1024]{1,0:T(8,128)(2,1)S(1)}, u32[]{:S(2)}, u32[]{:S(2)}) collective-permute-start(bf16[128,1024]{1,0:T(8,128)(2,1)S(1)} %pack.1.refs_0_), channel_id=1, source_target_pairs={{0,8},{2,10},{4,12},{6,14},{8,0},{10,2},{12,4},{14,6},{1,9},{3,11}... | collective-permute-start | bytes 786440 | tf_op jit(solution)/shard_map/ppermute | solution.py:177
  6.7 20.3 %collective-permute-start.2 = (bf16[128,1024]{1,0:T(8,128)(2,1)S(1)}, bf16[128,1024]{1,0:T(8,128)(2,1)S(1)}, u32[]{:S(2)}, u32[]{:S(2)}) collective-permute-start(bf16[128,1024]{1,0:T(8,128)(2,1)S(1)} %pack.1.refs_0_), channel_id=1, source_target_pairs={{0,12},{2,14},{4,8},{6,10},{8,4},{10,6},{12,0},{14,2},{1,13},{3,15... | collective-permute-start | bytes 786440 | tf_op jit(solution)/shard_map/ppermute | solution.py:177
  6.7 25.5 %collective-permute-start.3 = (bf16[128,1024]{1,0:T(8,128)(2,1)S(1)}, bf16[128,1024]{1,0:T(8,128)(2,1)S(1)}, u32[]{:S(2)}, u32[]{:S(2)}) collective-permute-start(bf16[128,1024]{1,0:T(8,128)(2,1)S(1)} %pack.1.refs_0_), channel_id=1, source_target_pairs={{0,2},{2,0},{4,6},{6,4},{8,10},{10,8},{12,14},{14,12},{1,3},{3,1},... | collective-permute-start | bytes 786440 | tf_op jit(solution)/shard_map/ppermute | solution.py:174
  15.2 24.6 %collective-permute-start.11 = (bf16[384,1024]{1,0:T(8,128)(2,1)}, bf16[384,1024]{1,0:T(8,128)(2,1)S(1)}, u32[]{:S(2)}, u32[]{:S(2)}) collective-permute-start(bf16[384,1024]{1,0:T(8,128)(2,1)} %dynamic-slice_bitcast_fusion), channel_id=1, source_target_pairs={{0,16},{16,0},{1,17},{17,1},{2,18},{18,2},{3,19},{19,3},{4,20},{20... | collective-permute-start | bytes 2359304 | tf_op jit(solution)/shard_map/ppermute | solution.py:168
  18.0 14.1 %collective-permute-start.4 = (bf16[128,1024]{1,0:T(8,128)(2,1)S(1)}, bf16[128,1024]{1,0:T(8,128)(2,1)S(1)}, u32[]{:S(2)}, u32[]{:S(2)}) collective-permute-start(bf16[128,1024]{1,0:T(8,128)(2,1)S(1)} %collective-permute-done.refs_1_), channel_id=1, source_target_pairs={{0,2},{2,0},{4,6},{6,4},{8,10},{10,8},{12,14},{14,12},{1,3},{3,1},... | collective-permute-start | bytes 786440 | tf_op jit(solution)/shard_map/ppermute | solution.py:174
  25.5 7.9 %collective-permute-start.5 = (bf16[128,1024]{1,0:T(8,128)(2,1)S(1)}, bf16[128,1024]{1,0:T(8,128)(2,1)S(1)}, u32[]{:S(2)}, u32[]{:S(2)}) collective-permute-start(bf16[128,1024]{1,0:T(8,128)(2,1)S(1)} %collective-permute-done.1.refs_2_), channel_id=1, source_target_pairs={{0,2},{2,0},{4,6},{6,4},{8,10},{10,8},{12,14},{14,12},{1,3},{3,1},... | collective-permute-start | bytes 786440 | tf_op jit(solution)/shard_map/ppermute | solution.py:174
  27.0 9.2 %collective-permute-start.6 = (bf16[128,1024]{1,0:T(8,128)(2,1)S(1)}, bf16[128,1024]{1,0:T(8,128)(2,1)S(1)}, u32[]{:S(2)}, u32[]{:S(2)}) collective-permute-start(bf16[128,1024]{1,0:T(8,128)(2,1)S(1)} %collective-permute-done.2.refs_3_), channel_id=1, source_target_pairs={{0,2},{2,0},{4,6},{6,4},{8,10},{10,8},{12,14},{14,12},{1,3},{3,1},... | collective-permute-start | bytes 786440 | tf_op jit(solution)/shard_map/ppermute | solution.py:174
  39.8 17.5 %collective-permute-start.12 = (bf16[384,1024]{1,0:T(8,128)(2,1)S(1)}, bf16[384,1024]{1,0:T(8,128)(2,1)S(1)}, u32[]{:S(2)}, u32[]{:S(2)}) collective-permute-start(bf16[384,1024]{1,0:T(8,128)(2,1)S(1)} %collective-permute-done.11.near_ref), channel_id=1, source_target_pairs={{0,1},{1,0},{2,3},{3,2},{4,5},{5,4},{6,7},{7,6},{8,9},{9,8},{10,11... | collective-permute-start | bytes 2359304 | tf_op jit(solution)/shard_map/ppermute | solution.py:171
  39.9 10.1 %collective-permute-start.8 = (bf16[80,2048]{1,0:T(8,128)(2,1)S(1)}, bf16[80,2048]{1,0:T(8,128)(2,1)S(1)}, u32[]{:S(2)}, u32[]{:S(2)}) collective-permute-start(bf16[80,2048]{1,0:T(8,128)(2,1)S(1)} %get-tuple-element.53.own_ref), channel_id=1, source_target_pairs={{0,16},{16,0},{1,17},{17,1},{2,18},{18,2},{3,19},{19,3},{4,20},{20... | collective-permute-start | bytes 983048 | tf_op jit(solution)/shard_map/ppermute | solution.py:168
  40.7 16.7 %collective-permute-start.14 = (bf16[80,2048]{1,0:T(8,128)(2,1)S(1)}, bf16[80,2048]{1,0:T(8,128)(2,1)S(1)}, u32[]{:S(2)}, u32[]{:S(2)}) collective-permute-start(bf16[80,2048]{1,0:T(8,128)(2,1)S(1)} %get-tuple-element.60), channel_id=1, source_target_pairs={{0,4},{2,6},{4,0},{6,2},{8,12},{10,14},{12,8},{14,10},{1,5},{3,7},... | collective-permute-start | bytes 983048 | tf_op jit(solution)/shard_map/ppermute | solution.py:177
  42.4 17.5 %collective-permute-start.21 = (bf16[80,2048]{1,0:T(8,128)(2,1)S(1)}, bf16[80,2048]{1,0:T(8,128)(2,1)S(1)}, u32[]{:S(2)}, u32[]{:S(2)}) collective-permute-start(bf16[80,2048]{1,0:T(8,128)(2,1)S(1)} %get-tuple-element.64), channel_id=1, source_target_pairs={{0,8},{2,10},{4,12},{6,14},{8,0},{10,2},{12,4},{14,6},{1,9},{3,11}... | collective-permute-start | bytes 983048 | tf_op jit(solution)/shard_map/ppermute | solution.py:177
  44.1 19.7 %collective-permute-start.7 = (bf16[80,2048]{1,0:T(8,128)(2,1)S(1)}, bf16[80,2048]{1,0:T(8,128)(2,1)S(1)}, u32[]{:S(2)}, u32[]{:S(2)}) collective-permute-start(bf16[80,2048]{1,0:T(8,128)(2,1)S(1)} %get-tuple-element.53.own_ref), channel_id=1, source_target_pairs={{0,2},{2,0},{4,6},{6,4},{8,10},{10,8},{12,14},{14,12},{1,3},{3,1},... | collective-permute-start | bytes 983048 | tf_op jit(solution)/shard_map/ppermute | solution.py:174
  50.1 14.3 %collective-permute-start.9 = (bf16[80,2048]{1,0:T(8,128)(2,1)S(1)}, bf16[80,2048]{1,0:T(8,128)(2,1)S(1)}, u32[]{:S(2)}, u32[]{:S(2)}) collective-permute-start(bf16[80,2048]{1,0:T(8,128)(2,1)S(1)} %collective-permute-done.8.x_ref), channel_id=1, source_target_pairs={{0,2},{2,0},{4,6},{6,4},{8,10},{10,8},{12,14},{14,12},{1,3},{3,1},... | collective-permute-start | bytes 983048 | tf_op jit(solution)/shard_map/ppermute | solution.py:174
  57.4 9.0 %collective-permute-start.16 = (bf16[80,2048]{1,0:T(8,128)(2,1)S(1)}, bf16[80,2048]{1,0:T(8,128)(2,1)S(1)}, u32[]{:S(2)}, u32[]{:S(2)}) collective-permute-start(bf16[80,2048]{1,0:T(8,128)(2,1)S(1)} %collective-permute-done.14.own_ref), channel_id=1, source_target_pairs={{0,16},{16,0},{1,17},{17,1},{2,18},{18,2},{3,19},{19,3},{4,20},{20... | collective-permute-start | bytes 983048 | tf_op jit(solution)/shard_map/ppermute | solution.py:168
  59.9 9.9 %collective-permute-start.22 = (bf16[80,2048]{1,0:T(8,128)(2,1)S(1)}, bf16[80,2048]{1,0:T(8,128)(2,1)S(1)}, u32[]{:S(2)}, u32[]{:S(2)}) collective-permute-start(bf16[80,2048]{1,0:T(8,128)(2,1)S(1)} %collective-permute-done.21.own_ref), channel_id=1, source_target_pairs={{0,2},{2,0},{4,6},{6,4},{8,10},{10,8},{12,14},{14,12},{1,3},{3,1},... | collective-permute-start | bytes 983048 | tf_op jit(solution)/shard_map/ppermute | solution.py:174
  61.4 9.7 %collective-permute-start.28 = (bf16[80,2048]{1,0:T(8,128)(2,1)S(1)}, bf16[80,2048]{1,0:T(8,128)(2,1)S(1)}, u32[]{:S(2)}, u32[]{:S(2)}) collective-permute-start(bf16[80,2048]{1,0:T(8,128)(2,1)S(1)} %get-tuple-element.70), channel_id=1, source_target_pairs={{0,12},{2,14},{4,8},{6,10},{8,4},{10,6},{12,0},{14,2},{1,13},{3,15... | collective-permute-start | bytes 983048 | tf_op jit(solution)/shard_map/ppermute | solution.py:177
  63.9 12.9 %collective-permute-start.15 = (bf16[80,2048]{1,0:T(8,128)(2,1)S(1)}, bf16[80,2048]{1,0:T(8,128)(2,1)S(1)}, u32[]{:S(2)}, u32[]{:S(2)}) collective-permute-start(bf16[80,2048]{1,0:T(8,128)(2,1)S(1)} %collective-permute-done.14.own_ref), channel_id=1, source_target_pairs={{0,2},{2,0},{4,6},{6,4},{8,10},{10,8},{12,14},{14,12},{1,3},{3,1},... | collective-permute-start | bytes 983048 | tf_op jit(solution)/shard_map/ppermute | solution.py:174
  65.7 6.9 %collective-permute-start.10 = (bf16[160,384]{1,0:T(8,128)(2,1)S(1)}, bf16[160,384]{1,0:T(8,128)(2,1)S(1)}, u32[]{:S(2)}, u32[]{:S(2)}) collective-permute-start(bf16[160,384]{1,0:T(8,128)(2,1)S(1)} %hidden.4.own_act), channel_id=1, source_target_pairs={{0,16},{16,0},{1,17},{17,1},{2,18},{18,2},{3,19},{19,3},{4,20},{20... | collective-permute-start | bytes 368648 | tf_op jit(solution)/shard_map/ppermute | solution.py:168
  66.3 17.5 %collective-permute-start.17 = (bf16[80,2048]{1,0:T(8,128)(2,1)S(1)}, bf16[80,2048]{1,0:T(8,128)(2,1)S(1)}, u32[]{:S(2)}, u32[]{:S(2)}) collective-permute-start(bf16[80,2048]{1,0:T(8,128)(2,1)S(1)} %collective-permute-done.16.x_ref), channel_id=1, source_target_pairs={{0,2},{2,0},{4,6},{6,4},{8,10},{10,8},{12,14},{14,12},{1,3},{3,1},... | collective-permute-start | bytes 983048 | tf_op jit(solution)/shard_map/ppermute | solution.py:174
  69.8 16.8 %collective-permute-start.23 = (bf16[80,2048]{1,0:T(8,128)(2,1)S(1)}, bf16[80,2048]{1,0:T(8,128)(2,1)S(1)}, u32[]{:S(2)}, u32[]{:S(2)}) collective-permute-start(bf16[80,2048]{1,0:T(8,128)(2,1)S(1)} %collective-permute-done.21.own_ref), channel_id=1, source_target_pairs={{0,16},{16,0},{1,17},{17,1},{2,18},{18,2},{3,19},{19,3},{4,20},{20... | collective-permute-start | bytes 983048 | tf_op jit(solution)/shard_map/ppermute | solution.py:168
  71.1 19.7 %collective-permute-start.29 = (bf16[80,2048]{1,0:T(8,128)(2,1)S(1)}, bf16[80,2048]{1,0:T(8,128)(2,1)S(1)}, u32[]{:S(2)}, u32[]{:S(2)}) collective-permute-start(bf16[80,2048]{1,0:T(8,128)(2,1)S(1)} %collective-permute-done.28.own_ref), channel_id=1, source_target_pairs={{0,2},{2,0},{4,6},{6,4},{8,10},{10,8},{12,14},{14,12},{1,3},{3,1},... | collective-permute-start | bytes 983048 | tf_op jit(solution)/shard_map/ppermute | solution.py:174
  72.6 19.5 %collective-permute-start.24 = (bf16[80,2048]{1,0:T(8,128)(2,1)S(1)}, bf16[80,2048]{1,0:T(8,128)(2,1)S(1)}, u32[]{:S(2)}, u32[]{:S(2)}) collective-permute-start(bf16[80,2048]{1,0:T(8,128)(2,1)S(1)} %collective-permute-done.22.y_ref), channel_id=1, source_target_pairs={{0,16},{16,0},{1,17},{17,1},{2,18},{18,2},{3,19},{19,3},{4,20},{20... | collective-permute-start | bytes 983048 | tf_op jit(solution)/shard_map/ppermute | solution.py:168
  76.8 21.1 %collective-permute-start.13 = (bf16[80,2048]{1,0:T(8,128)(2,1)S(1)}, bf16[80,2048]{1,0:T(8,128)(2,1)S(1)}, u32[]{:S(2)}, u32[]{:S(2)}) collective-permute-start(bf16[80,2048]{1,0:T(8,128)(2,1)S(1)} %get-tuple-element.59), channel_id=1, source_target_pairs={{0,2},{2,0},{4,6},{6,4},{8,10},{10,8},{12,14},{14,12},{1,3},{3,1},... | collective-permute-start | bytes 983048 | tf_op jit(solution)/shard_map/ppermute | solution.py:174
  85.1 9.1 %collective-permute-start.18 = (bf16[160,384]{1,0:T(8,128)(2,1)S(1)}, bf16[160,384]{1,0:T(8,128)(2,1)S(1)}, u32[]{:S(2)}, u32[]{:S(2)}) collective-permute-start(bf16[160,384]{1,0:T(8,128)(2,1)S(1)} %hidden.5.own_act), channel_id=1, source_target_pairs={{0,16},{16,0},{1,17},{17,1},{2,18},{18,2},{3,19},{19,3},{4,20},{20... | collective-permute-start | bytes 368648 | tf_op jit(solution)/shard_map/ppermute | solution.py:168
  86.5 19.4 %collective-permute-start.30 = (bf16[80,2048]{1,0:T(8,128)(2,1)S(1)}, bf16[80,2048]{1,0:T(8,128)(2,1)S(1)}, u32[]{:S(2)}, u32[]{:S(2)}) collective-permute-start(bf16[80,2048]{1,0:T(8,128)(2,1)S(1)} %collective-permute-done.28.own_ref), channel_id=1, source_target_pairs={{0,16},{16,0},{1,17},{17,1},{2,18},{18,2},{3,19},{19,3},{4,20},{20... | collective-permute-start | bytes 983048 | tf_op jit(solution)/shard_map/ppermute | solution.py:168
  90.8 15.1 %collective-permute-start.31 = (bf16[80,2048]{1,0:T(8,128)(2,1)S(1)}, bf16[80,2048]{1,0:T(8,128)(2,1)S(1)}, u32[]{:S(2)}, u32[]{:S(2)}) collective-permute-start(bf16[80,2048]{1,0:T(8,128)(2,1)S(1)} %collective-permute-done.29.y_ref), channel_id=1, source_target_pairs={{0,16},{16,0},{1,17},{17,1},{2,18},{18,2},{3,19},{19,3},{4,20},{20... | collective-permute-start | bytes 983048 | tf_op jit(solution)/shard_map/ppermute | solution.py:168
  93.5 10.1 %collective-permute-start.25 = (bf16[160,384]{1,0:T(8,128)(2,1)S(1)}, bf16[160,384]{1,0:T(8,128)(2,1)S(1)}, u32[]{:S(2)}, u32[]{:S(2)}) collective-permute-start(bf16[160,384]{1,0:T(8,128)(2,1)S(1)} %hidden.6.own_act), channel_id=1, source_target_pairs={{0,16},{16,0},{1,17},{17,1},{2,18},{18,2},{3,19},{19,3},{4,20},{20... | collective-permute-start | bytes 368648 | tf_op jit(solution)/shard_map/ppermute | solution.py:168
  95.2 13.5 %collective-permute-start.19 = (bf16[80,2048]{1,0:T(8,128)(2,1)S(1)}, bf16[80,2048]{1,0:T(8,128)(2,1)S(1)}, u32[]{:S(2)}, u32[]{:S(2)}) collective-permute-start(bf16[80,2048]{1,0:T(8,128)(2,1)S(1)} %get-tuple-element.63), channel_id=1, source_target_pairs={{0,2},{2,0},{4,6},{6,4},{8,10},{10,8},{12,14},{14,12},{1,3},{3,1},... | collective-permute-start | bytes 983048 | tf_op jit(solution)/shard_map/ppermute | solution.py:174
  104.5 9.6 %collective-permute-start.26 = (bf16[80,2048]{1,0:T(8,128)(2,1)S(1)}, bf16[80,2048]{1,0:T(8,128)(2,1)S(1)}, u32[]{:S(2)}, u32[]{:S(2)}) collective-permute-start(bf16[80,2048]{1,0:T(8,128)(2,1)S(1)} %get-tuple-element.68), channel_id=1, source_target_pairs={{0,2},{2,0},{4,6},{6,4},{8,10},{10,8},{12,14},{14,12},{1,3},{3,1},... | collective-permute-start | bytes 983048 | tf_op jit(solution)/shard_map/ppermute | solution.py:174
  107.2 4.9 %collective-permute-start.32 = (bf16[160,384]{1,0:T(8,128)(2,1)S(1)}, bf16[160,384]{1,0:T(8,128)(2,1)S(1)}, u32[]{:S(2)}, u32[]{:S(2)}) collective-permute-start(bf16[160,384]{1,0:T(8,128)(2,1)S(1)} %hidden.7.own_act), channel_id=1, source_target_pairs={{0,16},{16,0},{1,17},{17,1},{2,18},{18,2},{3,19},{19,3},{4,20},{20... | collective-permute-start | bytes 368648 | tf_op jit(solution)/shard_map/ppermute | solution.py:168
  113.1 7.1 %collective-permute-start.33 = (bf16[80,2048]{1,0:T(8,128)(2,1)S(1)}, bf16[80,2048]{1,0:T(8,128)(2,1)S(1)}, u32[]{:S(2)}, u32[]{:S(2)}) collective-permute-start(bf16[80,2048]{1,0:T(8,128)(2,1)S(1)} %get-tuple-element.74), channel_id=1, source_target_pairs={{0,2},{2,0},{4,6},{6,4},{8,10},{10,8},{12,14},{14,12},{1,3},{3,1},... | collective-permute-start | bytes 983048 | tf_op jit(solution)/shard_map/ppermute | solution.py:174
  114.2 17.6 %collective-permute-start.27 = (bf16[80,2048]{1,0:T(8,128)(2,1)S(1)}, bf16[80,2048]{1,0:T(8,128)(2,1)S(1)}, u32[]{:S(2)}, u32[]{:S(2)}) collective-permute-start(bf16[80,2048]{1,0:T(8,128)(2,1)S(1)} %add_convert_fusion.1), channel_id=1, source_target_pairs={{0,8},{2,10},{4,12},{6,14},{8,0},{10,2},{12,4},{14,6},{1,9},{3,11}... | collective-permute-start | bytes 983048 | tf_op jit(solution)/shard_map/ppermute | solution.py:177
  115.6 16.2 %collective-permute-start.20 = (bf16[80,2048]{1,0:T(8,128)(2,1)S(1)}, bf16[80,2048]{1,0:T(8,128)(2,1)S(1)}, u32[]{:S(2)}, u32[]{:S(2)}) collective-permute-start(bf16[80,2048]{1,0:T(8,128)(2,1)S(1)} %add_convert_fusion.2), channel_id=1, source_target_pairs={{0,4},{2,6},{4,0},{6,2},{8,12},{10,14},{12,8},{14,10},{1,5},{3,7},... | collective-permute-start | bytes 983048 | tf_op jit(solution)/shard_map/ppermute | solution.py:177
  120.3 15.5 %collective-permute-start.34 = (bf16[80,2048]{1,0:T(8,128)(2,1)S(1)}, bf16[80,2048]{1,0:T(8,128)(2,1)S(1)}, u32[]{:S(2)}, u32[]{:S(2)}) collective-permute-start(bf16[80,2048]{1,0:T(8,128)(2,1)S(1)} %add_convert_fusion), channel_id=1, source_target_pairs={{0,12},{2,14},{4,8},{6,10},{8,4},{10,6},{12,0},{14,2},{1,13},{3,15... | collective-permute-start | bytes 983048 | tf_op jit(solution)/shard_map/ppermute | solution.py:177
